TPU v7x, 32 devices: a whole 2x2x4 slice. The times are simulated.
32 devices in a mesh: survey: 2 (over y), cell: 4 (over z), stn: 4 (over x, core).
Axes of the slice: x: 2, y: 2, z: 4, core: 2. Of those that a mesh axis runs over, the one named last changes fastest.
Arguments:
- densities: float32 [32768], P(('survey', 'cell', 'stn')), parts along dimension 0, may hold values from -6 to 6
- residual: float32 [6, 16384], P(None, ('survey', 'cell', 'stn')), parts along dimension 1, may hold values from -36 to 36
- direction: float32 [32768], P(('survey', 'cell', 'stn')), parts along dimension 0, may hold values from -36 to 36
- gradient_norm: float32 [2], P('survey'), parts along dimension 0, may hold values from 16384 to 131072
- station_place: float32 [3, 16384], P(None, ('survey', 'cell', 'stn')), parts along dimension 1, may hold values from -2 to 2, as said below
- cell_place: float32 [3, 32768], P(None, ('survey', 'cell', 'stn')), parts along dimension 1, may hold values from -2 to 2, as said below
- station_blocks: int32 [8, 4, 256], P(('survey', 'cell'), 'stn'), parts along dimension 0, may hold values from 0 to 15
- cell_blocks: int32 [8, 4, 256], P(('survey', 'cell'), 'stn'), parts along dimension 0, may hold values from 0 to 7
- pair_count: int32 [8, 4], P(('survey', 'cell'), 'stn'), parts along dimension 0, may hold values from 128 to 256, as said below
Outputs:
- densities_next: float32 [32768], P(('survey', 'cell', 'stn')), parts along dimension 0
- residual_next: float32 [6, 16384], P(None, ('survey', 'cell', 'stn')), parts along dimension 1
- direction_next: float32 [32768], P(('survey', 'cell', 'stn')), parts along dimension 0
- gradient_norm_next: float32 [2], P('survey'), parts along dimension 0
There are 2 independent parts, one for each index of `survey`. A program takes and returns all parts, laid end to end along the dimension named above; each array names one. Nothing has to cross between parts.
Inputs may be any that keep to these rules, and one draw needn't show every extreme that they name: station_blocks[c, s, k] numbers a block of station group s as c' * 4 + b for block b of device (c', s). cell_blocks[c, s, k] numbers a block of cell group c as s' * 2 + b for block b of device (c, s'). Slots at or past pair_count hold valid block numbers and are ignored; in every survey some device holds 256 live slots. `station_place`: heights (third row) lie in 0.5 to 1.5. `cell_place`: depths (third row) lie in -1.5 to -0.5.
All inputs are finite; a program needn't handle non-finite values.
Results may differ from a plain program's by a relative error of at most 0.0003.
Values sent between devices are 32-bit elements; how exact they have to be, the bound alone decides.
No kernel may reach another device: no remote copies, remote signals or barrier semaphores. Data moves between devices by JAX's collectives and lax.ppermute only.
A program may use at most 64 MiB of HBM per device.

v0:
```python
import jax
import jax.numpy as jnp
from jax import lax
from jax.sharding import PartitionSpec as P

PAIR_BATCH = 16


strength = 0.1


def tile_kernel(stations, prisms):
    offset_x = stations[0][:, None] - prisms[0][None, :]
    offset_y = stations[1][:, None] - prisms[1][None, :]
    offset_z = stations[2][:, None] - prisms[2][None, :]
    squared = offset_x * offset_x + offset_y * offset_y + offset_z * offset_z
    falloff = strength / (squared * squared * jnp.sqrt(squared))
    return jnp.stack(
        [
            (3.0 * offset_x * offset_x - squared) * falloff,
            3.0 * offset_x * offset_y * falloff,
            3.0 * offset_x * offset_z * falloff,
            (3.0 * offset_y * offset_y - squared) * falloff,
            3.0 * offset_y * offset_z * falloff,
            (3.0 * offset_z * offset_z - squared) * falloff,
        ]
    )


def on_device(
    densities,
    residual,
    direction,
    gradient_norm,
    station_place,
    cell_place,
    station_blocks,
    cell_blocks,
    pair_count,
):
    station_all = lax.all_gather(station_place, "cell", axis=1, tiled=True)
    prism_all, direction_all = (
        lax.all_gather(cell_place, "stn", axis=1, tiled=True),
        lax.all_gather(direction, "stn", axis=0, tiled=True),
    )
    station_tiles = station_all.reshape(3, -1, 128)
    prism_tiles = prism_all.reshape(3, -1, 512)
    direction_tiles = direction_all.reshape(-1, 512)
    station_count = station_tiles.shape[1]
    prism_count = prism_tiles.shape[1]
    station_list = station_blocks.reshape(-1)
    prism_list = cell_blocks.reshape(-1)
    filled = pair_count.reshape(())
    rounds = (filled + PAIR_BATCH - 1) // PAIR_BATCH
    station_ids = jnp.arange(station_count, dtype=jnp.int32)
    prism_ids = jnp.arange(prism_count, dtype=jnp.int32)
    exact = lax.Precision.HIGHEST

    def batch_of(which):
        start = which * PAIR_BATCH
        picks = start + jnp.arange(PAIR_BATCH, dtype=jnp.int32)
        station_index = lax.dynamic_slice_in_dim(station_list, start, PAIR_BATCH)
        prism_index = lax.dynamic_slice_in_dim(prism_list, start, PAIR_BATCH)
        weight = (picks < filled).astype(jnp.float32)
        station_onehot = (station_index[:, None] == station_ids[None, :]).astype(
            jnp.float32
        ) * weight[:, None]
        prism_onehot = (prism_index[:, None] == prism_ids[None, :]).astype(jnp.float32) * weight[
            :, None
        ]
        kernels = jax.vmap(tile_kernel, in_axes=(1, 1))(
            jnp.take(station_tiles, station_index, axis=1),
            jnp.take(prism_tiles, prism_index, axis=1),
        )
        return (station_index, prism_index, station_onehot, prism_onehot, kernels)

    def forward_turn(which, totals):
        station_index, prism_index, station_onehot, prism_onehot, kernels = batch_of(which)
        values = jnp.take(direction_tiles, prism_index, axis=0)
        contrib = jnp.sum(kernels * values[:, None, None, :], axis=3)
        return totals + jnp.einsum("bs,bkr->ksr", station_onehot, contrib, precision=exact)

    image_part = lax.fori_loop(
        0, rounds, forward_turn, jnp.zeros((6, station_count, 128), jnp.float32)
    ).reshape(6, -1)
    image = lax.psum_scatter(image_part, "cell", scatter_dimension=1, tiled=True)
    image_local = jnp.sum(image * image)
    norm_image = lax.psum(image_local, ("cell", "stn"))
    step_size = gradient_norm[0] / norm_image
    residual_next = residual - step_size * image
    residual_group = lax.all_gather(residual_next, "cell", axis=1, tiled=True)
    vectors = residual_group.reshape(1, 6, station_count, 128)

    def adjoint_turn(which, totals):
        station_index, prism_index, station_onehot, prism_onehot, kernels = batch_of(which)
        picked = jnp.transpose(jnp.take(vectors, station_index, axis=2), (0, 2, 1, 3))
        contrib = jnp.sum(kernels[None] * picked[:, :, :, :, None], axis=(2, 3))
        return totals + jnp.einsum("bp,vbc->vpc", prism_onehot, contrib, precision=exact)

    start_sums = jnp.zeros((vectors.shape[0], prism_count, 512), jnp.float32)
    partial_value = lax.fori_loop(0, rounds, adjoint_turn, start_sums).reshape(vectors.shape[0], -1)
    gradient = lax.psum_scatter(partial_value, "stn", scatter_dimension=1, tiled=True)[0]
    norm_next = lax.psum(jnp.sum(gradient * gradient), ("cell", "stn"))
    densities_next = densities + step_size * direction
    direction_next = gradient + norm_next / gradient_norm[0] * direction
    return (densities_next, residual_next, direction_next, norm_next.reshape(1))


def solution(mesh):
    in_specs = (
        P(("survey", "cell", "stn")),
        P(None, ("survey", "cell", "stn")),
        P(("survey", "cell", "stn")),
        P("survey"),
        P(None, ("survey", "cell", "stn")),
        P(None, ("survey", "cell", "stn")),
        P(("survey", "cell"), "stn", None),
        P(("survey", "cell"), "stn", None),
        P(("survey", "cell"), "stn"),
    )
    out_specs = (
        P(("survey", "cell", "stn")),
        P(None, ("survey", "cell", "stn")),
        P(("survey", "cell", "stn")),
        P("survey"),
    )
    return jax.shard_map(
        on_device, mesh=mesh, in_specs=in_specs, out_specs=out_specs, check_vma=False
    )
```

profile of v0, /device:TPU:0, one launch (start us, length us, event | category | flops | bytes accessed | tf_op | source)
XLA Modules:
  0.0 1491.4 jit_solution(16384390619523279447)
XLA Ops:
  7.9 6.4 all_gather.13
  14.3 14.0 all_gather.12
  28.3 5.3 all_gather.14
  33.7 658.7 %while.22 = (s32[]{:T(128)}, f32[6,16,128]{2,1,0:T(8,128)S(1)}, s32[]{:T(128)}, s32[256]{0:T(256)}, f32[3,16,128]{2,0,1:T(4,128)S(1)}, /*index=5*/s32[256]{0:T(2...) while((s32[]{:T(128)}, f32[6,16,128]{2,1,0:T(8,128)S(1)}, ...), condition=%wide.region_2.5_spmd.clone, body=%wide.region_0.4_spmd.clone.sunk | while | flops 106210080 | bytes 52372616 | solution.py:83
  49.8 4.8 fusion.98
  64.5 9.5 multiply_reduce_fusion.4
  91.0 4.8 fusion.98
  105.7 9.5 multiply_reduce_fusion.4
  132.1 4.8 fusion.98
  146.8 9.5 multiply_reduce_fusion.4
  173.3 4.8 fusion.98
  188.0 9.5 multiply_reduce_fusion.4
  214.5 4.8 fusion.98
  229.2 9.5 multiply_reduce_fusion.4
  255.6 4.8 fusion.98
  270.3 9.5 multiply_reduce_fusion.4
  311.5 9.5 multiply_reduce_fusion.4
  352.7 9.5 multiply_reduce_fusion.4
  393.8 9.5 multiply_reduce_fusion.4
  435.0 9.5 multiply_reduce_fusion.4
  476.2 9.5 multiply_reduce_fusion.4
  517.3 9.5 multiply_reduce_fusion.4
  558.5 9.5 multiply_reduce_fusion.4
  599.7 9.5 multiply_reduce_fusion.4
  640.8 9.5 multiply_reduce_fusion.4
  682.0 9.5 multiply_reduce_fusion.4
  693.0 19.2 %reduce-scatter.5.cloned.1.call-done = f32[6,512]{1,0:T(8,128)} async-done(((f32[6,2048]{1,0:T(8,128)}), f32[6,512]{1,0:T(8,128)}) %reduce-scatter.5.cloned.1.call-update) | async-done | bytes 12304 | tf_op jit(solution)/shard_map/reduce_scatter | solution.py:86
  714.2 30.1 %psum.14 = f32[]{:T(128)} all-reduce(f32[]{:T(128)} %multiply_reduce_fusion.1), channel_id=1, replica_groups=mesh['survey'=2,'cell'=4,'stn'=4] {'cell','stn'}, use_global_device_ids=true, to_apply=%region_5.8 | all-reduce | flops 1 | bytes 8 | tf_op jit(solution)/shard_map/psum | solution.py:88
  745.7 13.2 all_gather.15
  758.9 660.0 %while.23 = (s32[]{:T(128)}, f32[1,8,512]{2,1,0:T(8,128)S(1)}, s32[]{:T(128)}, s32[256]{0:T(256)}, f32[3,16,128]{2,0,1:T(4,128)S(1)}, /*index=5*/s32[256]{0:T(25...) while((s32[]{:T(128)}, f32[1,8,512]{2,1,0:T(8,128)S(1)}, ...), condition=%wide.region_8.11_spmd.clone, body=%wide.region_6.10_spmd.clone.sunk | while | flops 104636960 | bytes 52454536 | solution.py:101
  789.8 9.6 fusion.113
  831.1 9.6 fusion.113
  872.3 9.6 fusion.113
  913.6 9.6 fusion.113
  954.8 9.6 fusion.113
  996.0 9.6 fusion.113
  1037.3 9.6 fusion.113
  1078.5 9.6 fusion.113
  1119.8 9.6 fusion.113
  1161.0 9.6 fusion.113
  1202.2 9.6 fusion.113
  1243.5 9.6 fusion.113
  1284.7 9.6 fusion.113
  1326.0 9.6 fusion.113
  1367.2 9.6 fusion.113
  1408.4 9.6 fusion.113
  1421.2 27.4 %reduce-scatter.7.cloned.1.call-done = f32[1024,1]{1,0:T(8,128)} async-done(((f32[4096,1]{1,0:T(8,128)}), f32[1024,1]{1,0:T(8,128)}) %reduce-scatter.7.cloned.1.call-update) | async-done | bytes 4112
  1450.4 32.9 %psum.15 = f32[]{:T(128)} all-reduce(f32[]{:T(128)} %multiply_reduce_fusion.2), channel_id=1, replica_groups=mesh['survey'=2,'cell'=4,'stn'=4] {'cell','stn'}, use_global_device_ids=true, to_apply=%region_11.14 | all-reduce | flops 1 | bytes 8 | tf_op jit(solution)/shard_map/psum | solution.py:103
  (770 shorter events, 988.8 us)
Async XLA Ops:
  7.2 705.0 %reduce-scatter.5.cloned.1.call-start = ((), (), s32[]{:S(2)}) async-start(), calls=%async_computation.2 | async-start | bytes 81920 | tf_op jit(solution)/shard_map/reduce_scatter | solution.py:86
  33.7 711.3 %copy-start.1 = (f32[6,512]{1,0:T(8,128)S(1)}, f32[6,512]{1,0:T(8,128)}, u32[]{:S(2)}) copy-start(f32[6,512]{1,0:T(8,128)} %param.18) | copy-start | bytes 36868
  693.0 755.6 %reduce-scatter.7.cloned.1.call-start = ((), (), s32[]{:S(2)}) async-start(), calls=%async_computation.3 | async-start | bytes 2621440
  745.7 13.2 copy-start
  1419.0 65.0 %copy-start.2 = (f32[1024]{0:T(1024)S(1)}, f32[1024]{0:T(1024)}, u32[]{:S(2)}) copy-start(f32[1024]{0:T(1024)} %param.19) | copy-start | bytes 12292
  1419.0 65.0 %copy-start.3 = (f32[1024]{0:T(1024)S(1)}, f32[1024]{0:T(1024)}, u32[]{:S(2)}) copy-start(f32[1024]{0:T(1024)} %param.17) | copy-start | bytes 12292
Sparse Core Ops, SparseCore 0:
  693.1 19.0 reduce-scatter.4
  1421.3 27.2 reduce-scatter.6
where the time goes:
time: 1490 us
  other arithmetic  1250 us (84%)
  blocking collectives  102 us (7%)
  local copies, waits for them, and re-layouts  64.5 us (4%)
  waiting for transfers between devices  46.6 us (3%)
  between operations  16.8 us (1%)
    while x160, other arithmetic  736 us
    reduce_sum x16, other arithmetic, adjoint_turn(): contrib = jnp.sum(kernels[None] * picked[:, :, :, :, None], axis=(2, 3))  153 us
    another operation x32, other arithmetic, tile_kernel(): jnp.stack([(3.0 * offset_x * offset_x - squared) * falloff, 3.0 * offset_...  152 us
    reduce_sum x16, other arithmetic, forward_turn(): contrib = jnp.sum(kernels * values[:, None, None, :], axis=3)  151 us
    psum x1, blocking collectives, on_device(): norm_next = lax.psum(jnp.sum(gradient * gradient), ('cell', 'stn'))  32.9 us
    psum x1, blocking collectives, on_device(): norm_image = lax.psum(image_local, ('cell', 'stn'))  30.1 us
  transfers between devices with their start and end apart: 2, of which 2 were waited for; matrix products, arithmetic and copies ran while one was open for 0% of the time, Pallas kernels for 0%

commit v1 on v0

v1 whole, which is shorter than its diff:
```python
import jax
import jax.numpy as jnp
from jax import lax
from jax.experimental import pallas as pl
from jax.experimental.pallas import tpu as pltpu
from jax.sharding import PartitionSpec as P

STATIONS = 128
CELLS = 512
SPAN = 2048
DEPTH = 32
STRENGTH = 0.1
F32 = jnp.float32
BF16 = jnp.bfloat16
NN = (((1,), (0,)), ((), ()))
NT = (((1,), (1,)), ((), ()))
VMEM_BYTES = 56 * 2**20


def rounded(value):
    return value.astype(BF16).astype(F32)


def three_parts(value):
    high = rounded(value)
    middle = rounded(value - high)
    return high, middle, value - high - middle


def multiply(left, right, numbers=NN):
    return lax.dot_general(left, right, numbers, preferred_element_type=F32)


def falloff_parts(squared):
    root = lax.rsqrt(squared)
    second = root * root
    falloff = second * second * root
    high = falloff.astype(BF16)
    return high, (falloff - high.astype(F32)).astype(BF16)


def square_sum(place):
    return place[0:1] * place[0:1] + place[1:2] * place[1:2] + place[2:3] * place[2:3]


def fill_station_rows(rows, place):
    high, middle, low = three_parts(place)
    norms = three_parts(square_sum(place))
    ones = jnp.ones_like(norms[0])
    for at, part in enumerate((high, high, middle, middle, high, low)):
        rows[3 * at : 3 * at + 3, :] = part
    for at, part in enumerate((*norms, ones, ones, ones)):
        rows[18 + at : 19 + at, :] = part
    rows[24:DEPTH, :] = jnp.zeros((DEPTH - 24, place.shape[1]), F32)


def fill_cell_rows(rows, place):
    high, middle, low = three_parts(-2.0 * place)
    norms = three_parts(square_sum(place))
    ones = jnp.ones_like(norms[0])
    for at, part in enumerate((high, middle, high, middle, low, high)):
        rows[3 * at : 3 * at + 3, :] = part
    for at, part in enumerate((ones, ones, ones, *norms)):
        rows[18 + at : 19 + at, :] = part
    rows[24:DEPTH, :] = jnp.zeros((DEPTH - 24, place.shape[1]), F32)


def join(target, pieces, rows):
    at = 0
    for piece in pieces:
        width = piece.shape[1]
        target[0:rows, at : at + width] = piece[0:rows, :]
        at += width


def transpose_into(target, rows):
    for at in range(0, rows.shape[1], 512):
        target[at : at + 512, :] = rows[:, at : at + 512].T.astype(BF16)


def listed_counts(info, station_list, cell_list, station_groups, blocks):
    slots = station_list.shape[1]
    station_total, cell_total = blocks
    per_cell = station_total // station_groups
    station_id = (
        lax.bitwise_xor(station_list[...] // per_cell, info[0]) * per_cell
        + station_list[...] % per_cell
    )
    cell_id = lax.bitwise_xor(cell_list[...] // 2, info[1]) * 2 + cell_list[...] % 2
    live = lax.broadcasted_iota(jnp.int32, (1, slots), 1) < info[2]
    cell_hot = (lax.broadcasted_iota(jnp.int32, (cell_total, slots), 0) == cell_id) & live
    station_hot = lax.broadcasted_iota(jnp.int32, (station_total, slots), 0) == station_id
    count = multiply(cell_hot.astype(F32).astype(BF16), station_hot.astype(F32).astype(BF16), NT)
    wide = (station_total, station_total * STATIONS)
    spread = lax.broadcasted_iota(jnp.int32, wide, 0) == (
        lax.broadcasted_iota(jnp.int32, wide, 1) // STATIONS
    )
    return multiply(count.astype(BF16), spread.astype(F32).astype(BF16))


def forward_kernel(station_pieces, cell_pieces, info, station_list, cell_list, *refs):
    station_refs = refs[:station_pieces]
    cell_refs = refs[station_pieces : station_pieces + cell_pieces]
    image, count, station, cell, station_rows, cell_rows, left, right, source, moments = refs[
        station_pieces + cell_pieces :
    ]
    width, extent = station.shape[1], cell.shape[1]
    join(station, station_refs, 3)
    join(cell, cell_refs, 4)
    count[...] = listed_counts(
        info,
        station_list,
        cell_list,
        width // CELLS,
        (width // STATIONS, extent // CELLS),
    )
    fill_station_rows(station_rows, station[0:3, :])
    right[...] = station_rows[...].astype(BF16)
    fill_cell_rows(cell_rows, cell[0:3, :])
    transpose_into(left, cell_rows)
    value = cell[3:4, :]
    x, y, z = cell[0:1, :], cell[1:2, :], cell[2:3, :]
    vx, vy, vz = value * x, value * y, value * z
    products = (value, vx, vy, vz, vx * x, vx * y, vx * z, vy * y, vy * z, vz * z)
    for at, row in enumerate(products):
        cell_rows[at : at + 1, :] = row
    cell_rows[10:16, :] = jnp.zeros((6, extent), F32)
    parts = three_parts(cell_rows[0:16, :])
    source[...] = jnp.concatenate([part.astype(BF16) for part in parts], axis=0)
    moments[...] = jnp.zeros_like(moments)
    spans = width // SPAN

    def turn(which, carry):
        block = which // spans
        lanes = pl.ds(pl.multiple_of(which % spans * SPAN, SPAN), SPAN)
        cells = pl.ds(pl.multiple_of(block * CELLS, CELLS), CELLS)
        squared = multiply(left[cells, :], right[:, lanes])
        high, low = falloff_parts(squared)
        weights = source[:, cells]
        total = multiply(weights, high) + multiply(weights, low)
        total = total[0:16] + total[16:32] + total[32:48]
        moments[:, lanes] += total * count[pl.ds(block, 1), lanes]
        return carry

    lax.fori_loop(0, spans * (extent // CELLS), turn, 0)
    sx, sy, sz = station[0:1, :], station[1:2, :], station[2:3, :]
    total, mx, my, mz, mxx, mxy, mxz, myy, myz, mzz = (moments[k : k + 1, :] for k in range(10))
    xx = sx * (sx * total - 2.0 * mx) + mxx
    yy = sy * (sy * total - 2.0 * my) + myy
    zz = sz * (sz * total - 2.0 * mz) + mzz
    xy = sx * (sy * total - my) - sy * mx + mxy
    xz = sx * (sz * total - mz) - sz * mx + mxz
    yz = sy * (sz * total - mz) - sz * my + myz
    image[0:1, :] = STRENGTH * (2.0 * xx - yy - zz)
    image[1:2, :] = (3.0 * STRENGTH) * xy
    image[2:3, :] = (3.0 * STRENGTH) * xz
    image[3:4, :] = STRENGTH * (2.0 * yy - xx - zz)
    image[4:5, :] = (3.0 * STRENGTH) * yz
    image[5:6, :] = STRENGTH * (2.0 * zz - xx - yy)
    image[6:8, :] = jnp.zeros((2, width), F32)


def tree(values):
    values = list(values)
    while len(values) > 1:
        values = [values[k] + values[k + 1] for k in range(0, len(values), 2)]
    return values[0]


def adjoint_kernel(station_pieces, cell_pieces, image_pieces, count, *refs):
    station_refs = refs[:station_pieces]
    at = station_pieces + cell_pieces
    cell_refs = refs[station_pieces:at]
    image_refs = refs[at : at + image_pieces]
    partial, own_image, station, cell, image, station_rows, cell_rows, left, right, vectors = refs[
        at + image_pieces :
    ]
    width, extent = station.shape[1], cell.shape[1]
    join(station, station_refs, 9)
    join(cell, cell_refs, 3)
    if image_pieces == 1:
        image[...] = image_refs[0][...]
        norm = jnp.sum(image[...] * image[...])
    else:
        part = width // image_pieces
        norms = []
        for k in range(image_pieces):
            block = tree(
                image_refs[other][:, (k ^ other) * part : ((k ^ other) + 1) * part]
                for other in range(image_pieces)
            )
            image[:, k * part : (k + 1) * part] = block
            norms.append(jnp.sum(block * block))
        norm = tree(norms)
    own_image[...] = image[:, 0 : own_image.shape[1]]
    fill_cell_rows(cell_rows, cell[0:3, :])
    right[...] = cell_rows[...].astype(BF16)
    fill_station_rows(station_rows, station[0:3, :])
    transpose_into(left, station_rows)
    sx, sy, sz = station[0:1, :], station[1:2, :], station[2:3, :]
    for first, source, offset in ((0, station, 3), (10, image, 0)):
        r = [STRENGTH * source[offset + k : offset + k + 1, :] for k in range(6)]
        axx, ayy, azz = 2.0 * r[0] - r[3] - r[5], 2.0 * r[3] - r[0] - r[5], 2.0 * r[5] - r[0] - r[3]
        axy, axz, ayz = 3.0 * r[1], 3.0 * r[2], 3.0 * r[4]
        whole = (
            sx * (axx * sx + axy * sy + axz * sz) + sy * (ayy * sy + ayz * sz) + azz * sz * sz
        )
        bx = 2.0 * axx * sx + axy * sy + axz * sz
        by = 2.0 * ayy * sy + axy * sx + ayz * sz
        bz = 2.0 * azz * sz + axz * sx + ayz * sy
        for k, row in enumerate((whole, bx, by, bz, axx, axy, axz, ayy, ayz, azz)):
            vectors[first + k : first + k + 1, :] = row
    vectors[20:24, :] = jnp.zeros((4, width), F32)
    partial[...] = jnp.zeros_like(partial)
    partial[:, CELLS:] = jnp.full((partial.shape[0], partial.shape[1] - CELLS), norm, F32)
    blocks = extent // CELLS

    def turn(block, carry):
        cells = pl.ds(pl.multiple_of(block * CELLS, CELLS), CELLS)

        def span_turn(which, sums):
            lanes = pl.ds(pl.multiple_of(which * SPAN, SPAN), SPAN)
            squared = multiply(left[lanes, :], right[:, cells])
            high, low = falloff_parts(squared)
            parts = three_parts(vectors[:, lanes] * count[pl.ds(block, 1), lanes])
            weights = jnp.concatenate(parts, axis=0).astype(BF16)
            total = multiply(weights, high) + multiply(weights, low)
            return sums + (total[0:24] + total[24:48] + total[48:72])

        sums = jnp.zeros((24, CELLS), F32)
        if width == SPAN:
            sums = span_turn(0, sums)
        else:
            sums = lax.fori_loop(0, width // SPAN, span_turn, sums)
        x, y, z = cell[0:1, cells], cell[1:2, cells], cell[2:3, cells]
        for vector in range(2):
            whole, bx, by, bz, axx, axy, axz, ayy, ayz, azz = (
                sums[10 * vector + k : 10 * vector + k + 1] for k in range(10)
            )
            value = (
                whole
                + x * (x * axx + y * axy + z * axz - bx)
                + y * (y * ayy + z * ayz - by)
                + z * (z * azz - bz)
            )
            partial[pl.ds(vector * blocks + block, 1), 0:CELLS] = value
        return carry

    lax.fori_loop(0, blocks, turn, 0)


def update_kernel(pieces, gradient_norm, densities, direction, residual, image, *refs):
    partial_refs = refs[:pieces]
    densities_next, residual_next, gradient, norm = refs[pieces:]
    blocks = partial_refs[0].shape[0] // 2
    each = blocks // pieces
    step = gradient_norm[0] / tree(ref[0:1, CELLS : CELLS + 1] for ref in partial_refs)
    sums = []
    for k in range(pieces):
        both = [
            tree(
                partial_refs[other][
                    vector * blocks + (k ^ other) * each : vector * blocks + ((k ^ other) + 1) * each,
                    0:CELLS,
                ]
                for other in range(pieces)
            )
            for vector in range(2)
        ]
        block = both[0] - step * both[1]
        sums.append(jnp.sum(block * block, axis=(0, 1), keepdims=True))
        if k == 0:
            across = CELLS // 128
            for b in range(each):
                for u in range(across):
                    at = b * across + u
                    gradient[at : at + 1, :] = block[b : b + 1, u * 128 : (u + 1) * 128]
    norm[...] = jnp.broadcast_to(tree(sums), norm.shape)
    densities_next[...] = densities[...] + step * direction[...]
    residual_next[...] = residual[...] - step * image[0:6, :]


def exchanged(value, axis, size):
    return [value] + [
        lax.ppermute(value, axis, [(rank, rank ^ other) for rank in range(size)])
        for other in range(1, size)
    ]


def on_device(
    densities,
    residual,
    direction,
    gradient_norm,
    station_place,
    cell_place,
    station_blocks,
    cell_blocks,
    pair_count,
):
    cell_size, stn_size = lax.axis_size("cell"), lax.axis_size("stn")
    direct = cell_size <= 4
    station_own = jnp.concatenate([station_place, residual], axis=0)
    cell_own = jnp.concatenate([cell_place, direction[None]], axis=0)
    cell_parts = exchanged(cell_own, "stn", stn_size)
    if direct:
        station_parts = exchanged(station_own, "cell", cell_size)
        cell_rank = lax.axis_index("cell")
    else:
        station_parts = [lax.all_gather(station_own, "cell", axis=1, tiled=True)]
        cell_rank = jnp.int32(0)
    info = jnp.stack([cell_rank, lax.axis_index("stn"), pair_count.reshape(())])
    width = cell_size * station_own.shape[1]
    extent = stn_size * cell_own.shape[1]
    blocks = extent // CELLS
    in_vmem, in_smem = pl.BlockSpec(memory_space=pltpu.VMEM), pl.BlockSpec(memory_space=pltpu.SMEM)
    params = pltpu.CompilerParams(vmem_limit_bytes=VMEM_BYTES)
    pieces = len(station_parts) + len(cell_parts)

    def forward(*refs):
        forward_kernel(len(station_parts), len(cell_parts), *refs)

    image_part, count = pl.pallas_call(
        forward,
        out_shape=(
            jax.ShapeDtypeStruct((8, width), F32),
            jax.ShapeDtypeStruct((blocks, width), F32),
        ),
        in_specs=[in_smem] + [in_vmem] * (2 + pieces),
        out_specs=(in_vmem, in_vmem),
        scratch_shapes=[
            pltpu.VMEM((8, width), F32),
            pltpu.VMEM((8, extent), F32),
            pltpu.VMEM((DEPTH, width), F32),
            pltpu.VMEM((DEPTH, extent), F32),
            pltpu.VMEM((extent, DEPTH), BF16),
            pltpu.VMEM((DEPTH, width), BF16),
            pltpu.VMEM((48, extent), BF16),
            pltpu.VMEM((16, width), F32),
        ],
        compiler_params=params,
        name="forward",
    )(
        info,
        station_blocks.reshape(1, -1),
        cell_blocks.reshape(1, -1),
        *station_parts,
        *cell_parts,
    )
    if direct:
        image_parts = exchanged(image_part, "cell", cell_size)
    else:
        image_parts = [lax.psum(image_part, "cell")]

    def adjoint(*refs):
        adjoint_kernel(len(station_parts), len(cell_parts), len(image_parts), *refs)

    own = station_own.shape[1]
    partial, image_own = pl.pallas_call(
        adjoint,
        out_shape=(
            jax.ShapeDtypeStruct((2 * blocks, CELLS + 128), F32),
            jax.ShapeDtypeStruct((8, own if direct else width), F32),
        ),
        in_specs=[in_vmem] * (1 + pieces + len(image_parts)),
        out_specs=(in_vmem, in_vmem),
        scratch_shapes=[
            pltpu.VMEM((16, width), F32),
            pltpu.VMEM((8, extent), F32),
            pltpu.VMEM((8, width), F32),
            pltpu.VMEM((DEPTH, width), F32),
            pltpu.VMEM((DEPTH, extent), F32),
            pltpu.VMEM((width, DEPTH), BF16),
            pltpu.VMEM((DEPTH, extent), BF16),
            pltpu.VMEM((24, width), F32),
        ],
        compiler_params=params,
        name="adjoint",
    )(count, *station_parts, *cell_parts, *image_parts)
    if not direct:
        image_own = lax.dynamic_slice_in_dim(image_own, lax.axis_index("cell") * own, own, axis=1)
    partial_parts = exchanged(partial, "stn", stn_size)
    shape = (-1, 128)

    def update(*refs):
        update_kernel(stn_size, *refs)

    flat = direction.reshape(shape)
    densities_next, residual_next, gradient, norm_part = pl.pallas_call(
        update,
        out_shape=(
            jax.ShapeDtypeStruct(flat.shape, F32),
            jax.ShapeDtypeStruct(residual.shape, F32),
            jax.ShapeDtypeStruct(flat.shape, F32),
            jax.ShapeDtypeStruct((1, 128), F32),
        ),
        in_specs=[in_smem] + [in_vmem] * (4 + stn_size),
        out_specs=(in_vmem,) * 4,
        name="update",
    )(gradient_norm, densities.reshape(shape), flat, residual, image_own, *partial_parts)
    if direct:
        norm_next = tree(exchanged(norm_part, "cell", cell_size))
    else:
        norm_next = lax.psum(norm_part, "cell")
    direction_next = gradient + norm_next / gradient_norm[0] * flat
    return (
        densities_next.reshape(-1),
        residual_next,
        direction_next.reshape(-1),
        norm_next[0, 0:1],
    )


def solution(mesh):
    in_specs = (
        P(("survey", "cell", "stn")),
        P(None, ("survey", "cell", "stn")),
        P(("survey", "cell", "stn")),
        P("survey"),
        P(None, ("survey", "cell", "stn")),
        P(None, ("survey", "cell", "stn")),
        P(("survey", "cell"), "stn", None),
        P(("survey", "cell"), "stn", None),
        P(("survey", "cell"), "stn"),
    )
    out_specs = (
        P(("survey", "cell", "stn")),
        P(None, ("survey", "cell", "stn")),
        P(("survey", "cell", "stn")),
        P("survey"),
    )
    return jax.shard_map(
        on_device, mesh=mesh, in_specs=in_specs, out_specs=out_specs, check_vma=False
    )
```

time: 1490 us -> 73 us (0.05)
  other arithmetic: 1250 us -> 2.53 us
  blocking collectives: 102 us -> 0 us
  local copies, waits for them, and re-layouts: 64.5 us -> 2.72 us
  Pallas kernels: 0 us -> 33.1 us
  waiting for transfers between devices: 46.6 us -> 13.6 us
  starting transfers between devices: 0.08 us -> 18.5 us
    while x160 -> x0, other arithmetic: 736 us -> none
    reduce_sum x34 -> x0, other arithmetic: 306 us -> none  [the longest x16 153 us: adjoint_turn(): contrib = jnp.sum(kernels[None] * picked[:, :, :, :, None], axis=(2, 3))]
    another operation x32 -> x1, other arithmetic: 152 us -> 0.66 us  [on_device(): info = jnp.stack([cell_rank, lax.axis_index('stn'), pair_count.reshape(())])]
    psum x2 -> x0, blocking collectives: 63 us -> none  [the longest x1 32.9 us: on_device(): norm_next = lax.psum(jnp.sum(gradient * gradient), ('cell', 'stn'))]
    gather x96 -> x0, local copies, waits for them, and re-layouts: 57 us -> none  [the longest x32 20 us: batch_of(): jnp.take(prism_tiles, prism_index, axis=1)]
    all_gather x4 -> x0, blocking collectives: 38.9 us -> none  [the longest x1 14 us: on_device(): station_all = lax.all_gather(station_place, 'cell', axis=1, tiled=True)]
    pallas_call x0 -> x3, Pallas kernels: none -> 33.1 us  [the longest x1 16.3 us: on_device(): pl.pallas_call(adjoint, out_shape=(jax.ShapeDtypeStruct((2 * blocks, CELL...]
    unnamed x3 -> x0, waiting for transfers between devices: 27.5 us -> none
  transfers between devices with their start and end apart: 2 -> 15, of which waited for: 2 -> 10; matrix products, arithmetic and copies ran while one was open for 0% -> 1% of each run, Pallas kernels for 0% -> 0%
where the time goes in v1:
time: 73 us; the launch traced here: 72.5 us
  Pallas kernels  33.1 us (45%)
  starting transfers between devices  18.5 us (25%)
  waiting for transfers between devices  13.6 us (19%)
  local copies, waits for them, and re-layouts  2.72 us (4%)
  other arithmetic  2.53 us (3%)
  between operations  2.05 us (3%)
    ppermute x15, starting transfers between devices, exchanged(): lax.ppermute(value, axis, [(rank, rank ^ other) for rank in range(size)])  18.5 us
    pallas_call x1, Pallas kernels, on_device(): pl.pallas_call(adjoint, out_shape=(jax.ShapeDtypeStruct((2 * blocks, CELL...  16.3 us
    pallas_call x1, Pallas kernels, on_device(): pl.pallas_call(forward, out_shape=(jax.ShapeDtypeStruct((8, width), F32),...  15.2 us
    ppermute x15, waiting for transfers between devices, exchanged(): lax.ppermute(value, axis, [(rank, rank ^ other) for rank in range(size)])  13.6 us
    unnamed x38, local copies, waits for them, and re-layouts  2.72 us
    pallas_call x1, Pallas kernels, on_device(): pl.pallas_call(update, out_shape=(jax.ShapeDtypeStruct(flat.shape, F32),...  1.63 us
  transfers between devices with their start and end apart: 15, of which 10 were waited for; matrix products, arithmetic and copies ran while one was open for 1% of the time, Pallas kernels for 0%

profile of v1, /device:TPU:0, one launch (start us, length us, event | category | flops | bytes accessed | tf_op | source)
XLA Modules:
  0.0 72.5 jit_solution(3934686069877544224)
XLA Ops:
  0.6 0.0 copy-start.5
  0.7 0.8 %pad_maximum_fusion.1.refs_7_.refs_5_ = f32[4,1024]{1,0:T(4,128)S(1)} fusion(f32[1,1024]{1,0:T(1,128)} %bitcast.19, f32[3,1024]{1,0:T(4,128)} %param.14), kind=kLoop, calls=%fused_computation.1 | loop fusion | flops 4096 | bytes 32768 | tf_op jit(solution)/shard_map/concatenate | solution.py:304
  1.4 0.0 copy-start.1
  1.4 0.5 collective-permute-start.3
  2.0 2.7 %collective-permute-start = (f32[9,512]{1,0:T(8,128)S(1)}, f32[9,512]{1,0:T(8,128)S(1)}, u32[]{:S(2)}, u32[]{:S(2)}) collective-permute-start(f32[9,512]{1,0:T(8,128)S(1)} %pad_maximum_fusion.refs_3_.refs_1_), channel_id=1, source_target_pairs={{0,4},{4,0},{8,12},{12,8},{1,5},{5,1},{9,13},{13,9},{2,6},{6,2},{1... | collective-permute-start | bytes 55304 | tf_op jit(solution)/shard_map/ppermute | solution.py:285
  4.6 2.6 %collective-permute-start.1 = (f32[9,512]{1,0:T(8,128)S(1)}, f32[9,512]{1,0:T(8,128)S(1)}, u32[]{:S(2)}, u32[]{:S(2)}) collective-permute-start(f32[9,512]{1,0:T(8,128)S(1)} %pad_maximum_fusion.refs_3_.refs_1_), channel_id=1, source_target_pairs={{0,8},{4,12},{8,0},{12,4},{1,9},{5,13},{9,1},{13,5},{2,10},{6,14},... | collective-permute-start | bytes 55304 | tf_op jit(solution)/shard_map/ppermute | solution.py:285
  7.2 0.0 collective-permute-start.2
  7.2 1.7 %collective-permute-start.4 = (f32[4,1024]{1,0:T(4,128)S(1)}, f32[4,1024]{1,0:T(4,128)S(1)}, u32[]{:S(2)}, u32[]{:S(2)}) collective-permute-start(f32[4,1024]{1,0:T(4,128)S(1)} %pad_maximum_fusion.1.refs_7_.refs_5_), channel_id=1, source_target_pairs={{0,2},{1,3},{2,0},{3,1},{4,6},{5,7},{6,4},{7,5},{8,10},{9,11},{10,... | collective-permute-start | bytes 49160 | tf_op jit(solution)/shard_map/ppermute | solution.py:285
  9.6 0.0 collective-permute-done.3.refs_8_.refs_6_
  9.6 0.1 collective-permute-start.5
  9.7 0.7 pad_add_fusion.refs_0_
  10.4 0.6 collective-permute-done.4.refs_9_.refs_7_
  11.0 1.9 %collective-permute-done.5.refs_10_.refs_8_ = f32[4,1024]{1,0:T(4,128)S(1)} collective-permute-done((f32[4,1024]{1,0:T(4,128)S(1)}, f32[4,1024]{1,0:T(4,128)S(1)}, u32[]{:S(2)}, u32[]{:S(2)}) %collective-permute-start.5) | collective-permute-done | bytes 16416 | tf_op jit(solution)/shard_map/ppermute | solution.py:285
  12.9 0.0 collective-permute-done.1.refs_5_.refs_3_
  12.9 0.1 collective-permute-done.2.refs_6_.refs_4_
  13.0 0.5 copy-done.8
  13.5 0.0 copy-done.2
  13.5 0.0 copy-done.3
  13.5 0.1 copy-done.4
  13.6 15.2 %forward.1 = (f32[8,2048]{1,0:T(8,128)}, f32[8,2048]{1,0:T(8,128)}) custom-call(s32[3]{0:T(128)} %pad_add_fusion.refs_0_, s32[1,256]{1,0:T(1,128)} %bitcast.22, s32[1,256]{1,0:T(1,128)} %bitcast.23, f32[9,512]{1,0:T(8,128)} %copy-done, f32[9,512]{1,0:T(8,128)} %copy-done.2, f32[9,512]{1,0:T(8,128)} %copy-done.3, f32[9,512]{1,0:T(8,128)} %copy-done.4, ...), custom_call_target="tpu_custom_call" | custom-call | tf_op jit(solution)/shard_map/forward/pallas_call | solution.py:323
  28.8 0.6 collective-permute-start.6
  29.4 3.5 %collective-permute-start.7 = (f32[8,2048]{1,0:T(8,128)}, f32[8,2048]{1,0:T(8,128)S(1)}, u32[]{:S(2)}, u32[]{:S(2)}) collective-permute-start(f32[8,2048]{1,0:T(8,128)} %get-tuple-element.13.refs_9_), channel_id=1, source_target_pairs={{0,8},{4,12},{8,0},{12,4},{1,9},{5,13},{9,1},{13,5},{2,10},{6,14},... | collective-permute-start | bytes 196616 | tf_op jit(solution)/shard_map/ppermute | solution.py:285
  32.9 0.3 collective-permute-start.8
  33.2 0.6 collective-permute-done.6.refs_10_
  33.7 3.6 %collective-permute-done.7.refs_11_ = f32[8,2048]{1,0:T(8,128)S(1)} collective-permute-done((f32[8,2048]{1,0:T(8,128)}, f32[8,2048]{1,0:T(8,128)S(1)}, u32[]{:S(2)}, u32[]{:S(2)}) %collective-permute-start.7) | collective-permute-done | bytes 65568 | tf_op jit(solution)/shard_map/ppermute | solution.py:285
  37.3 1.9 %collective-permute-done.8.refs_12_ = f32[8,2048]{1,0:T(8,128)S(1)} collective-permute-done((f32[8,2048]{1,0:T(8,128)}, f32[8,2048]{1,0:T(8,128)S(1)}, u32[]{:S(2)}, u32[]{:S(2)}) %collective-permute-start.8) | collective-permute-done | bytes 65568 | tf_op jit(solution)/shard_map/ppermute | solution.py:285
  39.2 0.6 copy-done.11
  39.8 16.3 %adjoint.1 = (f32[16,640]{1,0:T(8,128)}, f32[8,512]{1,0:T(8,128)}) custom-call(f32[8,2048]{1,0:T(8,128)} %get-tuple-element.12.refs_0_, f32[9,512]{1,0:T(8,128)} %copy-done, f32[9,512]{1,0:T(8,128)} %copy-done.2, f32[9,512]{1,0:T(8,128)} %copy-done.3, f32[9,512]{1,0:T(8,128)} %copy-done.4, f32[4,1024]{1,0:T(4,128)} %copy-done.1, f32[4,1024]{1,0:T(4,128)} %copy-done.6, ...), custom_call_target="tpu_custom_call" | custom-call | tf_op jit(solution)/shard_map/adjoint/pallas_call | solution.py:359
  56.1 0.7 %collective-permute-start.10 = (f32[16,640]{1,0:T(8,128)}, f32[16,640]{1,0:T(8,128)S(1)}, u32[]{:S(2)}, u32[]{:S(2)}) collective-permute-start(f32[16,640]{1,0:T(8,128)} %get-tuple-element.15.refs_5_), channel_id=1, source_target_pairs={{0,2},{1,3},{2,0},{3,1},{4,6},{5,7},{6,4},{7,5},{8,10},{9,11},{10,... | collective-permute-start | bytes 122888 | tf_op jit(solution)/shard_map/ppermute | solution.py:285
  56.8 0.0 collective-permute-start.11
  56.8 1.4 %collective-permute-start.9 = (f32[16,640]{1,0:T(8,128)}, f32[16,640]{1,0:T(8,128)S(1)}, u32[]{:S(2)}, u32[]{:S(2)}) collective-permute-start(f32[16,640]{1,0:T(8,128)} %get-tuple-element.15.refs_5_), channel_id=1, source_target_pairs={{0,1},{1,0},{2,3},{3,2},{4,5},{5,4},{6,7},{7,6},{8,9},{9,8},{10,11... | collective-permute-start | bytes 122888 | tf_op jit(solution)/shard_map/ppermute | solution.py:285
  58.9 1.7 %collective-permute-done.10.refs_7_ = f32[16,640]{1,0:T(8,128)S(1)} collective-permute-done((f32[16,640]{1,0:T(8,128)}, f32[16,640]{1,0:T(8,128)S(1)}, u32[]{:S(2)}, u32[]{:S(2)}) %collective-permute-start.10) | collective-permute-done | bytes 40992 | tf_op jit(solution)/shard_map/ppermute | solution.py:285
  60.6 0.3 collective-permute-done.11.refs_8_
  60.9 0.3 copy-done.12
  61.2 0.3 copy-done.13
  61.5 0.0 copy-done.14
  61.5 1.6 %update.1 = (f32[8,128]{1,0:T(8,128)}, f32[6,512]{1,0:T(8,128)}, f32[8,128]{1,0:T(8,128)}, f32[1,128]{1,0:T(1,128)}) custom-call(f32[1]{0:T(128)} %copy.13.refs_0_, f32[8,128]{1,0:T(8,128)} %bitcast.21, f32[8,128]{1,0:T(8,128)} %bitcast.20, f32[6,512]{1,0:T(8,128)} %refs_3_.1, f32[8,512]{1,0:T(8,128)} %get-tuple-element.14.refs_4_, ...), custom_call_target="tpu_custom_call" | custom-call | tf_op jit(solution)/shard_map/update/pallas_call | solution.py:389
  63.1 0.7 copy-done.18
  63.8 0.3 collective-permute-start.12
  64.1 1.7 %collective-permute-start.13 = (f32[1,128]{1,0:T(1,128)S(1)}, f32[1,128]{1,0:T(1,128)S(1)}, u32[]{:S(2)}, u32[]{:S(2)}) collective-permute-start(f32[1,128]{1,0:T(1,128)S(1)} %copy-done.18), channel_id=1, source_target_pairs={{0,8},{4,12},{8,0},{12,4},{1,9},{5,13},{9,1},{13,5},{2,10},{6,14},... | collective-permute-start | bytes 1544 | tf_op jit(solution)/shard_map/ppermute | solution.py:285
  65.9 2.3 %collective-permute-start.14 = (f32[1,128]{1,0:T(1,128)S(1)}, f32[1,128]{1,0:T(1,128)S(1)}, u32[]{:S(2)}, u32[]{:S(2)}) collective-permute-start(f32[1,128]{1,0:T(1,128)S(1)} %copy-done.18), channel_id=1, source_target_pairs={{0,12},{4,8},{8,4},{12,0},{1,13},{5,9},{9,5},{13,1},{2,14},{6,10},... | collective-permute-start | bytes 1544 | tf_op jit(solution)/shard_map/ppermute | solution.py:285
  68.2 0.0 collective-permute-done.12
  68.2 0.4 collective-permute-done.13
  68.6 2.6 %collective-permute-done.14 = f32[1,128]{1,0:T(1,128)S(1)} collective-permute-done((f32[1,128]{1,0:T(1,128)S(1)}, f32[1,128]{1,0:T(1,128)S(1)}, u32[]{:S(2)}, u32[]{:S(2)}) %collective-permute-start.14) | collective-permute-done | bytes 544 | tf_op jit(solution)/shard_map/ppermute | solution.py:285
  71.2 0.5 divide_bitcast_fusion
  71.7 0.2 copy-done.17
  71.9 0.0 copy-done.15
  71.9 0.6 add_bitcast_fusion
  (28 shorter events, 0.1 us)
Async XLA Ops:
  0.6 1.3 %copy-start.5 = (f32[6,512]{1,0:T(8,128)S(1)}, f32[6,512]{1,0:T(8,128)}, u32[]{:S(2)}) copy-start(f32[6,512]{1,0:T(8,128)} %refs_3_.1) | copy-start | bytes 36868
  0.6 1.3 %copy-start.16 = (f32[3,512]{1,0:T(4,128)S(1)}, f32[3,512]{1,0:T(4,128)}, u32[]{:S(2)}) copy-start(f32[3,512]{1,0:T(4,128)} %param.13) | copy-start | bytes 18436
  1.4 8.2 %copy-start.1 = (f32[4,1024]{1,0:T(4,128)}, f32[4,1024]{1,0:T(4,128)S(1)}, u32[]{:S(2)}) copy-start(f32[4,1024]{1,0:T(4,128)S(1)} %pad_maximum_fusion.1.refs_7_.refs_5_) | copy-start | bytes 49156
  1.4 8.2 %collective-permute-start.3 = (f32[4,1024]{1,0:T(4,128)S(1)}, f32[4,1024]{1,0:T(4,128)S(1)}, u32[]{:S(2)}, u32[]{:S(2)}) collective-permute-start(f32[4,1024]{1,0:T(4,128)S(1)} %pad_maximum_fusion.1.refs_7_.refs_5_), channel_id=1, source_target_pairs={{0,1},{1,0},{2,3},{3,2},{4,5},{5,4},{6,7},{7,6},{8,9},{9,8},{10,11... | collective-permute-start | bytes 49160 | tf_op jit(solution)/shard_map/ppermute | solution.py:285
  2.0 11.0 %copy-start = (f32[9,512]{1,0:T(8,128)}, f32[9,512]{1,0:T(8,128)S(1)}, u32[]{:S(2)}) copy-start(f32[9,512]{1,0:T(8,128)S(1)} %pad_maximum_fusion.refs_3_.refs_1_) | copy-start | bytes 55300
  2.0 10.9 %collective-permute-start = (f32[9,512]{1,0:T(8,128)S(1)}, f32[9,512]{1,0:T(8,128)S(1)}, u32[]{:S(2)}, u32[]{:S(2)}) collective-permute-start(f32[9,512]{1,0:T(8,128)S(1)} %pad_maximum_fusion.refs_3_.refs_1_), channel_id=1, source_target_pairs={{0,4},{4,0},{8,12},{12,8},{1,5},{5,1},{9,13},{13,9},{2,6},{6,2},{1... | collective-permute-start | bytes 55304 | tf_op jit(solution)/shard_map/ppermute | solution.py:285
  4.6 8.2 %collective-permute-start.1 = (f32[9,512]{1,0:T(8,128)S(1)}, f32[9,512]{1,0:T(8,128)S(1)}, u32[]{:S(2)}, u32[]{:S(2)}) collective-permute-start(f32[9,512]{1,0:T(8,128)S(1)} %pad_maximum_fusion.refs_3_.refs_1_), channel_id=1, source_target_pairs={{0,8},{4,12},{8,0},{12,4},{1,9},{5,13},{9,1},{13,5},{2,10},{6,14},... | collective-permute-start | bytes 55304 | tf_op jit(solution)/shard_map/ppermute | solution.py:285
  7.2 5.7 %collective-permute-start.2 = (f32[9,512]{1,0:T(8,128)S(1)}, f32[9,512]{1,0:T(8,128)S(1)}, u32[]{:S(2)}, u32[]{:S(2)}) collective-permute-start(f32[9,512]{1,0:T(8,128)S(1)} %pad_maximum_fusion.refs_3_.refs_1_), channel_id=1, source_target_pairs={{0,12},{4,8},{8,4},{12,0},{1,13},{5,9},{9,5},{13,1},{2,14},{6,10},... | collective-permute-start | bytes 55304 | tf_op jit(solution)/shard_map/ppermute | solution.py:285
  7.2 3.7 %collective-permute-start.4 = (f32[4,1024]{1,0:T(4,128)S(1)}, f32[4,1024]{1,0:T(4,128)S(1)}, u32[]{:S(2)}, u32[]{:S(2)}) collective-permute-start(f32[4,1024]{1,0:T(4,128)S(1)} %pad_maximum_fusion.1.refs_7_.refs_5_), channel_id=1, source_target_pairs={{0,2},{1,3},{2,0},{3,1},{4,6},{5,7},{6,4},{7,5},{8,10},{9,11},{10,... | collective-permute-start | bytes 49160 | tf_op jit(solution)/shard_map/ppermute | solution.py:285
  9.6 3.3 %copy-start.6 = (f32[4,1024]{1,0:T(4,128)}, f32[4,1024]{1,0:T(4,128)S(1)}, u32[]{:S(2)}) copy-start(f32[4,1024]{1,0:T(4,128)S(1)} %collective-permute-done.3.refs_8_.refs_6_) | copy-start | bytes 49156
  9.6 3.2 %collective-permute-start.5 = (f32[4,1024]{1,0:T(4,128)S(1)}, f32[4,1024]{1,0:T(4,128)S(1)}, u32[]{:S(2)}, u32[]{:S(2)}) collective-permute-start(f32[4,1024]{1,0:T(4,128)S(1)} %pad_maximum_fusion.1.refs_7_.refs_5_), channel_id=1, source_target_pairs={{0,3},{1,2},{2,1},{3,0},{4,7},{5,6},{6,5},{7,4},{8,11},{9,10},{10,... | collective-permute-start | bytes 49160 | tf_op jit(solution)/shard_map/ppermute | solution.py:285
  11.0 2.0 %copy-start.7 = (f32[4,1024]{1,0:T(4,128)}, f32[4,1024]{1,0:T(4,128)S(1)}, u32[]{:S(2)}) copy-start(f32[4,1024]{1,0:T(4,128)S(1)} %collective-permute-done.4.refs_9_.refs_7_) | copy-start | bytes 49156
  12.9 0.6 copy-start.8
  12.9 0.6 copy-start.2
  12.9 0.6 copy-start.3
  12.9 0.6 copy-start.4
  28.8 5.0 %collective-permute-start.6 = (f32[8,2048]{1,0:T(8,128)}, f32[8,2048]{1,0:T(8,128)S(1)}, u32[]{:S(2)}, u32[]{:S(2)}) collective-permute-start(f32[8,2048]{1,0:T(8,128)} %get-tuple-element.13.refs_9_), channel_id=1, source_target_pairs={{0,4},{4,0},{8,12},{12,8},{1,5},{5,1},{9,13},{13,9},{2,6},{6,2},{1... | collective-permute-start | bytes 196616 | tf_op jit(solution)/shard_map/ppermute | solution.py:285
  29.4 7.9 %collective-permute-start.7 = (f32[8,2048]{1,0:T(8,128)}, f32[8,2048]{1,0:T(8,128)S(1)}, u32[]{:S(2)}, u32[]{:S(2)}) collective-permute-start(f32[8,2048]{1,0:T(8,128)} %get-tuple-element.13.refs_9_), channel_id=1, source_target_pairs={{0,8},{4,12},{8,0},{12,4},{1,9},{5,13},{9,1},{13,5},{2,10},{6,14},... | collective-permute-start | bytes 196616 | tf_op jit(solution)/shard_map/ppermute | solution.py:285
  32.9 6.3 %collective-permute-start.8 = (f32[8,2048]{1,0:T(8,128)}, f32[8,2048]{1,0:T(8,128)S(1)}, u32[]{:S(2)}, u32[]{:S(2)}) collective-permute-start(f32[8,2048]{1,0:T(8,128)} %get-tuple-element.13.refs_9_), channel_id=1, source_target_pairs={{0,12},{4,8},{8,4},{12,0},{1,13},{5,9},{9,5},{13,1},{2,14},{6,10},... | collective-permute-start | bytes 196616 | tf_op jit(solution)/shard_map/ppermute | solution.py:285
  33.7 5.4 %copy-start.9 = (f32[8,2048]{1,0:T(8,128)}, f32[8,2048]{1,0:T(8,128)S(1)}, u32[]{:S(2)}) copy-start(f32[8,2048]{1,0:T(8,128)S(1)} %collective-permute-done.6.refs_10_) | copy-start | bytes 196612
  37.3 1.9 %copy-start.10 = (f32[8,2048]{1,0:T(8,128)}, f32[8,2048]{1,0:T(8,128)S(1)}, u32[]{:S(2)}) copy-start(f32[8,2048]{1,0:T(8,128)S(1)} %collective-permute-done.7.refs_11_) | copy-start | bytes 196612
  39.2 0.6 copy-start.11
  56.1 4.5 %collective-permute-start.10 = (f32[16,640]{1,0:T(8,128)}, f32[16,640]{1,0:T(8,128)S(1)}, u32[]{:S(2)}, u32[]{:S(2)}) collective-permute-start(f32[16,640]{1,0:T(8,128)} %get-tuple-element.15.refs_5_), channel_id=1, source_target_pairs={{0,2},{1,3},{2,0},{3,1},{4,6},{5,7},{6,4},{7,5},{8,10},{9,11},{10,... | collective-permute-start | bytes 122888 | tf_op jit(solution)/shard_map/ppermute | solution.py:285
  56.8 4.1 %collective-permute-start.11 = (f32[16,640]{1,0:T(8,128)}, f32[16,640]{1,0:T(8,128)S(1)}, u32[]{:S(2)}, u32[]{:S(2)}) collective-permute-start(f32[16,640]{1,0:T(8,128)} %get-tuple-element.15.refs_5_), channel_id=1, source_target_pairs={{0,3},{1,2},{2,1},{3,0},{4,7},{5,6},{6,5},{7,4},{8,11},{9,10},{10,... | collective-permute-start | bytes 122888 | tf_op jit(solution)/shard_map/ppermute | solution.py:285
  56.8 4.1 %collective-permute-start.9 = (f32[16,640]{1,0:T(8,128)}, f32[16,640]{1,0:T(8,128)S(1)}, u32[]{:S(2)}, u32[]{:S(2)}) collective-permute-start(f32[16,640]{1,0:T(8,128)} %get-tuple-element.15.refs_5_), channel_id=1, source_target_pairs={{0,1},{1,0},{2,3},{3,2},{4,5},{5,4},{6,7},{7,6},{8,9},{9,8},{10,11... | collective-permute-start | bytes 122888 | tf_op jit(solution)/shard_map/ppermute | solution.py:285
  60.6 0.6 copy-start.12
  60.9 0.6 copy-start.13
  60.9 0.6 copy-start.14
  63.1 0.7 copy-start.18
  63.8 4.4 %collective-permute-start.12 = (f32[1,128]{1,0:T(1,128)S(1)}, f32[1,128]{1,0:T(1,128)S(1)}, u32[]{:S(2)}, u32[]{:S(2)}) collective-permute-start(f32[1,128]{1,0:T(1,128)S(1)} %copy-done.18), channel_id=1, source_target_pairs={{0,4},{4,0},{8,12},{12,8},{1,5},{5,1},{9,13},{13,9},{2,6},{6,2},{1... | collective-permute-start | bytes 1544 | tf_op jit(solution)/shard_map/ppermute | solution.py:285
  64.1 4.4 %collective-permute-start.13 = (f32[1,128]{1,0:T(1,128)S(1)}, f32[1,128]{1,0:T(1,128)S(1)}, u32[]{:S(2)}, u32[]{:S(2)}) collective-permute-start(f32[1,128]{1,0:T(1,128)S(1)} %copy-done.18), channel_id=1, source_target_pairs={{0,8},{4,12},{8,0},{12,4},{1,9},{5,13},{9,1},{13,5},{2,10},{6,14},... | collective-permute-start | bytes 1544 | tf_op jit(solution)/shard_map/ppermute | solution.py:285
  65.9 5.3 %collective-permute-start.14 = (f32[1,128]{1,0:T(1,128)S(1)}, f32[1,128]{1,0:T(1,128)S(1)}, u32[]{:S(2)}, u32[]{:S(2)}) collective-permute-start(f32[1,128]{1,0:T(1,128)S(1)} %copy-done.18), channel_id=1, source_target_pairs={{0,12},{4,8},{8,4},{12,0},{1,13},{5,9},{9,5},{13,1},{2,14},{6,10},... | collective-permute-start | bytes 1544 | tf_op jit(solution)/shard_map/ppermute | solution.py:285
  71.2 0.7 copy-start.17
  71.2 0.7 copy-start.15

commit v2 on v1

v2 whole, which is shorter than its diff:
```python
import jax
import jax.numpy as jnp
from jax import lax
from jax.experimental import pallas as pl
from jax.experimental.pallas import tpu as pltpu
from jax.sharding import PartitionSpec as P

STATIONS = 128
CELLS = 512
SPAN = 2048
DEPTH = 32
STRENGTH = 0.1
SHRINK = 2.0**-6
GROWN = 2.0**-15 * STRENGTH
TURN = 1024
F8_TOP = 256.0
F32 = jnp.float32
BF16 = jnp.bfloat16
F8 = jnp.float8_e4m3fn
NN = (((1,), (0,)), ((), ()))
NT = (((1,), (1,)), ((), ()))


def rounded(value):
    return value.astype(BF16).astype(F32)


def three_parts(value):
    high = rounded(value)
    middle = rounded(value - high)
    return high, middle, value - high - middle


def multiply(left, right, numbers=NN):
    return lax.dot_general(left, right, numbers, preferred_element_type=F32)


def falloff_parts(squared, low_type):
    root = lax.rsqrt(squared)
    second = root * root
    falloff = second * second * root
    high = falloff.astype(BF16)
    return high, (falloff - high.astype(F32)).astype(low_type)


def narrow_parts(value):
    top = jnp.maximum(jnp.max(jnp.abs(value), axis=1, keepdims=True), 1e-30)
    scaled = value * (F8_TOP / top)
    high = scaled.astype(F8).astype(F32)
    return high, (scaled - high) * 16.0, top * (1.0 / F8_TOP)


def square_sum(place):
    return place[0:1] * place[0:1] + place[1:2] * place[1:2] + place[2:3] * place[2:3]


def fill_station_rows(rows, place):
    high, middle, low = three_parts(place)
    norms = three_parts(square_sum(place))
    ones = jnp.ones_like(norms[0])
    for at, part in enumerate((high, high, middle, middle, high, low)):
        rows[3 * at : 3 * at + 3, :] = part
    for at, part in enumerate((*norms, ones, ones, ones)):
        rows[18 + at : 19 + at, :] = part
    rows[24:DEPTH, :] = jnp.zeros((DEPTH - 24, place.shape[1]), F32)


def fill_cell_rows(rows, place):
    high, middle, low = three_parts((-2.0 * SHRINK) * place)
    norms = three_parts(SHRINK * square_sum(place))
    ones = jnp.full_like(norms[0], SHRINK)
    for at, part in enumerate((high, middle, high, middle, low, high)):
        rows[3 * at : 3 * at + 3, :] = part
    for at, part in enumerate((ones, ones, ones, *norms)):
        rows[18 + at : 19 + at, :] = part
    rows[24:DEPTH, :] = jnp.zeros((DEPTH - 24, place.shape[1]), F32)


def join(target, pieces, rows):
    at = 0
    for piece in pieces:
        width = piece.shape[1]
        target[0:rows, at : at + width] = piece[0:rows, :]
        at += width


def transpose_into(target, rows):
    for at in range(0, rows.shape[1], 512):
        target[at : at + 512, :] = rows[:, at : at + 512].T.astype(BF16)


def pack(target, base, row):
    for at in range(row.shape[1] // 128):
        target[base + at : base + at + 1, :] = row[:, at * 128 : (at + 1) * 128]


def unpack(target, row, lane, source):
    for at in range(source.shape[0]):
        start = lane + at * 128
        target[row : row + 1, start : start + 128] = source[at : at + 1, :]


def listed_tiles(station_list, cell_list, filled, ranks, own_blocks):
    per_cell, per_stn = own_blocks
    station_id = (
        lax.bitwise_xor(station_list // per_cell, ranks[0]) * per_cell + station_list % per_cell
    )
    cell_id = lax.bitwise_xor(cell_list // per_stn, ranks[1]) * per_stn + cell_list % per_stn
    live = lax.broadcasted_iota(jnp.int32, cell_list.shape, 1) < filled
    return jnp.concatenate([station_id, jnp.where(live, cell_id, -1)], axis=0)


def listed_counts(tiles, station_total, cell_total):
    slots = tiles.shape[1]
    station_hot = lax.broadcasted_iota(jnp.int32, (station_total, slots), 0) == tiles[0:1, :]
    cell_hot = lax.broadcasted_iota(jnp.int32, (cell_total, slots), 0) == tiles[1:2, :]
    count = multiply(cell_hot.astype(F32).astype(BF16), station_hot.astype(F32).astype(BF16), NT)
    wide = (station_total, station_total * STATIONS)
    spread = lax.broadcasted_iota(jnp.int32, wide, 0) == (
        lax.broadcasted_iota(jnp.int32, wide, 1) // STATIONS
    )
    return multiply(count.astype(BF16), spread.astype(F32).astype(BF16))


def forward_kernel(station_pieces, cell_pieces, keep, tiles, residual, *refs):
    station_refs = refs[:station_pieces]
    refs = refs[station_pieces:]
    cell_refs = refs[:cell_pieces]
    image, count, station, cell, *outs = refs[cell_pieces:]
    kept = outs[:2] if keep else None
    station_rows, cell_rows, left, right, source, narrow, moments = outs[2 if keep else 0 :]
    width, extent = station.shape[1], cell.shape[1]
    join(cell, cell_refs, 4)
    join(station, station_refs, 3 if keep else 9)
    count[...] = listed_counts(tiles, width // STATIONS, extent // CELLS)
    fill_station_rows(station_rows, station[0:3, :])
    right[...] = station_rows[...].astype(BF16)
    fill_cell_rows(cell_rows, cell[0:3, :])
    transpose_into(left, cell_rows)
    value = cell[3:4, :]
    x, y, z = cell[0:1, :], cell[1:2, :], cell[2:3, :]
    vx, vy, vz = value * x, value * y, value * z
    products = (value, vx, vy, vz, vx * x, vx * y, vx * z, vy * y, vy * z, vz * z)
    for at, row in enumerate(products):
        cell_rows[at : at + 1, :] = row
    cell_rows[10:16, :] = jnp.zeros((6, extent), F32)
    parts = three_parts(cell_rows[0:16, :])
    source[...] = jnp.concatenate([part.astype(BF16) for part in parts], axis=0)
    high, low, unit = narrow_parts(cell_rows[0:16, :])
    narrow[...] = jnp.concatenate([high, low], axis=0).astype(F8)
    moments[...] = jnp.zeros_like(moments)
    spans = width // SPAN

    def turn(which, carry):
        group = which // spans
        lanes = pl.ds(pl.multiple_of(which % spans * SPAN, SPAN), SPAN)
        cells = pl.ds(pl.multiple_of(group * TURN, TURN), TURN)
        squared = multiply(left[cells, :], right[:, lanes])
        high, low = falloff_parts(squared, F8)
        if keep:
            kept[0][cells, :] = high
            kept[1][cells, :] = low
        sums = moments[:, lanes]
        for at in range(TURN // CELLS):
            block = group * (TURN // CELLS) + at
            here = pl.ds(pl.multiple_of(block * CELLS, CELLS), CELLS)
            rows = slice(at * CELLS, (at + 1) * CELLS)
            wide = multiply(source[:, here], high[rows])
            fine = multiply(narrow[:, here], low[rows])
            total = wide[0:16] + wide[16:32] + wide[32:48]
            total = total + (fine[0:16] + fine[16:32] * (1.0 / 16.0)) * unit
            sums = sums + total * count[pl.ds(block, 1), lanes]
        moments[:, lanes] = sums
        return carry

    lax.fori_loop(0, spans * (extent // TURN), turn, 0)
    sx, sy, sz = station[0:1, :], station[1:2, :], station[2:3, :]
    total, mx, my, mz, mxx, mxy, mxz, myy, myz, mzz = (moments[k : k + 1, :] for k in range(10))
    xx = sx * (sx * total - 2.0 * mx) + mxx
    yy = sy * (sy * total - 2.0 * my) + myy
    zz = sz * (sz * total - 2.0 * mz) + mzz
    xy = sx * (sy * total - my) - sy * mx + mxy
    xz = sx * (sz * total - mz) - sz * mx + mxz
    yz = sy * (sz * total - mz) - sz * my + myz
    rows = (2.0 * xx - yy - zz, 3.0 * xy, 3.0 * xz, 2.0 * yy - xx - zz, 3.0 * yz)
    for k, row in enumerate(rows):
        pack(image, k * (width // 128), GROWN * row)
    if keep:
        image[5 * (width // 128) :, :] = residual[...]


def tree(values):
    values = list(values)
    while len(values) > 1:
        values = [values[k] + values[k + 1] for k in range(0, len(values), 2)]
    return values[0]


def gather_images(image, residual, image_refs, own):
    width = image.shape[1]
    rows, each = width // 128, own // 128
    norms = []
    for owner in range(width // own):
        blocks = []
        for k in range(5):
            blocks.append(
                tree(
                    ref[k * rows + (owner ^ other) * each : k * rows + ((owner ^ other) + 1) * each, :]
                    for other, ref in enumerate(image_refs)
                )
            )
        blocks.append(-(blocks[0] + blocks[3]))
        squares = 0.0
        for k, block in enumerate(blocks):
            unpack(image, k, owner * own, block)
            squares = squares + block * block
        norms.append(jnp.sum(squares))
    if residual is not None:
        for other, ref in enumerate(image_refs):
            for k in range(6):
                first = 5 * rows + k * each
                unpack(residual, k, other * own, ref[first : first + each, :])
    return tree(norms)


def fill_vectors(vectors, station, residual, image):
    sx, sy, sz = station[0:1, :], station[1:2, :], station[2:3, :]
    for first, source, offset in ((0, *residual), (10, *image)):
        r = [GROWN * source[offset + k : offset + k + 1, :] for k in range(6)]
        axx, ayy, azz = 2.0 * r[0] - r[3] - r[5], 2.0 * r[3] - r[0] - r[5], 2.0 * r[5] - r[0] - r[3]
        axy, axz, ayz = 3.0 * r[1], 3.0 * r[2], 3.0 * r[4]
        whole = (
            sx * (axx * sx + axy * sy + axz * sz) + sy * (ayy * sy + ayz * sz) + azz * sz * sz
        )
        bx = 2.0 * axx * sx + axy * sy + axz * sz
        by = 2.0 * ayy * sy + axy * sx + ayz * sz
        bz = 2.0 * azz * sz + axz * sx + ayz * sy
        for k, row in enumerate((whole, bx, by, bz, axx, axy, axz, ayy, ayz, azz)):
            vectors[first + k : first + k + 1, :] = row
    vectors[20:24, :] = jnp.zeros((4, vectors.shape[1]), F32)


def start_partial(partial, norm):
    side = partial.shape[1] - CELLS
    partial[:, CELLS:] = jnp.full((partial.shape[0], side), norm, F32)


def write_partial(partial, sums, place, block, blocks):
    x, y, z = place[0:1], place[1:2], place[2:3]
    for vector in range(2):
        whole, bx, by, bz, axx, axy, axz, ayy, ayz, azz = (
            sums[10 * vector + k : 10 * vector + k + 1] for k in range(10)
        )
        value = (
            whole
            + x * (x * axx + y * axy + z * axz - bx)
            + y * (y * ayy + z * ayz - by)
            + z * (z * azz - bz)
        )
        partial[pl.ds(vector * blocks + block, 1), 0:CELLS] = value


def kept_adjoint_kernel(count, station, cell, high, low, *refs):
    *image_refs, partial, own_image, image, residual, vectors = refs
    extent, own = cell.shape[1], own_image.shape[1]
    norm = gather_images(image, residual, image_refs, own)
    own_image[...] = image[:, 0:own]
    fill_vectors(vectors, station, (residual, 0), (image, 0))
    start_partial(partial, norm)
    blocks = extent // CELLS

    def turn(group, carry):
        for at in range(TURN // CELLS):
            block = group * (TURN // CELLS) + at
            cells = pl.ds(pl.multiple_of(block * CELLS, CELLS), CELLS)
            counted = vectors[...] * count[pl.ds(block, 1), :]
            weights = jnp.concatenate(three_parts(counted), axis=0).astype(BF16)
            above, below, unit = narrow_parts(counted)
            narrow = jnp.concatenate([above, below], axis=0).astype(F8)
            wide = multiply(high[cells, :], weights, NT).T
            fine = multiply(low[cells, :], narrow, NT).T
            sums = wide[0:24] + wide[24:48] + wide[48:72]
            sums = sums + (fine[0:24] + fine[24:48] * (1.0 / 16.0)) * unit
            write_partial(partial, sums, cell[0:3, cells], block, blocks)
        return carry

    lax.fori_loop(0, extent // TURN, turn, 0)


def adjoint_kernel(count, station, cell, image_ref, *refs):
    partial, own_image, image, station_rows, cell_rows, left, right, vectors = refs
    width, extent = station.shape[1], cell.shape[1]
    norm = gather_images(image, None, [image_ref], CELLS)
    own_image[...] = image[...]
    fill_cell_rows(cell_rows, cell[0:3, :])
    right[...] = cell_rows[...].astype(BF16)
    fill_station_rows(station_rows, station[0:3, :])
    transpose_into(left, station_rows)
    fill_vectors(vectors, station, (station, 3), (image, 0))
    start_partial(partial, norm)
    blocks = extent // CELLS

    def turn(block, carry):
        cells = pl.ds(pl.multiple_of(block * CELLS, CELLS), CELLS)

        def span_turn(which, sums):
            lanes = pl.ds(pl.multiple_of(which * SPAN, SPAN), SPAN)
            squared = multiply(left[lanes, :], right[:, cells])
            high, low = falloff_parts(squared, BF16)
            parts = three_parts(vectors[:, lanes] * count[pl.ds(block, 1), lanes])
            weights = jnp.concatenate(parts, axis=0).astype(BF16)
            total = multiply(weights, high) + multiply(weights, low)
            return sums + (total[0:24] + total[24:48] + total[48:72])

        sums = lax.fori_loop(0, width // SPAN, span_turn, jnp.zeros((24, CELLS), F32))
        write_partial(partial, sums, cell[0:3, cells], block, blocks)
        return carry

    lax.fori_loop(0, blocks, turn, 0)


def update_kernel(pieces, gradient_norm, densities, direction, residual, image, *refs):
    partial_refs = refs[:pieces]
    densities_next, residual_next, gradient, norm = refs[pieces:]
    blocks = partial_refs[0].shape[0] // 2
    each = blocks // pieces
    step = gradient_norm[0] / tree(ref[0:1, CELLS : CELLS + 1] for ref in partial_refs)
    sums = []
    for k in range(pieces):
        both = [
            tree(
                partial_refs[other][
                    vector * blocks + (k ^ other) * each : vector * blocks + ((k ^ other) + 1) * each,
                    0:CELLS,
                ]
                for other in range(pieces)
            )
            for vector in range(2)
        ]
        block = both[0] - step * both[1]
        sums.append(jnp.sum(block * block, axis=(0, 1), keepdims=True))
        if k == 0:
            for b in range(each):
                pack(gradient, b * (CELLS // 128), block[b : b + 1, :])
    norm[...] = jnp.broadcast_to(tree(sums), norm.shape)
    densities_next[...] = densities[...] + step * direction[...]
    residual_next[...] = residual[...] - step * image[0:6, :]


def finish_kernel(gradient_norm, gradient, direction, *refs):
    *norms, direction_next, norm_next = refs
    total = tree(ref[...] for ref in norms)
    direction_next[...] = gradient[...] + total / gradient_norm[0] * direction[...]
    norm_next[0] = total[0, 0]


def sent(value, axis, size, other):
    return lax.ppermute(value, axis, [(rank, rank ^ other) for rank in range(size)])


def doubled(value, axis, size):
    step = 1
    while step < size // 2:
        value = jnp.concatenate([value, sent(value, axis, size, step)], axis=1)
        step *= 2
    return [value, sent(value, axis, size, step)]


def exchanged(value, axis, size):
    return [value] + [sent(value, axis, size, other) for other in range(1, size)]


def on_device(
    densities,
    residual,
    direction,
    gradient_norm,
    station_place,
    cell_place,
    station_blocks,
    cell_blocks,
    pair_count,
):
    cell_size, stn_size = lax.axis_size("cell"), lax.axis_size("stn")
    direct = cell_size <= 4
    own, cell_own = station_place.shape[1], cell_place.shape[1]
    width, extent = cell_size * own, stn_size * cell_own
    rows, blocks = width // 128, extent // CELLS
    ranks = (lax.axis_index("cell") if direct else 0, lax.axis_index("stn"))
    tiles = listed_tiles(
        station_blocks.reshape(1, -1),
        cell_blocks.reshape(1, -1),
        pair_count.reshape(()),
        ranks,
        (own // STATIONS, cell_own // CELLS),
    )
    if direct:
        station_parts = doubled(station_place, "cell", cell_size)
    else:
        both = jnp.concatenate([station_place, residual], axis=0)
        station_parts = [lax.all_gather(both, "cell", axis=1, tiled=True)]
    cell_mine = jnp.concatenate([cell_place, direction[None]], axis=0)
    cell_parts = doubled(cell_mine, "stn", stn_size)
    in_vmem, in_smem = pl.BlockSpec(memory_space=pltpu.VMEM), pl.BlockSpec(memory_space=pltpu.SMEM)
    params = pltpu.CompilerParams(vmem_limit_bytes=(16 if direct else 56) * 2**20)
    small = pltpu.CompilerParams(vmem_limit_bytes=2**20)
    counts = (len(station_parts), len(cell_parts))
    pieces = sum(counts)

    def forward(*refs):
        forward_kernel(*counts, direct, *refs)

    out_shape = [
        jax.ShapeDtypeStruct((5 * rows + (6 * own // 128 if direct else 0), 128), F32),
        jax.ShapeDtypeStruct((blocks, width), F32),
        jax.ShapeDtypeStruct((16, width), F32),
        jax.ShapeDtypeStruct((8, extent), F32),
    ]
    if direct:
        out_shape += [
            jax.ShapeDtypeStruct((extent, width), BF16),
            jax.ShapeDtypeStruct((extent, width), F8),
        ]
    image_part, *kept = pl.pallas_call(
        forward,
        out_shape=out_shape,
        in_specs=[in_vmem] * (2 + pieces),
        out_specs=[in_vmem] * len(out_shape),
        scratch_shapes=[
            pltpu.VMEM((DEPTH, width), F32),
            pltpu.VMEM((DEPTH, extent), F32),
            pltpu.VMEM((extent, DEPTH), BF16),
            pltpu.VMEM((DEPTH, width), BF16),
            pltpu.VMEM((48, extent), BF16),
            pltpu.VMEM((32, extent), F8),
            pltpu.VMEM((16, width), F32),
        ],
        compiler_params=params,
        name="forward",
    )(tiles, residual.reshape(-1, 128), *station_parts, *cell_parts)
    if direct:
        image_parts = exchanged(image_part, "cell", cell_size)
    else:
        image_parts = [lax.psum(image_part, "cell")]

    def adjoint(*refs):
        (kept_adjoint_kernel if direct else adjoint_kernel)(*refs)

    if direct:
        scratch = [pltpu.VMEM((8, width), F32)]
    else:
        scratch = [
            pltpu.VMEM((DEPTH, width), F32),
            pltpu.VMEM((DEPTH, extent), F32),
            pltpu.VMEM((width, DEPTH), BF16),
            pltpu.VMEM((DEPTH, extent), BF16),
        ]
    partial, image_own = pl.pallas_call(
        adjoint,
        out_shape=(
            jax.ShapeDtypeStruct((2 * blocks, CELLS + 128), F32),
            jax.ShapeDtypeStruct((8, own if direct else width), F32),
        ),
        in_specs=[in_vmem] * (len(kept) + len(image_parts)),
        out_specs=(in_vmem, in_vmem),
        scratch_shapes=[
            pltpu.VMEM((8, width), F32),
            *scratch,
            pltpu.VMEM((24, width), F32),
        ],
        compiler_params=params,
        name="adjoint",
    )(*kept, *image_parts)
    if not direct:
        image_own = lax.dynamic_slice_in_dim(image_own, lax.axis_index("cell") * own, own, axis=1)
    partial_parts = exchanged(partial, "stn", stn_size)

    def update(*refs):
        update_kernel(stn_size, *refs)

    flat = direction.reshape(-1, 128)
    densities_next, residual_next, gradient, norm_part = pl.pallas_call(
        update,
        out_shape=(
            jax.ShapeDtypeStruct(flat.shape, F32),
            jax.ShapeDtypeStruct(residual.shape, F32),
            jax.ShapeDtypeStruct(flat.shape, F32),
            jax.ShapeDtypeStruct((1, 128), F32),
        ),
        in_specs=[in_smem] + [in_vmem] * (4 + stn_size),
        out_specs=(in_vmem,) * 4,
        compiler_params=small,
        name="update",
    )(gradient_norm, densities.reshape(flat.shape), flat, residual, image_own, *partial_parts)
    if direct:
        norm_parts = exchanged(norm_part, "cell", cell_size)
    else:
        norm_parts = [lax.psum(norm_part, "cell")]
    direction_next, norm_next = pl.pallas_call(
        finish_kernel,
        out_shape=(
            jax.ShapeDtypeStruct(flat.shape, F32),
            jax.ShapeDtypeStruct((1,), F32),
        ),
        in_specs=[in_smem] + [in_vmem] * (2 + len(norm_parts)),
        out_specs=(in_vmem, in_smem),
        compiler_params=small,
        name="finish",
    )(gradient_norm, gradient, flat, *norm_parts)
    return (densities_next.reshape(-1), residual_next, direction_next.reshape(-1), norm_next)


def solution(mesh):
    in_specs = (
        P(("survey", "cell", "stn")),
        P(None, ("survey", "cell", "stn")),
        P(("survey", "cell", "stn")),
        P("survey"),
        P(None, ("survey", "cell", "stn")),
        P(None, ("survey", "cell", "stn")),
        P(("survey", "cell"), "stn", None),
        P(("survey", "cell"), "stn", None),
        P(("survey", "cell"), "stn"),
    )
    out_specs = (
        P(("survey", "cell", "stn")),
        P(None, ("survey", "cell", "stn")),
        P(("survey", "cell", "stn")),
        P("survey"),
    )
    return jax.shard_map(
        on_device, mesh=mesh, in_specs=in_specs, out_specs=out_specs, check_vma=False
    )
```

time: 73 us -> 58.2 us (0.80)
  Pallas kernels: 33.1 us -> 22 us
  waiting for transfers between devices: 13.6 us -> 11.7 us
  local copies, waits for them, and re-layouts: 2.72 us -> 1.45 us
    pallas_call x1, Pallas kernels: 16.3 us -> 8.13 us  [on_device(): pl.pallas_call(adjoint, out_shape=(jax.ShapeDtypeStruct((2 * blocks, CELL...]
    pallas_call x1 -> x2, Pallas kernels: 15.2 us -> 13.1 us  [the longest x1 12.5 us: on_device(): pl.pallas_call(forward, out_shape=out_shape, in_specs=[in_vmem] * (2 + pi...]
    unnamed x38 -> x7, local copies, waits for them, and re-layouts: 2.72 us -> 0.72 us
    ppermute x15 -> x13, waiting for transfers between devices: 13.6 us -> 11.7 us  [sent(): lax.ppermute(value, axis, [(rank, rank ^ other) for rank in range(size)])]
    pallas_call x1, Pallas kernels: 1.63 us -> 0.7 us  [on_device(): pl.pallas_call(update, out_shape=(jax.ShapeDtypeStruct(flat.shape, F32),...]
    concatenate x2 -> x3, other arithmetic: 0.77 us -> 1.52 us  [the longest x1 0.76 us: on_device(): cell_mine = jnp.concatenate([cell_place, direction[None]], axis=0)]
    ppermute x15 -> x13, starting transfers between devices: 18.5 us -> 18.3 us  [sent(): lax.ppermute(value, axis, [(rank, rank ^ other) for rank in range(size)])]
  transfers between devices with their start and end apart: 15 -> 13, of which waited for: 10 -> 7; matrix products, arithmetic and copies ran while one was open for 1% -> 5% of each run, Pallas kernels for 0% -> 0%
where the time goes in v2:
time: 58.2 us; the launch traced here: 57.6 us
  Pallas kernels  22 us (38%)
  starting transfers between devices  18.3 us (31%)
  waiting for transfers between devices  11.7 us (20%)
  other arithmetic  2.24 us (4%)
  between operations  2.01 us (3%)
  local copies, waits for them, and re-layouts  1.45 us (2%)
    ppermute x13, starting transfers between devices, sent(): lax.ppermute(value, axis, [(rank, rank ^ other) for rank in range(size)])  18.3 us
    pallas_call x1, Pallas kernels, on_device(): pl.pallas_call(forward, out_shape=out_shape, in_specs=[in_vmem] * (2 + pi...  12.5 us
    ppermute x13, waiting for transfers between devices, sent(): lax.ppermute(value, axis, [(rank, rank ^ other) for rank in range(size)])  11.7 us
    pallas_call x1, Pallas kernels, on_device(): pl.pallas_call(adjoint, out_shape=(jax.ShapeDtypeStruct((2 * blocks, CELL...  8.13 us
  transfers between devices with their start and end apart: 13, of which 7 were waited for; matrix products, arithmetic and copies ran while one was open for 5% of the time, Pallas kernels for 0%

profile of v2, /device:TPU:0, one launch (start us, length us, event | category | flops | bytes accessed | tf_op | source)
XLA Modules:
  0.0 57.6 jit_solution(6664440103312693752)
XLA Ops:
  0.6 0.0 copy-start.1
  0.6 0.0 copy-start
  0.7 0.0 copy-start.2
  0.7 0.8 %pad_maximum_fusion.1 = f32[4,1024]{1,0:T(4,128)S(1)} fusion(f32[1,1024]{1,0:T(1,128)} %bitcast.33, f32[3,1024]{1,0:T(4,128)} %param.14), kind=kLoop, calls=%fused_computation.1 | loop fusion | flops 4096 | bytes 32768 | tf_op jit(solution)/shard_map/concatenate | solution.py:402
  1.4 0.5 collective-permute-start.2
  1.9 2.6 %collective-permute-start = (f32[3,512]{1,0:T(4,128)}, f32[3,512]{1,0:T(4,128)S(1)}, u32[]{:S(2)}, u32[]{:S(2)}) collective-permute-start(f32[3,512]{1,0:T(4,128)} %param.13), channel_id=1, source_target_pairs={{0,4},{4,0},{8,12},{12,8},{1,5},{5,1},{9,13},{13,9},{2,6},{6,2},{1... | collective-permute-start | bytes 18440 | tf_op jit(solution)/shard_map/ppermute | solution.py:358
  5.2 0.7 %compare_select_fusion = (s32[1,256]{1,0:T(1,128)S(1)}, s32[1,256]{1,0:T(1,128)S(1)}) fusion(s32[1,1,256]{2,1,0:T(1,128)} %param.16, s32[]{:T(128)S(6)} %axis_index.25, s32[]{:T(128)} %bitcast.32, s32[]{:T(128)S(6)} %axis_index.23, s32[1,1,256]{2,1,0:T(1,128)} %param.15), kind=kLoop, calls=%fused_computation.6 | loop fusion | flops 11776 | bytes 4108 | tf_op jit(solution)/shard_map/jit(_where)/select_n | solution.py:110
  6.0 0.7 %constant_dynamic-update-slice_fusion.1 = f32[3,1024]{1,0:T(4,128)S(1)} fusion(f32[3,512]{1,0:T(4,128)} %param.13), kind=kLoop, calls=%fused_computation.3 | loop fusion | bytes 14336
  6.7 0.0 collective-permute-done
  6.7 2.8 %collective-permute-start.1 = (f32[3,1024]{1,0:T(4,128)S(1)}, f32[3,1024]{1,0:T(4,128)S(1)}, u32[]{:S(2)}, u32[]{:S(2)}) collective-permute-start(f32[3,1024]{1,0:T(4,128)S(1)} %constant_dynamic-update-slice_fusion.refs_2_), channel_id=1, source_target_pairs={{0,8},{4,12},{8,0},{12,4},{1,9},{5,13},{9,1},{13,5},{2,10},{6,14},... | collective-permute-start | bytes 36872 | tf_op jit(solution)/shard_map/ppermute | solution.py:358
  9.5 0.0 collective-permute-done.2
  9.5 0.7 %pad_maximum_fusion.refs_4_ = f32[4,2048]{1,0:T(4,128)S(1)} fusion(f32[4,1024]{1,0:T(4,128)S(1)} %collective-permute-done.2, f32[1,1024]{1,0:T(1,128)} %bitcast.34, f32[3,1024]{1,0:T(4,128)} %param.14), kind=kLoop, calls=%fused_computation | loop fusion | flops 16384 | bytes 65536 | tf_op jit(solution)/shard_map/concatenate | solution.py:364
  10.2 1.6 %collective-permute-start.3 = (f32[4,2048]{1,0:T(4,128)S(1)}, f32[4,2048]{1,0:T(4,128)S(1)}, u32[]{:S(2)}, u32[]{:S(2)}) collective-permute-start(f32[4,2048]{1,0:T(4,128)S(1)} %pad_maximum_fusion.refs_4_), channel_id=1, source_target_pairs={{0,2},{1,3},{2,0},{3,1},{4,6},{5,7},{6,4},{7,5},{8,10},{9,11},{10,... | collective-permute-start | bytes 98312 | tf_op jit(solution)/shard_map/ppermute | solution.py:358
  11.8 0.7 %reshape.341.refs_1_ = f32[24,128]{1,0:T(8,128)S(1)} reshape(f32[6,512]{1,0:T(8,128)} %refs_3_.1) | data formatting | bytes 24576 | tf_op jit(solution)/shard_map/reshape | solution.py:440
  12.5 0.0 collective-permute-done.1.refs_3_
  12.5 1.7 %collective-permute-done.3.refs_5_ = f32[4,2048]{1,0:T(4,128)S(1)} collective-permute-done((f32[4,2048]{1,0:T(4,128)S(1)}, f32[4,2048]{1,0:T(4,128)S(1)}, u32[]{:S(2)}, u32[]{:S(2)}) %collective-permute-start.3) | collective-permute-done | bytes 32800 | tf_op jit(solution)/shard_map/ppermute | solution.py:358
  14.2 12.5 %forward.1 = (f32[104,128]{1,0:T(8,128)S(1)}, f32[8,2048]{1,0:T(8,128)S(1)}, f32[16,2048]{1,0:T(8,128)S(1)}, f32[8,4096]{1,0:T(8,128)S(1)}, bf16[4096,2048]{1,0:...) custom-call(s32[2,256]{1,0:T(2,128)S(1)} %pad_add_fusion.refs_0_, f32[24,128]{1,0:T(8,128)S(1)} %reshape.341.refs_1_, ...), custom_call_target="tpu_custom_call" | custom-call | tf_op jit(solution)/shard_map/forward/pallas_call | solution.py:424
  26.7 1.6 %collective-permute-start.4 = (f32[104,128]{1,0:T(8,128)S(1)}, f32[104,128]{1,0:T(8,128)S(1)}, u32[]{:S(2)}, u32[]{:S(2)}) collective-permute-start(f32[104,128]{1,0:T(8,128)S(1)} %get-tuple-element.23.refs_5_), channel_id=1, source_target_pairs={{0,4},{4,0},{8,12},{12,8},{1,5},{5,1},{9,13},{13,9},{2,6},{6,2},{1... | collective-permute-start | bytes 159752 | tf_op jit(solution)/shard_map/ppermute | solution.py:358
  28.4 0.3 collective-permute-start.5
  28.7 2.5 %collective-permute-start.6 = (f32[104,128]{1,0:T(8,128)S(1)}, f32[104,128]{1,0:T(8,128)S(1)}, u32[]{:S(2)}, u32[]{:S(2)}) collective-permute-start(f32[104,128]{1,0:T(8,128)S(1)} %get-tuple-element.23.refs_5_), channel_id=1, source_target_pairs={{0,12},{4,8},{8,4},{12,0},{1,13},{5,9},{9,5},{13,1},{2,14},{6,10},... | collective-permute-start | bytes 159752 | tf_op jit(solution)/shard_map/ppermute | solution.py:358
  31.2 0.0 collective-permute-done.4.refs_6_
  31.2 2.7 %collective-permute-done.5.refs_7_ = f32[104,128]{1,0:T(8,128)S(1)} collective-permute-done((f32[104,128]{1,0:T(8,128)S(1)}, f32[104,128]{1,0:T(8,128)S(1)}, u32[]{:S(2)}, u32[]{:S(2)}) %collective-permute-start.5) | collective-permute-done | bytes 53280 | tf_op jit(solution)/shard_map/ppermute | solution.py:358
  33.9 0.9 %collective-permute-done.6.refs_8_ = f32[104,128]{1,0:T(8,128)S(1)} collective-permute-done((f32[104,128]{1,0:T(8,128)S(1)}, f32[104,128]{1,0:T(8,128)S(1)}, u32[]{:S(2)}, u32[]{:S(2)}) %collective-permute-start.6) | collective-permute-done | bytes 53280 | tf_op jit(solution)/shard_map/ppermute | solution.py:358
  34.8 8.1 %adjoint.1 = (f32[16,640]{1,0:T(8,128)S(1)}, f32[8,512]{1,0:T(8,128)S(1)}) custom-call(f32[8,2048]{1,0:T(8,128)S(1)} %get-tuple-element.18.refs_0_, f32[16,2048]{1,0:T(8,128)S(1)} %get-tuple-element.19.refs_1_, f32[8,4096]{1,0:T(8,128)S(1)} %get-tuple-element.20.refs_2_, bf16[4096,2048]{1,0:T(8,128)(2,1)S(1)} %get-tuple-element.21.refs_3_, ...), custom_call_target="tpu_custom_call" | custom-call | tf_op jit(solution)/shard_map/adjoint/pallas_call | solution.py:458
  42.9 0.1 collective-permute-start.7
  43.0 1.6 %collective-permute-start.8 = (f32[16,640]{1,0:T(8,128)S(1)}, f32[16,640]{1,0:T(8,128)S(1)}, u32[]{:S(2)}, u32[]{:S(2)}) collective-permute-start(f32[16,640]{1,0:T(8,128)S(1)} %get-tuple-element.25.refs_5_), channel_id=1, source_target_pairs={{0,2},{1,3},{2,0},{3,1},{4,6},{5,7},{6,4},{7,5},{8,10},{9,11},{10,... | collective-permute-start | bytes 122888 | tf_op jit(solution)/shard_map/ppermute | solution.py:358
  44.5 0.3 collective-permute-start.9
  45.5 0.0 collective-permute-done.7.refs_6_
  45.5 1.5 %collective-permute-done.8.refs_7_ = f32[16,640]{1,0:T(8,128)S(1)} collective-permute-done((f32[16,640]{1,0:T(8,128)S(1)}, f32[16,640]{1,0:T(8,128)S(1)}, u32[]{:S(2)}, u32[]{:S(2)}) %collective-permute-start.8) | collective-permute-done | bytes 40992 | tf_op jit(solution)/shard_map/ppermute | solution.py:358
  47.0 1.0 %collective-permute-done.9.refs_8_ = f32[16,640]{1,0:T(8,128)S(1)} collective-permute-done((f32[16,640]{1,0:T(8,128)S(1)}, f32[16,640]{1,0:T(8,128)S(1)}, u32[]{:S(2)}, u32[]{:S(2)}) %collective-permute-start.9) | collective-permute-done | bytes 40992 | tf_op jit(solution)/shard_map/ppermute | solution.py:358
  48.0 0.0 copy-done.1
  48.0 0.0 copy-done
  48.0 0.0 copy-done.2
  48.0 0.7 %update.1 = (f32[8,128]{1,0:T(8,128)}, f32[6,512]{1,0:T(8,128)}, f32[8,128]{1,0:T(8,128)S(1)}, f32[1,128]{1,0:T(1,128)S(1)}) custom-call(f32[1]{0:T(128)S(6)} %copy.14.refs_0_.gradient_norm, f32[8,128]{1,0:T(8,128)S(1)} %bitcast.37, f32[8,128]{1,0:T(8,128)S(1)} %bitcast.35, f32[6,512]{1,0:T(8,128)S(1)} %copy-done, f32[8,512]{1,0:T(8,128)S(1)} %get-tuple-element.24.refs_4_, ...), custom_call_target="tpu_custom_call" | custom-call | tf_op jit(solution)/shard_map/update/pallas_call | solution.py:482
  48.8 0.8 %collective-permute-start.10 = (f32[1,128]{1,0:T(1,128)S(1)}, f32[1,128]{1,0:T(1,128)S(1)}, u32[]{:S(2)}, u32[]{:S(2)}) collective-permute-start(f32[1,128]{1,0:T(1,128)S(1)} %get-tuple-element.29.refs_0_), channel_id=1, source_target_pairs={{0,4},{4,0},{8,12},{12,8},{1,5},{5,1},{9,13},{13,9},{2,6},{6,2},{1... | collective-permute-start | bytes 1544 | tf_op jit(solution)/shard_map/ppermute | solution.py:358
  49.6 2.1 %collective-permute-start.11 = (f32[1,128]{1,0:T(1,128)S(1)}, f32[1,128]{1,0:T(1,128)S(1)}, u32[]{:S(2)}, u32[]{:S(2)}) collective-permute-start(f32[1,128]{1,0:T(1,128)S(1)} %get-tuple-element.29.refs_0_), channel_id=1, source_target_pairs={{0,8},{4,12},{8,0},{12,4},{1,9},{5,13},{9,1},{13,5},{2,10},{6,14},... | collective-permute-start | bytes 1544 | tf_op jit(solution)/shard_map/ppermute | solution.py:358
  51.7 1.5 %collective-permute-start.12 = (f32[1,128]{1,0:T(1,128)S(1)}, f32[1,128]{1,0:T(1,128)S(1)}, u32[]{:S(2)}, u32[]{:S(2)}) collective-permute-start(f32[1,128]{1,0:T(1,128)S(1)} %get-tuple-element.29.refs_0_), channel_id=1, source_target_pairs={{0,12},{4,8},{8,4},{12,0},{1,13},{5,9},{9,5},{13,1},{2,14},{6,10},... | collective-permute-start | bytes 1544 | tf_op jit(solution)/shard_map/ppermute | solution.py:358
  53.1 0.0 collective-permute-done.10.refs_1_
  53.1 0.9 %collective-permute-done.11.refs_2_ = f32[1,128]{1,0:T(1,128)S(1)} collective-permute-done((f32[1,128]{1,0:T(1,128)S(1)}, f32[1,128]{1,0:T(1,128)S(1)}, u32[]{:S(2)}, u32[]{:S(2)}) %collective-permute-start.11) | collective-permute-done | bytes 544 | tf_op jit(solution)/shard_map/ppermute | solution.py:358
  54.0 3.0 %collective-permute-done.12.refs_3_ = f32[1,128]{1,0:T(1,128)S(1)} collective-permute-done((f32[1,128]{1,0:T(1,128)S(1)}, f32[1,128]{1,0:T(1,128)S(1)}, u32[]{:S(2)}, u32[]{:S(2)}) %collective-permute-start.12) | collective-permute-done | bytes 544 | tf_op jit(solution)/shard_map/ppermute | solution.py:358
  57.0 0.6 %finish.1 = (f32[8,128]{1,0:T(8,128)}, f32[1]{0:T(128)}) custom-call(f32[1]{0:T(128)S(6)} %copy.14.refs_0_.gradient_norm, f32[8,128]{1,0:T(8,128)S(1)} %get-tuple-element.28.gradient, f32[8,128]{1,0:T(8,128)S(1)} %bitcast.36, f32[1,128]{1,0:T(1,128)S(1)} %get-tuple-element.29.refs_0_, f32[1,128]{1,0:T(1,128)S(1)} %collective-permute-done.10.refs_1_, ...), custom_call_target="tpu_custom_call" | custom-call | tf_op jit(solution)/shard_map/finish/pallas_call | solution.py:499
  (2 shorter events, 0.0 us)
Async XLA Ops:
  0.6 47.4 %copy-start.1 = (f32[1024]{0:T(1024)S(1)}, f32[1024]{0:T(1024)}, u32[]{:S(2)}) copy-start(f32[1024]{0:T(1024)} %param.11) | copy-start | bytes 12292
  0.6 47.4 %copy-start = (f32[6,512]{1,0:T(8,128)S(1)}, f32[6,512]{1,0:T(8,128)}, u32[]{:S(2)}) copy-start(f32[6,512]{1,0:T(8,128)} %refs_3_.1) | copy-start | bytes 36868
  0.7 47.4 %copy-start.2 = (f32[1024]{0:T(1024)S(1)}, f32[1024]{0:T(1024)}, u32[]{:S(2)}) copy-start(f32[1024]{0:T(1024)} %param.9) | copy-start | bytes 12292
  1.4 8.1 %collective-permute-start.2 = (f32[4,1024]{1,0:T(4,128)S(1)}, f32[4,1024]{1,0:T(4,128)S(1)}, u32[]{:S(2)}, u32[]{:S(2)}) collective-permute-start(f32[4,1024]{1,0:T(4,128)S(1)} %pad_maximum_fusion.1), channel_id=1, source_target_pairs={{0,1},{1,0},{2,3},{3,2},{4,5},{5,4},{6,7},{7,6},{8,9},{9,8},{10,11... | collective-permute-start | bytes 49160 | tf_op jit(solution)/shard_map/ppermute | solution.py:358
  1.9 4.7 %collective-permute-start = (f32[3,512]{1,0:T(4,128)}, f32[3,512]{1,0:T(4,128)S(1)}, u32[]{:S(2)}, u32[]{:S(2)}) collective-permute-start(f32[3,512]{1,0:T(4,128)} %param.13), channel_id=1, source_target_pairs={{0,4},{4,0},{8,12},{12,8},{1,5},{5,1},{9,13},{13,9},{2,6},{6,2},{1... | collective-permute-start | bytes 18440 | tf_op jit(solution)/shard_map/ppermute | solution.py:358
  6.7 5.8 %collective-permute-start.1 = (f32[3,1024]{1,0:T(4,128)S(1)}, f32[3,1024]{1,0:T(4,128)S(1)}, u32[]{:S(2)}, u32[]{:S(2)}) collective-permute-start(f32[3,1024]{1,0:T(4,128)S(1)} %constant_dynamic-update-slice_fusion.refs_2_), channel_id=1, source_target_pairs={{0,8},{4,12},{8,0},{12,4},{1,9},{5,13},{9,1},{13,5},{2,10},{6,14},... | collective-permute-start | bytes 36872 | tf_op jit(solution)/shard_map/ppermute | solution.py:358
  10.2 4.0 %collective-permute-start.3 = (f32[4,2048]{1,0:T(4,128)S(1)}, f32[4,2048]{1,0:T(4,128)S(1)}, u32[]{:S(2)}, u32[]{:S(2)}) collective-permute-start(f32[4,2048]{1,0:T(4,128)S(1)} %pad_maximum_fusion.refs_4_), channel_id=1, source_target_pairs={{0,2},{1,3},{2,0},{3,1},{4,6},{5,7},{6,4},{7,5},{8,10},{9,11},{10,... | collective-permute-start | bytes 98312 | tf_op jit(solution)/shard_map/ppermute | solution.py:358
  26.7 4.5 %collective-permute-start.4 = (f32[104,128]{1,0:T(8,128)S(1)}, f32[104,128]{1,0:T(8,128)S(1)}, u32[]{:S(2)}, u32[]{:S(2)}) collective-permute-start(f32[104,128]{1,0:T(8,128)S(1)} %get-tuple-element.23.refs_5_), channel_id=1, source_target_pairs={{0,4},{4,0},{8,12},{12,8},{1,5},{5,1},{9,13},{13,9},{2,6},{6,2},{1... | collective-permute-start | bytes 159752 | tf_op jit(solution)/shard_map/ppermute | solution.py:358
  28.4 5.5 %collective-permute-start.5 = (f32[104,128]{1,0:T(8,128)S(1)}, f32[104,128]{1,0:T(8,128)S(1)}, u32[]{:S(2)}, u32[]{:S(2)}) collective-permute-start(f32[104,128]{1,0:T(8,128)S(1)} %get-tuple-element.23.refs_5_), channel_id=1, source_target_pairs={{0,8},{4,12},{8,0},{12,4},{1,9},{5,13},{9,1},{13,5},{2,10},{6,14},... | collective-permute-start | bytes 159752 | tf_op jit(solution)/shard_map/ppermute | solution.py:358
  28.7 6.0 %collective-permute-start.6 = (f32[104,128]{1,0:T(8,128)S(1)}, f32[104,128]{1,0:T(8,128)S(1)}, u32[]{:S(2)}, u32[]{:S(2)}) collective-permute-start(f32[104,128]{1,0:T(8,128)S(1)} %get-tuple-element.23.refs_5_), channel_id=1, source_target_pairs={{0,12},{4,8},{8,4},{12,0},{1,13},{5,9},{9,5},{13,1},{2,14},{6,10},... | collective-permute-start | bytes 159752 | tf_op jit(solution)/shard_map/ppermute | solution.py:358
  42.9 2.6 %collective-permute-start.7 = (f32[16,640]{1,0:T(8,128)S(1)}, f32[16,640]{1,0:T(8,128)S(1)}, u32[]{:S(2)}, u32[]{:S(2)}) collective-permute-start(f32[16,640]{1,0:T(8,128)S(1)} %get-tuple-element.25.refs_5_), channel_id=1, source_target_pairs={{0,1},{1,0},{2,3},{3,2},{4,5},{5,4},{6,7},{7,6},{8,9},{9,8},{10,11... | collective-permute-start | bytes 122888 | tf_op jit(solution)/shard_map/ppermute | solution.py:358
  43.0 4.1 %collective-permute-start.8 = (f32[16,640]{1,0:T(8,128)S(1)}, f32[16,640]{1,0:T(8,128)S(1)}, u32[]{:S(2)}, u32[]{:S(2)}) collective-permute-start(f32[16,640]{1,0:T(8,128)S(1)} %get-tuple-element.25.refs_5_), channel_id=1, source_target_pairs={{0,2},{1,3},{2,0},{3,1},{4,6},{5,7},{6,4},{7,5},{8,10},{9,11},{10,... | collective-permute-start | bytes 122888 | tf_op jit(solution)/shard_map/ppermute | solution.py:358
  44.5 3.5 %collective-permute-start.9 = (f32[16,640]{1,0:T(8,128)S(1)}, f32[16,640]{1,0:T(8,128)S(1)}, u32[]{:S(2)}, u32[]{:S(2)}) collective-permute-start(f32[16,640]{1,0:T(8,128)S(1)} %get-tuple-element.25.refs_5_), channel_id=1, source_target_pairs={{0,3},{1,2},{2,1},{3,0},{4,7},{5,6},{6,5},{7,4},{8,11},{9,10},{10,... | collective-permute-start | bytes 122888 | tf_op jit(solution)/shard_map/ppermute | solution.py:358
  48.8 4.4 %collective-permute-start.10 = (f32[1,128]{1,0:T(1,128)S(1)}, f32[1,128]{1,0:T(1,128)S(1)}, u32[]{:S(2)}, u32[]{:S(2)}) collective-permute-start(f32[1,128]{1,0:T(1,128)S(1)} %get-tuple-element.29.refs_0_), channel_id=1, source_target_pairs={{0,4},{4,0},{8,12},{12,8},{1,5},{5,1},{9,13},{13,9},{2,6},{6,2},{1... | collective-permute-start | bytes 1544 | tf_op jit(solution)/shard_map/ppermute | solution.py:358
  49.6 4.4 %collective-permute-start.11 = (f32[1,128]{1,0:T(1,128)S(1)}, f32[1,128]{1,0:T(1,128)S(1)}, u32[]{:S(2)}, u32[]{:S(2)}) collective-permute-start(f32[1,128]{1,0:T(1,128)S(1)} %get-tuple-element.29.refs_0_), channel_id=1, source_target_pairs={{0,8},{4,12},{8,0},{12,4},{1,9},{5,13},{9,1},{13,5},{2,10},{6,14},... | collective-permute-start | bytes 1544 | tf_op jit(solution)/shard_map/ppermute | solution.py:358
  51.7 5.3 %collective-permute-start.12 = (f32[1,128]{1,0:T(1,128)S(1)}, f32[1,128]{1,0:T(1,128)S(1)}, u32[]{:S(2)}, u32[]{:S(2)}) collective-permute-start(f32[1,128]{1,0:T(1,128)S(1)} %get-tuple-element.29.refs_0_), channel_id=1, source_target_pairs={{0,12},{4,8},{8,4},{12,0},{1,13},{5,9},{9,5},{13,1},{2,14},{6,10},... | collective-permute-start | bytes 1544 | tf_op jit(solution)/shard_map/ppermute | solution.py:358

commit v3 on v2

--- a/solution.py
+++ b/solution.py
@@ -13,6 +13,7 @@
 SHRINK = 2.0**-6
 GROWN = 2.0**-15 * STRENGTH
 TURN = 1024
+BLOCKS_A_TURN = 8
 F8_TOP = 256.0
 F32 = jnp.float32
 BF16 = jnp.bfloat16
@@ -100,20 +101,20 @@
         target[row : row + 1, start : start + 128] = source[at : at + 1, :]
 
 
-def listed_tiles(station_list, cell_list, filled, ranks, own_blocks):
+def listed_counts(station_list, cell_list, filled, ranks, blocks, own_blocks):
+    slots = station_list.shape[1]
+    station_total, cell_total = blocks
     per_cell, per_stn = own_blocks
     station_id = (
-        lax.bitwise_xor(station_list // per_cell, ranks[0]) * per_cell + station_list % per_cell
-    )
-    cell_id = lax.bitwise_xor(cell_list // per_stn, ranks[1]) * per_stn + cell_list % per_stn
-    live = lax.broadcasted_iota(jnp.int32, cell_list.shape, 1) < filled
-    return jnp.concatenate([station_id, jnp.where(live, cell_id, -1)], axis=0)
-
-
-def listed_counts(tiles, station_total, cell_total):
-    slots = tiles.shape[1]
-    station_hot = lax.broadcasted_iota(jnp.int32, (station_total, slots), 0) == tiles[0:1, :]
-    cell_hot = lax.broadcasted_iota(jnp.int32, (cell_total, slots), 0) == tiles[1:2, :]
+        lax.bitwise_xor(station_list[...] // per_cell, ranks[0]) * per_cell
+        + station_list[...] % per_cell
+    )
+    cell_id = (
+        lax.bitwise_xor(cell_list[...] // per_stn, ranks[1]) * per_stn + cell_list[...] % per_stn
+    )
+    live = lax.broadcasted_iota(jnp.int32, (1, slots), 1) < filled
+    station_hot = lax.broadcasted_iota(jnp.int32, (station_total, slots), 0) == station_id
+    cell_hot = (lax.broadcasted_iota(jnp.int32, (cell_total, slots), 0) == cell_id) & live
     count = multiply(cell_hot.astype(F32).astype(BF16), station_hot.astype(F32).astype(BF16), NT)
     wide = (station_total, station_total * STATIONS)
     spread = lax.broadcasted_iota(jnp.int32, wide, 0) == (
@@ -122,17 +123,26 @@
     return multiply(count.astype(BF16), spread.astype(F32).astype(BF16))
 
 
-def forward_kernel(station_pieces, cell_pieces, keep, tiles, residual, *refs):
+def forward_kernel(station_pieces, cell_pieces, keep, filled, *refs):
+    lists_here, refs = refs[:3], refs[3:]
     station_refs = refs[:station_pieces]
     refs = refs[station_pieces:]
     cell_refs = refs[:cell_pieces]
     image, count, station, cell, *outs = refs[cell_pieces:]
     kept = outs[:2] if keep else None
-    station_rows, cell_rows, left, right, source, narrow, moments = outs[2 if keep else 0 :]
+    station_rows, cell_rows, left, right, source, narrow, moments, dense, *held, arrived = outs[
+        2 if keep else 0 :
+    ]
+    copies = [
+        pltpu.make_async_copy(here, there, arrived.at[at])
+        for at, (here, there) in enumerate(zip(lists_here, held))
+    ]
+    for copy in copies:
+        copy.start()
+    station_list, cell_list, residual = held
     width, extent = station.shape[1], cell.shape[1]
     join(cell, cell_refs, 4)
     join(station, station_refs, 3 if keep else 9)
-    count[...] = listed_counts(tiles, width // STATIONS, extent // CELLS)
     fill_station_rows(station_rows, station[0:3, :])
     right[...] = station_rows[...].astype(BF16)
     fill_cell_rows(cell_rows, cell[0:3, :])
@@ -148,7 +158,6 @@
     source[...] = jnp.concatenate([part.astype(BF16) for part in parts], axis=0)
     high, low, unit = narrow_parts(cell_rows[0:16, :])
     narrow[...] = jnp.concatenate([high, low], axis=0).astype(F8)
-    moments[...] = jnp.zeros_like(moments)
     spans = width // SPAN
 
     def turn(which, carry):
@@ -158,9 +167,8 @@
         squared = multiply(left[cells, :], right[:, lanes])
         high, low = falloff_parts(squared, F8)
         if keep:
-            kept[0][cells, :] = high
-            kept[1][cells, :] = low
-        sums = moments[:, lanes]
+            kept[0][cells, lanes] = high
+            kept[1][cells, lanes] = low
         for at in range(TURN // CELLS):
             block = group * (TURN // CELLS) + at
             here = pl.ds(pl.multiple_of(block * CELLS, CELLS), CELLS)
@@ -169,24 +177,45 @@
             fine = multiply(narrow[:, here], low[rows])
             total = wide[0:16] + wide[16:32] + wide[32:48]
             total = total + (fine[0:16] + fine[16:32] * (1.0 / 16.0)) * unit
-            sums = sums + total * count[pl.ds(block, 1), lanes]
-        moments[:, lanes] = sums
+            moments[block, :, lanes] = total
         return carry
 
     lax.fori_loop(0, spans * (extent // TURN), turn, 0)
-    sx, sy, sz = station[0:1, :], station[1:2, :], station[2:3, :]
-    total, mx, my, mz, mxx, mxy, mxz, myy, myz, mzz = (moments[k : k + 1, :] for k in range(10))
+    for copy in copies:
+        copy.wait()
+    count[...] = listed_counts(
+        station_list,
+        cell_list,
+        filled[0, 0],
+        (lax.axis_index("cell") if keep else 0, lax.axis_index("stn")),
+        (width // STATIONS, extent // CELLS),
+        (residual.shape[1] // STATIONS, extent // CELLS // lax.axis_size("stn")),
+    )
+    sums = moments[0] * count[0:1, :]
+    for block in range(1, extent // CELLS):
+        sums = sums + moments[block] * count[block : block + 1, :]
+    moments[0] = sums
+    rows = width // 128
+    for k in range(10):
+        pack(dense, k * rows, moments[0, k : k + 1, :])
+    for k in range(3):
+        pack(dense, (10 + k) * rows, station[k : k + 1, :])
+    total, mx, my, mz, mxx, mxy, mxz, myy, myz, mzz, sx, sy, sz = (
+        dense[k * rows : (k + 1) * rows, :] for k in range(13)
+    )
     xx = sx * (sx * total - 2.0 * mx) + mxx
     yy = sy * (sy * total - 2.0 * my) + myy
     zz = sz * (sz * total - 2.0 * mz) + mzz
     xy = sx * (sy * total - my) - sy * mx + mxy
     xz = sx * (sz * total - mz) - sz * mx + mxz
     yz = sy * (sz * total - mz) - sz * my + myz
-    rows = (2.0 * xx - yy - zz, 3.0 * xy, 3.0 * xz, 2.0 * yy - xx - zz, 3.0 * yz)
-    for k, row in enumerate(rows):
-        pack(image, k * (width // 128), GROWN * row)
+    parts = (2.0 * xx - yy - zz, 3.0 * xy, 3.0 * xz, 2.0 * yy - xx - zz, 3.0 * yz)
+    for k, part in enumerate(parts):
+        image[k * rows : (k + 1) * rows, :] = GROWN * part
     if keep:
-        image[5 * (width // 128) :, :] = residual[...]
+        for k in range(6):
+            at = 5 * rows + k * (residual.shape[1] // 128)
+            pack(image, at, residual[k : k + 1, :])
 
 
 def tree(values):
@@ -270,8 +299,8 @@
     blocks = extent // CELLS
 
     def turn(group, carry):
-        for at in range(TURN // CELLS):
-            block = group * (TURN // CELLS) + at
+        for at in range(BLOCKS_A_TURN):
+            block = group * BLOCKS_A_TURN + at
             cells = pl.ds(pl.multiple_of(block * CELLS, CELLS), CELLS)
             counted = vectors[...] * count[pl.ds(block, 1), :]
             weights = jnp.concatenate(three_parts(counted), axis=0).astype(BF16)
@@ -284,7 +313,7 @@
             write_partial(partial, sums, cell[0:3, cells], block, blocks)
         return carry
 
-    lax.fori_loop(0, extent // TURN, turn, 0)
+    lax.fori_loop(0, blocks // BLOCKS_A_TURN, turn, 0)
 
 
 def adjoint_kernel(count, station, cell, image_ref, *refs):
@@ -386,22 +415,16 @@
     own, cell_own = station_place.shape[1], cell_place.shape[1]
     width, extent = cell_size * own, stn_size * cell_own
     rows, blocks = width // 128, extent // CELLS
-    ranks = (lax.axis_index("cell") if direct else 0, lax.axis_index("stn"))
-    tiles = listed_tiles(
-        station_blocks.reshape(1, -1),
-        cell_blocks.reshape(1, -1),
-        pair_count.reshape(()),
-        ranks,
-        (own // STATIONS, cell_own // CELLS),
-    )
     if direct:
         station_parts = doubled(station_place, "cell", cell_size)
     else:
         both = jnp.concatenate([station_place, residual], axis=0)
         station_parts = [lax.all_gather(both, "cell", axis=1, tiled=True)]
     cell_mine = jnp.concatenate([cell_place, direction[None]], axis=0)
-    cell_parts = doubled(cell_mine, "stn", stn_size)
+    cell_parts = exchanged(cell_mine, "stn", stn_size)
     in_vmem, in_smem = pl.BlockSpec(memory_space=pltpu.VMEM), pl.BlockSpec(memory_space=pltpu.SMEM)
+    in_hbm = pl.BlockSpec(memory_space=pltpu.HBM)
+    lists = (station_blocks.reshape(1, -1), cell_blocks.reshape(1, -1), residual)
     params = pltpu.CompilerParams(vmem_limit_bytes=(16 if direct else 56) * 2**20)
     small = pltpu.CompilerParams(vmem_limit_bytes=2**20)
     counts = (len(station_parts), len(cell_parts))
@@ -424,7 +447,7 @@
     image_part, *kept = pl.pallas_call(
         forward,
         out_shape=out_shape,
-        in_specs=[in_vmem] * (2 + pieces),
+        in_specs=[in_smem] + [in_hbm] * 3 + [in_vmem] * pieces,
         out_specs=[in_vmem] * len(out_shape),
         scratch_shapes=[
             pltpu.VMEM((DEPTH, width), F32),
@@ -433,11 +456,19 @@
             pltpu.VMEM((DEPTH, width), BF16),
             pltpu.VMEM((48, extent), BF16),
             pltpu.VMEM((32, extent), F8),
-            pltpu.VMEM((16, width), F32),
+            pltpu.VMEM((blocks, 16, width), F32),
+            pltpu.VMEM((13 * rows, 128), F32),
+            *(pltpu.VMEM(here.shape, here.dtype) for here in lists),
+            pltpu.SemaphoreType.DMA((3,)),
         ],
         compiler_params=params,
         name="forward",
-    )(tiles, residual.reshape(-1, 128), *station_parts, *cell_parts)
+    )(
+        pair_count,
+        *(pltpu.with_memory_space_constraint(here, pltpu.HBM) for here in lists),
+        *station_parts,
+        *cell_parts,
+    )
     if direct:
         image_parts = exchanged(image_part, "cell", cell_size)
     else:

time: 58.2 us -> 57.4 us (0.986)
  waiting for transfers between devices: 11.7 us -> 13.3 us
  other arithmetic: 2.24 us -> 0.76 us
  local copies, waits for them, and re-layouts: 1.45 us -> 0.75 us
  Pallas kernels: 22 us -> 21.3 us
  starting transfers between devices: 18.3 us -> 18.9 us
    ppermute x13 -> x14, waiting for transfers between devices: 11.7 us -> 13.3 us  [sent(): lax.ppermute(value, axis, [(rank, rank ^ other) for rank in range(size)])]
    pallas_call x1, Pallas kernels: 8.13 us -> 7.09 us  [on_device(): pl.pallas_call(adjoint, out_shape=(jax.ShapeDtypeStruct((2 * blocks, CELL...]
    concatenate x2 -> x0, other arithmetic: 0.75 us -> none  [the longest x1 0.75 us: doubled(): value = jnp.concatenate([value, sent(value, axis, size, step)], axis=1)]
    select_n x1 -> x0, other arithmetic: 0.72 us -> none  [listed_tiles(): return jnp.concatenate([station_id, jnp.where(live, cell_id, -1)], axis=0)]
    reshape x1 -> x0, local copies, waits for them, and re-layouts: 0.72 us -> none  [on_device(): residual.reshape(-1, 128)]
    ppermute x13 -> x14, starting transfers between devices: 18.3 us -> 18.9 us  [sent(): lax.ppermute(value, axis, [(rank, rank ^ other) for rank in range(size)])]
  transfers between devices with their start and end apart: 13 -> 14, of which waited for: 7 -> 8; matrix products, arithmetic and copies ran while one was open for 5% -> 1% of each run, Pallas kernels for 0% -> 0%
where the time goes in v3:
time: 57.4 us; the launch traced here: 57.1 us
  Pallas kernels  21.3 us (37%)
  starting transfers between devices  18.9 us (33%)
  waiting for transfers between devices  13.3 us (23%)
  between operations  2.02 us (4%)
  other arithmetic  0.76 us (1%)
  local copies, waits for them, and re-layouts  0.75 us (1%)
    ppermute x14, starting transfers between devices, sent(): lax.ppermute(value, axis, [(rank, rank ^ other) for rank in range(size)])  18.9 us
    ppermute x14, waiting for transfers between devices, sent(): lax.ppermute(value, axis, [(rank, rank ^ other) for rank in range(size)])  13.3 us
    pallas_call x1, Pallas kernels, on_device(): pl.pallas_call(forward, out_shape=out_shape, in_specs=[in_smem] + [in_hbm...  12.9 us
    pallas_call x1, Pallas kernels, on_device(): pl.pallas_call(adjoint, out_shape=(jax.ShapeDtypeStruct((2 * blocks, CELL...  7.09 us
  transfers between devices with their start and end apart: 14, of which 8 were waited for; matrix products, arithmetic and copies ran while one was open for 1% of the time, Pallas kernels for 0%

profile of v3, /device:TPU:0, one launch (start us, length us, event | category | flops | bytes accessed | tf_op | source)
XLA Modules:
  0.0 57.1 jit_solution(9381957945286726535)
XLA Ops:
  0.6 0.0 copy-start.1
  0.6 0.0 copy-start
  0.7 0.0 copy-start.2
  0.7 0.8 %pad_maximum_fusion.refs_6_ = f32[4,1024]{1,0:T(4,128)S(1)} fusion(f32[1,1024]{1,0:T(1,128)} %bitcast.7, f32[3,1024]{1,0:T(4,128)} %param.14), kind=kLoop, calls=%fused_computation | loop fusion | flops 4096 | bytes 32768 | tf_op jit(solution)/shard_map/concatenate | solution.py:423
  1.4 0.5 collective-permute-start.2
  1.9 2.6 %collective-permute-start.3 = (f32[4,1024]{1,0:T(4,128)S(1)}, f32[4,1024]{1,0:T(4,128)S(1)}, u32[]{:S(2)}, u32[]{:S(2)}) collective-permute-start(f32[4,1024]{1,0:T(4,128)S(1)} %pad_maximum_fusion.refs_6_), channel_id=1, source_target_pairs={{0,2},{1,3},{2,0},{3,1},{4,6},{5,7},{6,4},{7,5},{8,10},{9,11},{10,... | collective-permute-start | bytes 49160 | tf_op jit(solution)/shard_map/ppermute | solution.py:387
  4.5 0.1 collective-permute-start.4
  4.6 1.8 %collective-permute-start = (f32[3,512]{1,0:T(4,128)}, f32[3,512]{1,0:T(4,128)S(1)}, u32[]{:S(2)}, u32[]{:S(2)}) collective-permute-start(f32[3,512]{1,0:T(4,128)} %param.13), channel_id=1, source_target_pairs={{0,4},{4,0},{8,12},{12,8},{1,5},{5,1},{9,13},{13,9},{2,6},{6,2},{1... | collective-permute-start | bytes 18440 | tf_op jit(solution)/shard_map/ppermute | solution.py:387
  6.4 0.7 %constant_dynamic-update-slice_fusion.1 = f32[3,1024]{1,0:T(4,128)S(1)} fusion(f32[3,512]{1,0:T(4,128)} %param.13), kind=kLoop, calls=%fused_computation.2 | loop fusion | bytes 14336
  7.1 1.3 %collective-permute-done = f32[3,512]{1,0:T(4,128)S(1)} collective-permute-done((f32[3,512]{1,0:T(4,128)}, f32[3,512]{1,0:T(4,128)S(1)}, u32[]{:S(2)}, u32[]{:S(2)}) %collective-permute-start) | collective-permute-done | bytes 6176 | tf_op jit(solution)/shard_map/ppermute | solution.py:387
  8.4 2.8 %collective-permute-start.1 = (f32[3,1024]{1,0:T(4,128)S(1)}, f32[3,1024]{1,0:T(4,128)S(1)}, u32[]{:S(2)}, u32[]{:S(2)}) collective-permute-start(f32[3,1024]{1,0:T(4,128)S(1)} %constant_dynamic-update-slice_fusion.refs_4_), channel_id=1, source_target_pairs={{0,8},{4,12},{8,0},{12,4},{1,9},{5,13},{9,1},{13,5},{2,10},{6,14},... | collective-permute-start | bytes 36872 | tf_op jit(solution)/shard_map/ppermute | solution.py:387
  11.9 0.0 collective-permute-done.2.refs_7_
  11.9 0.0 collective-permute-done.3.refs_8_
  11.9 0.0 collective-permute-done.4.refs_9_
  12.0 1.1 %collective-permute-done.1.refs_5_ = f32[3,1024]{1,0:T(4,128)S(1)} collective-permute-done((f32[3,1024]{1,0:T(4,128)S(1)}, f32[3,1024]{1,0:T(4,128)S(1)}, u32[]{:S(2)}, u32[]{:S(2)}) %collective-permute-start.1) | collective-permute-done | bytes 12320 | tf_op jit(solution)/shard_map/ppermute | solution.py:387
  13.1 12.9 %forward.1 = (f32[104,128]{1,0:T(8,128)S(1)}, f32[8,2048]{1,0:T(8,128)S(1)}, f32[16,2048]{1,0:T(8,128)S(1)}, f32[8,4096]{1,0:T(8,128)S(1)}, bf16[4096,2048]{1,0:...) custom-call(s32[1,1]{1,0:T(1,128)S(6)} %copy.15.refs_0_, s32[1,256]{1,0:T(1,128)} %bitcast.11, s32[1,256]{1,0:T(1,128)} %bitcast.12, ...), custom_call_target="tpu_custom_call" | custom-call | tf_op jit(solution)/shard_map/forward/pallas_call | solution.py:447
  26.0 1.9 %collective-permute-start.5 = (f32[104,128]{1,0:T(8,128)S(1)}, f32[104,128]{1,0:T(8,128)S(1)}, u32[]{:S(2)}, u32[]{:S(2)}) collective-permute-start(f32[104,128]{1,0:T(8,128)S(1)} %get-tuple-element.23.refs_5_), channel_id=1, source_target_pairs={{0,4},{4,0},{8,12},{12,8},{1,5},{5,1},{9,13},{13,9},{2,6},{6,2},{1... | collective-permute-start | bytes 159752 | tf_op jit(solution)/shard_map/ppermute | solution.py:387
  27.9 2.6 %collective-permute-start.6 = (f32[104,128]{1,0:T(8,128)S(1)}, f32[104,128]{1,0:T(8,128)S(1)}, u32[]{:S(2)}, u32[]{:S(2)}) collective-permute-start(f32[104,128]{1,0:T(8,128)S(1)} %get-tuple-element.23.refs_5_), channel_id=1, source_target_pairs={{0,8},{4,12},{8,0},{12,4},{1,9},{5,13},{9,1},{13,5},{2,10},{6,14},... | collective-permute-start | bytes 159752 | tf_op jit(solution)/shard_map/ppermute | solution.py:387
  30.6 0.0 collective-permute-start.7
  30.6 0.0 collective-permute-done.5.refs_6_
  30.6 3.5 %collective-permute-done.6.refs_7_ = f32[104,128]{1,0:T(8,128)S(1)} collective-permute-done((f32[104,128]{1,0:T(8,128)S(1)}, f32[104,128]{1,0:T(8,128)S(1)}, u32[]{:S(2)}, u32[]{:S(2)}) %collective-permute-start.6) | collective-permute-done | bytes 53280 | tf_op jit(solution)/shard_map/ppermute | solution.py:387
  34.1 2.4 %collective-permute-done.7.refs_8_ = f32[104,128]{1,0:T(8,128)S(1)} collective-permute-done((f32[104,128]{1,0:T(8,128)S(1)}, f32[104,128]{1,0:T(8,128)S(1)}, u32[]{:S(2)}, u32[]{:S(2)}) %collective-permute-start.7) | collective-permute-done | bytes 53280 | tf_op jit(solution)/shard_map/ppermute | solution.py:387
  36.5 7.1 %adjoint.1 = (f32[16,640]{1,0:T(8,128)S(1)}, f32[8,512]{1,0:T(8,128)S(1)}) custom-call(f32[8,2048]{1,0:T(8,128)S(1)} %get-tuple-element.18.refs_0_, f32[16,2048]{1,0:T(8,128)S(1)} %get-tuple-element.19.refs_1_, f32[8,4096]{1,0:T(8,128)S(1)} %get-tuple-element.20.refs_2_, bf16[4096,2048]{1,0:T(8,128)(2,1)S(1)} %get-tuple-element.21.refs_3_, ...), custom_call_target="tpu_custom_call" | custom-call | tf_op jit(solution)/shard_map/adjoint/pallas_call | solution.py:489
  43.6 0.1 collective-permute-start.10
  43.7 1.6 %collective-permute-start.8 = (f32[16,640]{1,0:T(8,128)S(1)}, f32[16,640]{1,0:T(8,128)S(1)}, u32[]{:S(2)}, u32[]{:S(2)}) collective-permute-start(f32[16,640]{1,0:T(8,128)S(1)} %get-tuple-element.25.refs_5_), channel_id=1, source_target_pairs={{0,1},{1,0},{2,3},{3,2},{4,5},{5,4},{6,7},{7,6},{8,9},{9,8},{10,11... | collective-permute-start | bytes 122888 | tf_op jit(solution)/shard_map/ppermute | solution.py:387
  45.3 0.5 collective-permute-start.9
  46.4 1.0 %collective-permute-done.10.refs_8_ = f32[16,640]{1,0:T(8,128)S(1)} collective-permute-done((f32[16,640]{1,0:T(8,128)S(1)}, f32[16,640]{1,0:T(8,128)S(1)}, u32[]{:S(2)}, u32[]{:S(2)}) %collective-permute-start.10) | collective-permute-done | bytes 40992 | tf_op jit(solution)/shard_map/ppermute | solution.py:387
  47.5 0.0 collective-permute-done.8.refs_6_
  47.5 1.8 %collective-permute-done.9.refs_7_ = f32[16,640]{1,0:T(8,128)S(1)} collective-permute-done((f32[16,640]{1,0:T(8,128)S(1)}, f32[16,640]{1,0:T(8,128)S(1)}, u32[]{:S(2)}, u32[]{:S(2)}) %collective-permute-start.9) | collective-permute-done | bytes 40992 | tf_op jit(solution)/shard_map/ppermute | solution.py:387
  49.3 0.0 copy-done.1
  49.3 0.0 copy-done
  49.3 0.0 copy-done.2
  49.3 0.7 %update.1 = (f32[8,128]{1,0:T(8,128)}, f32[6,512]{1,0:T(8,128)}, f32[8,128]{1,0:T(8,128)S(1)}, f32[1,128]{1,0:T(1,128)S(1)}) custom-call(f32[1]{0:T(128)S(6)} %copy.14.refs_0_.gradient_norm, f32[8,128]{1,0:T(8,128)S(1)} %bitcast.10, f32[8,128]{1,0:T(8,128)S(1)} %bitcast.8, f32[6,512]{1,0:T(8,128)S(1)} %copy-done, f32[8,512]{1,0:T(8,128)S(1)} %get-tuple-element.24.refs_4_, ...), custom_call_target="tpu_custom_call" | custom-call | tf_op jit(solution)/shard_map/update/pallas_call | solution.py:513
  50.0 0.0 collective-permute-start.11
  50.0 1.2 %collective-permute-start.12 = (f32[1,128]{1,0:T(1,128)S(1)}, f32[1,128]{1,0:T(1,128)S(1)}, u32[]{:S(2)}, u32[]{:S(2)}) collective-permute-start(f32[1,128]{1,0:T(1,128)S(1)} %get-tuple-element.29.refs_0_), channel_id=1, source_target_pairs={{0,8},{4,12},{8,0},{12,4},{1,9},{5,13},{9,1},{13,5},{2,10},{6,14},... | collective-permute-start | bytes 1544 | tf_op jit(solution)/shard_map/ppermute | solution.py:387
  51.2 3.2 %collective-permute-start.13 = (f32[1,128]{1,0:T(1,128)S(1)}, f32[1,128]{1,0:T(1,128)S(1)}, u32[]{:S(2)}, u32[]{:S(2)}) collective-permute-start(f32[1,128]{1,0:T(1,128)S(1)} %get-tuple-element.29.refs_0_), channel_id=1, source_target_pairs={{0,12},{4,8},{8,4},{12,0},{1,13},{5,9},{9,5},{13,1},{2,14},{6,10},... | collective-permute-start | bytes 1544 | tf_op jit(solution)/shard_map/ppermute | solution.py:387
  54.4 0.0 collective-permute-done.11.refs_1_
  54.4 0.1 collective-permute-done.12.refs_2_
  54.4 2.1 %collective-permute-done.13.refs_3_ = f32[1,128]{1,0:T(1,128)S(1)} collective-permute-done((f32[1,128]{1,0:T(1,128)S(1)}, f32[1,128]{1,0:T(1,128)S(1)}, u32[]{:S(2)}, u32[]{:S(2)}) %collective-permute-start.13) | collective-permute-done | bytes 544 | tf_op jit(solution)/shard_map/ppermute | solution.py:387
  56.5 0.6 %finish.1 = (f32[8,128]{1,0:T(8,128)}, f32[1]{0:T(128)}) custom-call(f32[1]{0:T(128)S(6)} %copy.14.refs_0_.gradient_norm, f32[8,128]{1,0:T(8,128)S(1)} %get-tuple-element.28.gradient, f32[8,128]{1,0:T(8,128)S(1)} %bitcast.9, f32[1,128]{1,0:T(1,128)S(1)} %get-tuple-element.29.refs_0_, f32[1,128]{1,0:T(1,128)S(1)} %collective-permute-done.11.refs_1_, ...), custom_call_target="tpu_custom_call" | custom-call | tf_op jit(solution)/shard_map/finish/pallas_call | solution.py:530
  (1 shorter events, 0.0 us)
Async XLA Ops:
  0.6 48.6 %copy-start.1 = (f32[1024]{0:T(1024)S(1)}, f32[1024]{0:T(1024)}, u32[]{:S(2)}) copy-start(f32[1024]{0:T(1024)} %param.11) | copy-start | bytes 12292
  0.6 48.6 %copy-start = (f32[6,512]{1,0:T(8,128)S(1)}, f32[6,512]{1,0:T(8,128)}, u32[]{:S(2)}) copy-start(f32[6,512]{1,0:T(8,128)} %refs_3_.3) | copy-start | bytes 36868
  0.7 48.6 %copy-start.2 = (f32[1024]{0:T(1024)S(1)}, f32[1024]{0:T(1024)}, u32[]{:S(2)}) copy-start(f32[1024]{0:T(1024)} %param.9) | copy-start | bytes 12292
  1.4 10.5 %collective-permute-start.2 = (f32[4,1024]{1,0:T(4,128)S(1)}, f32[4,1024]{1,0:T(4,128)S(1)}, u32[]{:S(2)}, u32[]{:S(2)}) collective-permute-start(f32[4,1024]{1,0:T(4,128)S(1)} %pad_maximum_fusion.refs_6_), channel_id=1, source_target_pairs={{0,1},{1,0},{2,3},{3,2},{4,5},{5,4},{6,7},{7,6},{8,9},{9,8},{10,11... | collective-permute-start | bytes 49160 | tf_op jit(solution)/shard_map/ppermute | solution.py:387
  1.9 10.0 %collective-permute-start.3 = (f32[4,1024]{1,0:T(4,128)S(1)}, f32[4,1024]{1,0:T(4,128)S(1)}, u32[]{:S(2)}, u32[]{:S(2)}) collective-permute-start(f32[4,1024]{1,0:T(4,128)S(1)} %pad_maximum_fusion.refs_6_), channel_id=1, source_target_pairs={{0,2},{1,3},{2,0},{3,1},{4,6},{5,7},{6,4},{7,5},{8,10},{9,11},{10,... | collective-permute-start | bytes 49160 | tf_op jit(solution)/shard_map/ppermute | solution.py:387
  4.5 7.4 %collective-permute-start.4 = (f32[4,1024]{1,0:T(4,128)S(1)}, f32[4,1024]{1,0:T(4,128)S(1)}, u32[]{:S(2)}, u32[]{:S(2)}) collective-permute-start(f32[4,1024]{1,0:T(4,128)S(1)} %pad_maximum_fusion.refs_6_), channel_id=1, source_target_pairs={{0,3},{1,2},{2,1},{3,0},{4,7},{5,6},{6,5},{7,4},{8,11},{9,10},{10,... | collective-permute-start | bytes 49160 | tf_op jit(solution)/shard_map/ppermute | solution.py:387
  4.6 3.9 %collective-permute-start = (f32[3,512]{1,0:T(4,128)}, f32[3,512]{1,0:T(4,128)S(1)}, u32[]{:S(2)}, u32[]{:S(2)}) collective-permute-start(f32[3,512]{1,0:T(4,128)} %param.13), channel_id=1, source_target_pairs={{0,4},{4,0},{8,12},{12,8},{1,5},{5,1},{9,13},{13,9},{2,6},{6,2},{1... | collective-permute-start | bytes 18440 | tf_op jit(solution)/shard_map/ppermute | solution.py:387
  8.4 4.6 %collective-permute-start.1 = (f32[3,1024]{1,0:T(4,128)S(1)}, f32[3,1024]{1,0:T(4,128)S(1)}, u32[]{:S(2)}, u32[]{:S(2)}) collective-permute-start(f32[3,1024]{1,0:T(4,128)S(1)} %constant_dynamic-update-slice_fusion.refs_4_), channel_id=1, source_target_pairs={{0,8},{4,12},{8,0},{12,4},{1,9},{5,13},{9,1},{13,5},{2,10},{6,14},... | collective-permute-start | bytes 36872 | tf_op jit(solution)/shard_map/ppermute | solution.py:387
  26.0 4.5 %collective-permute-start.5 = (f32[104,128]{1,0:T(8,128)S(1)}, f32[104,128]{1,0:T(8,128)S(1)}, u32[]{:S(2)}, u32[]{:S(2)}) collective-permute-start(f32[104,128]{1,0:T(8,128)S(1)} %get-tuple-element.23.refs_5_), channel_id=1, source_target_pairs={{0,4},{4,0},{8,12},{12,8},{1,5},{5,1},{9,13},{13,9},{2,6},{6,2},{1... | collective-permute-start | bytes 159752 | tf_op jit(solution)/shard_map/ppermute | solution.py:387
  27.9 6.2 %collective-permute-start.6 = (f32[104,128]{1,0:T(8,128)S(1)}, f32[104,128]{1,0:T(8,128)S(1)}, u32[]{:S(2)}, u32[]{:S(2)}) collective-permute-start(f32[104,128]{1,0:T(8,128)S(1)} %get-tuple-element.23.refs_5_), channel_id=1, source_target_pairs={{0,8},{4,12},{8,0},{12,4},{1,9},{5,13},{9,1},{13,5},{2,10},{6,14},... | collective-permute-start | bytes 159752 | tf_op jit(solution)/shard_map/ppermute | solution.py:387
  30.6 5.9 %collective-permute-start.7 = (f32[104,128]{1,0:T(8,128)S(1)}, f32[104,128]{1,0:T(8,128)S(1)}, u32[]{:S(2)}, u32[]{:S(2)}) collective-permute-start(f32[104,128]{1,0:T(8,128)S(1)} %get-tuple-element.23.refs_5_), channel_id=1, source_target_pairs={{0,12},{4,8},{8,4},{12,0},{1,13},{5,9},{9,5},{13,1},{2,14},{6,10},... | collective-permute-start | bytes 159752 | tf_op jit(solution)/shard_map/ppermute | solution.py:387
  43.6 3.9 %collective-permute-start.10 = (f32[16,640]{1,0:T(8,128)S(1)}, f32[16,640]{1,0:T(8,128)S(1)}, u32[]{:S(2)}, u32[]{:S(2)}) collective-permute-start(f32[16,640]{1,0:T(8,128)S(1)} %get-tuple-element.25.refs_5_), channel_id=1, source_target_pairs={{0,3},{1,2},{2,1},{3,0},{4,7},{5,6},{6,5},{7,4},{8,11},{9,10},{10,... | collective-permute-start | bytes 122888 | tf_op jit(solution)/shard_map/ppermute | solution.py:387
  43.7 3.8 %collective-permute-start.8 = (f32[16,640]{1,0:T(8,128)S(1)}, f32[16,640]{1,0:T(8,128)S(1)}, u32[]{:S(2)}, u32[]{:S(2)}) collective-permute-start(f32[16,640]{1,0:T(8,128)S(1)} %get-tuple-element.25.refs_5_), channel_id=1, source_target_pairs={{0,1},{1,0},{2,3},{3,2},{4,5},{5,4},{6,7},{7,6},{8,9},{9,8},{10,11... | collective-permute-start | bytes 122888 | tf_op jit(solution)/shard_map/ppermute | solution.py:387
  45.3 4.0 %collective-permute-start.9 = (f32[16,640]{1,0:T(8,128)S(1)}, f32[16,640]{1,0:T(8,128)S(1)}, u32[]{:S(2)}, u32[]{:S(2)}) collective-permute-start(f32[16,640]{1,0:T(8,128)S(1)} %get-tuple-element.25.refs_5_), channel_id=1, source_target_pairs={{0,2},{1,3},{2,0},{3,1},{4,6},{5,7},{6,4},{7,5},{8,10},{9,11},{10,... | collective-permute-start | bytes 122888 | tf_op jit(solution)/shard_map/ppermute | solution.py:387
  50.0 4.4 %collective-permute-start.11 = (f32[1,128]{1,0:T(1,128)S(1)}, f32[1,128]{1,0:T(1,128)S(1)}, u32[]{:S(2)}, u32[]{:S(2)}) collective-permute-start(f32[1,128]{1,0:T(1,128)S(1)} %get-tuple-element.29.refs_0_), channel_id=1, source_target_pairs={{0,4},{4,0},{8,12},{12,8},{1,5},{5,1},{9,13},{13,9},{2,6},{6,2},{1... | collective-permute-start | bytes 1544 | tf_op jit(solution)/shard_map/ppermute | solution.py:387
  50.0 4.4 %collective-permute-start.12 = (f32[1,128]{1,0:T(1,128)S(1)}, f32[1,128]{1,0:T(1,128)S(1)}, u32[]{:S(2)}, u32[]{:S(2)}) collective-permute-start(f32[1,128]{1,0:T(1,128)S(1)} %get-tuple-element.29.refs_0_), channel_id=1, source_target_pairs={{0,8},{4,12},{8,0},{12,4},{1,9},{5,13},{9,1},{13,5},{2,10},{6,14},... | collective-permute-start | bytes 1544 | tf_op jit(solution)/shard_map/ppermute | solution.py:387
  51.2 5.3 %collective-permute-start.13 = (f32[1,128]{1,0:T(1,128)S(1)}, f32[1,128]{1,0:T(1,128)S(1)}, u32[]{:S(2)}, u32[]{:S(2)}) collective-permute-start(f32[1,128]{1,0:T(1,128)S(1)} %get-tuple-element.29.refs_0_), channel_id=1, source_target_pairs={{0,12},{4,8},{8,4},{12,0},{1,13},{5,9},{9,5},{13,1},{2,14},{6,10},... | collective-permute-start | bytes 1544 | tf_op jit(solution)/shard_map/ppermute | solution.py:387

commit v4 on v3

--- a/solution.py
+++ b/solution.py
@@ -123,16 +123,9 @@
     return multiply(count.astype(BF16), spread.astype(F32).astype(BF16))
 
 
-def forward_kernel(station_pieces, cell_pieces, keep, filled, *refs):
-    lists_here, refs = refs[:3], refs[3:]
-    station_refs = refs[:station_pieces]
-    refs = refs[station_pieces:]
-    cell_refs = refs[:cell_pieces]
-    image, count, station, cell, *outs = refs[cell_pieces:]
-    kept = outs[:2] if keep else None
-    station_rows, cell_rows, left, right, source, narrow, moments, dense, *held, arrived = outs[
-        2 if keep else 0 :
-    ]
+def prepare_kernel(cell_pieces, keep, scalars, *refs):
+    lists_here, cell_refs, refs = refs[:3], refs[3 : 3 + cell_pieces], refs[3 + cell_pieces :]
+    cell, count, last_norm, left, source, narrow, units, packed, cell_rows, *held, arrived = refs
     copies = [
         pltpu.make_async_copy(here, there, arrived.at[at])
         for at, (here, there) in enumerate(zip(lists_here, held))
@@ -140,11 +133,8 @@
     for copy in copies:
         copy.start()
     station_list, cell_list, residual = held
-    width, extent = station.shape[1], cell.shape[1]
+    width, extent = count.shape[1], cell.shape[1]
     join(cell, cell_refs, 4)
-    join(station, station_refs, 3 if keep else 9)
-    fill_station_rows(station_rows, station[0:3, :])
-    right[...] = station_rows[...].astype(BF16)
     fill_cell_rows(cell_rows, cell[0:3, :])
     transpose_into(left, cell_rows)
     value = cell[3:4, :]
@@ -158,6 +148,32 @@
     source[...] = jnp.concatenate([part.astype(BF16) for part in parts], axis=0)
     high, low, unit = narrow_parts(cell_rows[0:16, :])
     narrow[...] = jnp.concatenate([high, low], axis=0).astype(F8)
+    units[...] = jnp.broadcast_to(unit, units.shape)
+    last_norm[...] = scalars[3:4, scalars.shape[1] - 128 :]
+    for copy in copies:
+        copy.wait()
+    count[...] = listed_counts(
+        station_list,
+        cell_list,
+        scalars[3:4, 0:1].astype(jnp.int32),
+        (lax.axis_index("cell") if keep else 0, lax.axis_index("stn")),
+        (width // STATIONS, extent // CELLS),
+        (residual.shape[1] // STATIONS, extent // CELLS // lax.axis_size("stn")),
+    )
+    for k in range(6):
+        pack(packed, k * (residual.shape[1] // 128), residual[k : k + 1, :])
+
+
+def forward_kernel(station_pieces, keep, count, left, source, narrow, units, packed, *refs):
+    station_refs = refs[:station_pieces]
+    image, station, *outs = refs[station_pieces:]
+    kept = outs[:2] if keep else None
+    station_rows, right, moments, dense = outs[2 if keep else 0 :]
+    width, extent = station.shape[1], left.shape[0]
+    join(station, station_refs, 3 if keep else 9)
+    fill_station_rows(station_rows, station[0:3, :])
+    right[...] = station_rows[...].astype(BF16)
+    unit = units[:, 0:1]
     spans = width // SPAN
 
     def turn(which, carry):
@@ -181,16 +197,6 @@
         return carry
 
     lax.fori_loop(0, spans * (extent // TURN), turn, 0)
-    for copy in copies:
-        copy.wait()
-    count[...] = listed_counts(
-        station_list,
-        cell_list,
-        filled[0, 0],
-        (lax.axis_index("cell") if keep else 0, lax.axis_index("stn")),
-        (width // STATIONS, extent // CELLS),
-        (residual.shape[1] // STATIONS, extent // CELLS // lax.axis_size("stn")),
-    )
     sums = moments[0] * count[0:1, :]
     for block in range(1, extent // CELLS):
         sums = sums + moments[block] * count[block : block + 1, :]
@@ -213,9 +219,7 @@
     for k, part in enumerate(parts):
         image[k * rows : (k + 1) * rows, :] = GROWN * part
     if keep:
-        for k in range(6):
-            at = 5 * rows + k * (residual.shape[1] // 128)
-            pack(image, at, residual[k : k + 1, :])
+        image[5 * rows :, :] = packed[...]
 
 
 def tree(values):
@@ -353,7 +357,7 @@
     densities_next, residual_next, gradient, norm = refs[pieces:]
     blocks = partial_refs[0].shape[0] // 2
     each = blocks // pieces
-    step = gradient_norm[0] / tree(ref[0:1, CELLS : CELLS + 1] for ref in partial_refs)
+    step = gradient_norm[0:1, 0:1] / tree(ref[0:1, CELLS : CELLS + 1] for ref in partial_refs)
     sums = []
     for k in range(pieces):
         both = [
@@ -379,20 +383,12 @@
 def finish_kernel(gradient_norm, gradient, direction, *refs):
     *norms, direction_next, norm_next = refs
     total = tree(ref[...] for ref in norms)
-    direction_next[...] = gradient[...] + total / gradient_norm[0] * direction[...]
+    direction_next[...] = gradient[...] + total / gradient_norm[...] * direction[...]
     norm_next[0] = total[0, 0]
 
 
 def sent(value, axis, size, other):
     return lax.ppermute(value, axis, [(rank, rank ^ other) for rank in range(size)])
-
-
-def doubled(value, axis, size):
-    step = 1
-    while step < size // 2:
-        value = jnp.concatenate([value, sent(value, axis, size, step)], axis=1)
-        step *= 2
-    return [value, sent(value, axis, size, step)]
 
 
 def exchanged(value, axis, size):
@@ -415,60 +411,90 @@
     own, cell_own = station_place.shape[1], cell_place.shape[1]
     width, extent = cell_size * own, stn_size * cell_own
     rows, blocks = width // 128, extent // CELLS
+    scalar_row = jnp.concatenate(
+        [
+            jnp.broadcast_to(pair_count.astype(F32), (1, own)),
+            jnp.broadcast_to(gradient_norm[None], (1, own)),
+        ],
+        axis=1,
+    )
     if direct:
-        station_parts = doubled(station_place, "cell", cell_size)
+        near = sent(station_place, "cell", cell_size, 1)
+        scalars = jnp.concatenate(
+            [jnp.concatenate([station_place, near], axis=1), scalar_row], axis=0
+        )
+        station_parts = [scalars] + [
+            sent(scalars, "cell", cell_size, other) for other in range(2, cell_size, 2)
+        ]
     else:
         both = jnp.concatenate([station_place, residual], axis=0)
         station_parts = [lax.all_gather(both, "cell", axis=1, tiled=True)]
+        scalars = jnp.concatenate([jnp.zeros((3, 2 * own), F32), scalar_row], axis=0)
     cell_mine = jnp.concatenate([cell_place, direction[None]], axis=0)
     cell_parts = exchanged(cell_mine, "stn", stn_size)
-    in_vmem, in_smem = pl.BlockSpec(memory_space=pltpu.VMEM), pl.BlockSpec(memory_space=pltpu.SMEM)
+    in_vmem, in_smem = (pl.BlockSpec(memory_space=space) for space in (pltpu.VMEM, pltpu.SMEM))
     in_hbm = pl.BlockSpec(memory_space=pltpu.HBM)
     lists = (station_blocks.reshape(1, -1), cell_blocks.reshape(1, -1), residual)
     params = pltpu.CompilerParams(vmem_limit_bytes=(16 if direct else 56) * 2**20)
     small = pltpu.CompilerParams(vmem_limit_bytes=2**20)
-    counts = (len(station_parts), len(cell_parts))
-    pieces = sum(counts)
+
+    def prepare(*refs):
+        prepare_kernel(len(cell_parts), direct, *refs)
+
+    cell_all, count, last_norm, *prepared = pl.pallas_call(
+        prepare,
+        out_shape=(
+            jax.ShapeDtypeStruct((8, extent), F32),
+            jax.ShapeDtypeStruct((blocks, width), F32),
+            jax.ShapeDtypeStruct((1, 128), F32),
+            jax.ShapeDtypeStruct((extent, DEPTH), BF16),
+            jax.ShapeDtypeStruct((48, extent), BF16),
+            jax.ShapeDtypeStruct((32, extent), F8),
+            jax.ShapeDtypeStruct((16, 128), F32),
+            jax.ShapeDtypeStruct((6 * own // 128, 128), F32),
+        ),
+        in_specs=[in_vmem] + [in_hbm] * 3 + [in_vmem] * len(cell_parts),
+        out_specs=(in_vmem,) * 8,
+        scratch_shapes=[
+            pltpu.VMEM((DEPTH, extent), F32),
+            *(pltpu.VMEM(here.shape, here.dtype) for here in lists),
+            pltpu.SemaphoreType.DMA((3,)),
+        ],
+        compiler_params=pltpu.CompilerParams(vmem_limit_bytes=(8 if direct else 56) * 2**20),
+        cost_estimate=pl.CostEstimate(flops=2**22, bytes_accessed=2**21, transcendentals=0),
+        name="prepare",
+    )(
+        scalars,
+        *(pltpu.with_memory_space_constraint(here, pltpu.HBM) for here in lists),
+        *cell_parts,
+    )
 
     def forward(*refs):
-        forward_kernel(*counts, direct, *refs)
+        forward_kernel(len(station_parts), direct, *refs)
 
     out_shape = [
         jax.ShapeDtypeStruct((5 * rows + (6 * own // 128 if direct else 0), 128), F32),
-        jax.ShapeDtypeStruct((blocks, width), F32),
         jax.ShapeDtypeStruct((16, width), F32),
-        jax.ShapeDtypeStruct((8, extent), F32),
     ]
     if direct:
         out_shape += [
             jax.ShapeDtypeStruct((extent, width), BF16),
             jax.ShapeDtypeStruct((extent, width), F8),
         ]
-    image_part, *kept = pl.pallas_call(
+    image_part, station_all, *kept = pl.pallas_call(
         forward,
         out_shape=out_shape,
-        in_specs=[in_smem] + [in_hbm] * 3 + [in_vmem] * pieces,
+        in_specs=[in_vmem] * (1 + len(prepared) + len(station_parts)),
         out_specs=[in_vmem] * len(out_shape),
         scratch_shapes=[
             pltpu.VMEM((DEPTH, width), F32),
-            pltpu.VMEM((DEPTH, extent), F32),
-            pltpu.VMEM((extent, DEPTH), BF16),
             pltpu.VMEM((DEPTH, width), BF16),
-            pltpu.VMEM((48, extent), BF16),
-            pltpu.VMEM((32, extent), F8),
             pltpu.VMEM((blocks, 16, width), F32),
             pltpu.VMEM((13 * rows, 128), F32),
-            *(pltpu.VMEM(here.shape, here.dtype) for here in lists),
-            pltpu.SemaphoreType.DMA((3,)),
         ],
         compiler_params=params,
         name="forward",
-    )(
-        pair_count,
-        *(pltpu.with_memory_space_constraint(here, pltpu.HBM) for here in lists),
-        *station_parts,
-        *cell_parts,
-    )
+    )(count, *prepared, *station_parts)
     if direct:
         image_parts = exchanged(image_part, "cell", cell_size)
     else:
@@ -492,7 +518,7 @@
             jax.ShapeDtypeStruct((2 * blocks, CELLS + 128), F32),
             jax.ShapeDtypeStruct((8, own if direct else width), F32),
         ),
-        in_specs=[in_vmem] * (len(kept) + len(image_parts)),
+        in_specs=[in_vmem] * (3 + len(kept) + len(image_parts)),
         out_specs=(in_vmem, in_vmem),
         scratch_shapes=[
             pltpu.VMEM((8, width), F32),
@@ -501,7 +527,7 @@
         ],
         compiler_params=params,
         name="adjoint",
-    )(*kept, *image_parts)
+    )(count, station_all, cell_all, *kept, *image_parts)
     if not direct:
         image_own = lax.dynamic_slice_in_dim(image_own, lax.axis_index("cell") * own, own, axis=1)
     partial_parts = exchanged(partial, "stn", stn_size)
@@ -518,11 +544,11 @@
             jax.ShapeDtypeStruct(flat.shape, F32),
             jax.ShapeDtypeStruct((1, 128), F32),
         ),
-        in_specs=[in_smem] + [in_vmem] * (4 + stn_size),
+        in_specs=[in_vmem] * (5 + stn_size),
         out_specs=(in_vmem,) * 4,
         compiler_params=small,
         name="update",
-    )(gradient_norm, densities.reshape(flat.shape), flat, residual, image_own, *partial_parts)
+    )(last_norm, densities.reshape(flat.shape), flat, residual, image_own, *partial_parts)
     if direct:
         norm_parts = exchanged(norm_part, "cell", cell_size)
     else:
@@ -533,11 +559,11 @@
             jax.ShapeDtypeStruct(flat.shape, F32),
             jax.ShapeDtypeStruct((1,), F32),
         ),
-        in_specs=[in_smem] + [in_vmem] * (2 + len(norm_parts)),
+        in_specs=[in_vmem] * (3 + len(norm_parts)),
         out_specs=(in_vmem, in_smem),
         compiler_params=small,
         name="finish",
-    )(gradient_norm, gradient, flat, *norm_parts)
+    )(last_norm, gradient, flat, *norm_parts)
     return (densities_next.reshape(-1), residual_next, direction_next.reshape(-1), norm_next)
 
 

time: 57.4 us -> 53 us (0.923)
  waiting for transfers between devices: 13.3 us -> 8.9 us
  local copies, waits for them, and re-layouts: 0.75 us -> 0.02 us
  other arithmetic: 0.76 us -> 1.46 us
  Pallas kernels: 21.3 us -> 21.9 us
    ppermute x14, waiting for transfers between devices: 13.3 us -> 8.9 us  [sent(): lax.ppermute(value, axis, [(rank, rank ^ other) for rank in range(size)])]
    unnamed x7 -> x6, local copies, waits for them, and re-layouts: 0.75 us -> 0.01 us
    concatenate x0 -> x1, other arithmetic: none -> 0.71 us  [on_device(): jnp.concatenate([jnp.concatenate([station_place, near], axis=1), scalar_r...]
    pallas_call x1 -> x2, Pallas kernels: 12.9 us -> 13.5 us  [the longest x1 12 us: on_device(): pl.pallas_call(forward, out_shape=out_shape, in_specs=[in_vmem] * (1 + le...]
  transfers between devices with their start and end apart: 14 -> 14, of which waited for: 8 -> 7; matrix products, arithmetic and copies ran while one was open for 1% -> 3% of each run, Pallas kernels for 0% -> 3%
where the time goes in v4:
time: 53 us; the launch traced here: 52.7 us
  Pallas kernels  21.9 us (41%)
  starting transfers between devices  18.4 us (35%)
  waiting for transfers between devices  8.9 us (17%)
  between operations  2.04 us (4%)
  other arithmetic  1.46 us (3%)
    ppermute x14, starting transfers between devices, sent(): lax.ppermute(value, axis, [(rank, rank ^ other) for rank in range(size)])  18.4 us
    pallas_call x1, Pallas kernels, on_device(): pl.pallas_call(forward, out_shape=out_shape, in_specs=[in_vmem] * (1 + le...  12 us
    ppermute x14, waiting for transfers between devices, sent(): lax.ppermute(value, axis, [(rank, rank ^ other) for rank in range(size)])  8.9 us
    pallas_call x1, Pallas kernels, on_device(): pl.pallas_call(adjoint, out_shape=(jax.ShapeDtypeStruct((2 * blocks, CELL...  7.05 us
    pallas_call x1, Pallas kernels, on_device(): pl.pallas_call(prepare, out_shape=(jax.ShapeDtypeStruct((8, extent), F32)...  1.48 us
  transfers between devices with their start and end apart: 14, of which 7 were waited for; matrix products, arithmetic and copies ran while one was open for 3% of the time, Pallas kernels for 3%

profile of v4, /device:TPU:0, one launch (start us, length us, event | category | flops | bytes accessed | tf_op | source)
XLA Modules:
  0.0 52.7 jit_solution(15513131816446395869)
XLA Ops:
  0.6 0.0 copy-start.1
  0.6 0.0 copy-start
  0.7 0.0 copy-start.2
  0.7 3.1 %collective-permute-start = (f32[3,512]{1,0:T(4,128)}, f32[3,512]{1,0:T(4,128)S(1)}, u32[]{:S(2)}, u32[]{:S(2)}) collective-permute-start(f32[3,512]{1,0:T(4,128)} %param.13), channel_id=1, source_target_pairs={{0,4},{4,0},{8,12},{12,8},{1,5},{5,1},{9,13},{13,9},{2,6},{6,2},{1... | collective-permute-start | bytes 18440 | tf_op jit(solution)/shard_map/ppermute | solution.py:391
  3.8 0.7 %pad_maximum_fusion.1.refs_4_ = f32[4,1024]{1,0:T(4,128)S(1)} fusion(f32[1,1024]{1,0:T(1,128)} %bitcast.11, f32[3,1024]{1,0:T(4,128)} %param.14), kind=kLoop, calls=%fused_computation.1 | loop fusion | flops 4096 | bytes 32768 | tf_op jit(solution)/shard_map/concatenate | solution.py:433
  4.5 0.7 %collective-permute-start.3 = (f32[4,1024]{1,0:T(4,128)S(1)}, f32[4,1024]{1,0:T(4,128)S(1)}, u32[]{:S(2)}, u32[]{:S(2)}) collective-permute-start(f32[4,1024]{1,0:T(4,128)S(1)} %pad_maximum_fusion.1.refs_4_), channel_id=1, source_target_pairs={{0,3},{1,2},{2,1},{3,0},{4,7},{5,6},{6,5},{7,4},{8,11},{9,10},{10,... | collective-permute-start | bytes 49160 | tf_op jit(solution)/shard_map/ppermute | solution.py:391
  5.2 0.9 %collective-permute-start.2 = (f32[4,1024]{1,0:T(4,128)S(1)}, f32[4,1024]{1,0:T(4,128)S(1)}, u32[]{:S(2)}, u32[]{:S(2)}) collective-permute-start(f32[4,1024]{1,0:T(4,128)S(1)} %pad_maximum_fusion.1.refs_4_), channel_id=1, source_target_pairs={{0,2},{1,3},{2,0},{3,1},{4,6},{5,7},{6,4},{7,5},{8,10},{9,11},{10,... | collective-permute-start | bytes 49160 | tf_op jit(solution)/shard_map/ppermute | solution.py:391
  6.1 0.3 collective-permute-start.1
  7.7 0.0 collective-permute-done
  7.8 0.7 %pad_maximum_fusion.refs_0_.refs_6_ = f32[4,1024]{1,0:T(4,128)S(1)} fusion(f32[1,1024]{1,0:T(1,128)S(1)} %bitcast.15, f32[3,512]{1,0:T(4,128)S(1)} %collective-permute-done, f32[3,512]{1,0:T(4,128)} %param.13), kind=kLoop, calls=%fused_computation | loop fusion | flops 8192 | bytes 32768 | tf_op jit(solution)/shard_map/concatenate | solution.py:423
  8.5 2.7 %collective-permute-start.4 = (f32[4,1024]{1,0:T(4,128)S(1)}, f32[4,1024]{1,0:T(4,128)S(1)}, u32[]{:S(2)}, u32[]{:S(2)}) collective-permute-start(f32[4,1024]{1,0:T(4,128)S(1)} %pad_maximum_fusion.refs_0_.refs_6_), channel_id=1, source_target_pairs={{0,8},{4,12},{8,0},{12,4},{1,9},{5,13},{9,1},{13,5},{2,10},{6,14},... | collective-permute-start | bytes 49160 | tf_op jit(solution)/shard_map/ppermute | solution.py:391
  11.1 0.0 collective-permute-done.3.refs_7_
  11.1 0.0 collective-permute-done.2.refs_6_
  11.1 0.0 collective-permute-done.1.refs_5_
  11.1 1.5 %prepare.1 = (f32[8,4096]{1,0:T(8,128)S(1)}, f32[8,2048]{1,0:T(8,128)S(1)}, f32[1,128]{1,0:T(1,128)S(1)}, bf16[4096,32]{1,0:T(8,128)(2,1)S(1)}, bf16[48,4096]{1,...) custom-call(f32[4,1024]{1,0:T(4,128)S(1)} %pad_maximum_fusion.refs_0_.refs_6_, ...), custom_call_target="tpu_custom_call" | custom-call | flops 4194304 | bytes 2097152 | tf_op jit(solution)/shard_map/prepare/pallas_call | solution.py:444
  12.6 0.5 %collective-permute-done.4.refs_7_ = f32[4,1024]{1,0:T(4,128)S(1)} collective-permute-done((f32[4,1024]{1,0:T(4,128)S(1)}, f32[4,1024]{1,0:T(4,128)S(1)}, u32[]{:S(2)}, u32[]{:S(2)}) %collective-permute-start.4) | collective-permute-done | bytes 16416 | tf_op jit(solution)/shard_map/ppermute | solution.py:391
  13.2 12.0 %forward.1 = (f32[104,128]{1,0:T(8,128)S(1)}, f32[16,2048]{1,0:T(8,128)S(1)}, bf16[4096,2048]{1,0:T(8,128)(2,1)S(1)}, f8e4m3fn[4096,2048]{1,0:T(32,128)(4,1)S(1)}) custom-call(f32[8,2048]{1,0:T(8,128)S(1)} %get-tuple-element.25.refs_0_, bf16[4096,32]{1,0:T(8,128)(2,1)S(1)} %get-tuple-element.26.refs_1_, bf16[48,4096]{1,0:T(8,128)(2,1)S(1)} %get-tuple-element.27.refs_2_, ...), custom_call_target="tpu_custom_call" | custom-call | tf_op jit(solution)/shard_map/forward/pallas_call | solution.py:484
  25.2 2.5 %collective-permute-start.7 = (f32[104,128]{1,0:T(8,128)S(1)}, f32[104,128]{1,0:T(8,128)S(1)}, u32[]{:S(2)}, u32[]{:S(2)}) collective-permute-start(f32[104,128]{1,0:T(8,128)S(1)} %get-tuple-element.35.refs_5_), channel_id=1, source_target_pairs={{0,12},{4,8},{8,4},{12,0},{1,13},{5,9},{9,5},{13,1},{2,14},{6,10},... | collective-permute-start | bytes 159752 | tf_op jit(solution)/shard_map/ppermute | solution.py:391
  27.8 0.2 collective-permute-start.6
  28.0 1.7 %collective-permute-start.5 = (f32[104,128]{1,0:T(8,128)S(1)}, f32[104,128]{1,0:T(8,128)S(1)}, u32[]{:S(2)}, u32[]{:S(2)}) collective-permute-start(f32[104,128]{1,0:T(8,128)S(1)} %get-tuple-element.35.refs_5_), channel_id=1, source_target_pairs={{0,4},{4,0},{8,12},{12,8},{1,5},{5,1},{9,13},{13,9},{2,6},{6,2},{1... | collective-permute-start | bytes 159752 | tf_op jit(solution)/shard_map/ppermute | solution.py:391
  29.7 1.8 %collective-permute-done.7.refs_8_ = f32[104,128]{1,0:T(8,128)S(1)} collective-permute-done((f32[104,128]{1,0:T(8,128)S(1)}, f32[104,128]{1,0:T(8,128)S(1)}, u32[]{:S(2)}, u32[]{:S(2)}) %collective-permute-start.7) | collective-permute-done | bytes 53280 | tf_op jit(solution)/shard_map/ppermute | solution.py:391
  31.5 1.8 %collective-permute-done.6.refs_7_ = f32[104,128]{1,0:T(8,128)S(1)} collective-permute-done((f32[104,128]{1,0:T(8,128)S(1)}, f32[104,128]{1,0:T(8,128)S(1)}, u32[]{:S(2)}, u32[]{:S(2)}) %collective-permute-start.6) | collective-permute-done | bytes 53280 | tf_op jit(solution)/shard_map/ppermute | solution.py:391
  33.4 0.0 collective-permute-done.5.refs_6_
  33.4 7.1 %adjoint.1 = (f32[16,640]{1,0:T(8,128)S(1)}, f32[8,512]{1,0:T(8,128)S(1)}) custom-call(f32[8,2048]{1,0:T(8,128)S(1)} %get-tuple-element.25.refs_0_, f32[16,2048]{1,0:T(8,128)S(1)} %get-tuple-element.31.refs_1_, f32[8,4096]{1,0:T(8,128)S(1)} %get-tuple-element.32.refs_2_, bf16[4096,2048]{1,0:T(8,128)(2,1)S(1)} %get-tuple-element.33.refs_3_, ...), custom_call_target="tpu_custom_call" | custom-call | tf_op jit(solution)/shard_map/adjoint/pallas_call | solution.py:515
  40.4 0.1 collective-permute-start.10
  40.5 1.7 %collective-permute-start.9 = (f32[16,640]{1,0:T(8,128)S(1)}, f32[16,640]{1,0:T(8,128)S(1)}, u32[]{:S(2)}, u32[]{:S(2)}) collective-permute-start(f32[16,640]{1,0:T(8,128)S(1)} %get-tuple-element.37.refs_5_), channel_id=1, source_target_pairs={{0,2},{1,3},{2,0},{3,1},{4,6},{5,7},{6,4},{7,5},{8,10},{9,11},{10,... | collective-permute-start | bytes 122888 | tf_op jit(solution)/shard_map/ppermute | solution.py:391
  42.2 0.2 collective-permute-start.8
  42.4 1.8 %collective-permute-done.10.refs_8_ = f32[16,640]{1,0:T(8,128)S(1)} collective-permute-done((f32[16,640]{1,0:T(8,128)S(1)}, f32[16,640]{1,0:T(8,128)S(1)}, u32[]{:S(2)}, u32[]{:S(2)}) %collective-permute-start.10) | collective-permute-done | bytes 40992 | tf_op jit(solution)/shard_map/ppermute | solution.py:391
  44.2 0.6 %collective-permute-done.9.refs_7_ = f32[16,640]{1,0:T(8,128)S(1)} collective-permute-done((f32[16,640]{1,0:T(8,128)S(1)}, f32[16,640]{1,0:T(8,128)S(1)}, u32[]{:S(2)}, u32[]{:S(2)}) %collective-permute-start.9) | collective-permute-done | bytes 40992 | tf_op jit(solution)/shard_map/ppermute | solution.py:391
  44.8 0.0 collective-permute-done.8.refs_6_
  44.8 0.0 copy-done.1
  44.8 0.0 copy-done
  44.8 0.0 copy-done.2
  44.8 0.7 %update.1 = (f32[8,128]{1,0:T(8,128)}, f32[6,512]{1,0:T(8,128)}, f32[8,128]{1,0:T(8,128)S(1)}, f32[1,128]{1,0:T(1,128)S(1)}) custom-call(f32[1,128]{1,0:T(1,128)S(1)} %get-tuple-element.24.refs_0_.gradient_norm, f32[8,128]{1,0:T(8,128)S(1)} %bitcast.14, f32[8,128]{1,0:T(8,128)S(1)} %bitcast.12, f32[6,512]{1,0:T(8,128)S(1)} %copy-done, ...), custom_call_target="tpu_custom_call" | custom-call | tf_op jit(solution)/shard_map/update/pallas_call | solution.py:539
  45.5 2.1 %collective-permute-start.13 = (f32[1,128]{1,0:T(1,128)S(1)}, f32[1,128]{1,0:T(1,128)S(1)}, u32[]{:S(2)}, u32[]{:S(2)}) collective-permute-start(f32[1,128]{1,0:T(1,128)S(1)} %get-tuple-element.41.refs_0_), channel_id=1, source_target_pairs={{0,12},{4,8},{8,4},{12,0},{1,13},{5,9},{9,5},{13,1},{2,14},{6,10},... | collective-permute-start | bytes 1544 | tf_op jit(solution)/shard_map/ppermute | solution.py:391
  47.7 0.0 collective-permute-start.12
  47.7 2.2 %collective-permute-start.11 = (f32[1,128]{1,0:T(1,128)S(1)}, f32[1,128]{1,0:T(1,128)S(1)}, u32[]{:S(2)}, u32[]{:S(2)}) collective-permute-start(f32[1,128]{1,0:T(1,128)S(1)} %get-tuple-element.41.refs_0_), channel_id=1, source_target_pairs={{0,4},{4,0},{8,12},{12,8},{1,5},{5,1},{9,13},{13,9},{2,6},{6,2},{1... | collective-permute-start | bytes 1544 | tf_op jit(solution)/shard_map/ppermute | solution.py:391
  49.9 0.9 %collective-permute-done.13.refs_3_ = f32[1,128]{1,0:T(1,128)S(1)} collective-permute-done((f32[1,128]{1,0:T(1,128)S(1)}, f32[1,128]{1,0:T(1,128)S(1)}, u32[]{:S(2)}, u32[]{:S(2)}) %collective-permute-start.13) | collective-permute-done | bytes 544 | tf_op jit(solution)/shard_map/ppermute | solution.py:391
  50.9 1.2 %collective-permute-done.12.refs_2_ = f32[1,128]{1,0:T(1,128)S(1)} collective-permute-done((f32[1,128]{1,0:T(1,128)S(1)}, f32[1,128]{1,0:T(1,128)S(1)}, u32[]{:S(2)}, u32[]{:S(2)}) %collective-permute-start.12) | collective-permute-done | bytes 544 | tf_op jit(solution)/shard_map/ppermute | solution.py:391
  52.1 0.0 collective-permute-done.11.refs_1_
  52.1 0.6 %finish.1 = (f32[8,128]{1,0:T(8,128)}, f32[1]{0:T(128)}) custom-call(f32[1,128]{1,0:T(1,128)S(1)} %get-tuple-element.24.refs_0_.gradient_norm, f32[8,128]{1,0:T(8,128)S(1)} %get-tuple-element.40.gradient, f32[8,128]{1,0:T(8,128)S(1)} %bitcast.13, f32[1,128]{1,0:T(1,128)S(1)} %get-tuple-element.41.refs_0_, f32[1,128]{1,0:T(1,128)S(1)} %collective-permute-done.11.refs_1_, ...), custom_call_target="tpu_custom_call" | custom-call | tf_op jit(solution)/shard_map/finish/pallas_call | solution.py:556
  (2 shorter events, 0.0 us)
Async XLA Ops:
  0.6 44.2 %copy-start.1 = (f32[1024]{0:T(1024)S(1)}, f32[1024]{0:T(1024)}, u32[]{:S(2)}) copy-start(f32[1024]{0:T(1024)} %param.11) | copy-start | bytes 12292
  0.6 44.2 %copy-start = (f32[6,512]{1,0:T(8,128)S(1)}, f32[6,512]{1,0:T(8,128)}, u32[]{:S(2)}) copy-start(f32[6,512]{1,0:T(8,128)} %refs_3_.3) | copy-start | bytes 36868
  0.7 44.2 %copy-start.2 = (f32[1024]{0:T(1024)S(1)}, f32[1024]{0:T(1024)}, u32[]{:S(2)}) copy-start(f32[1024]{0:T(1024)} %param.9) | copy-start | bytes 12292
  0.7 7.1 %collective-permute-start = (f32[3,512]{1,0:T(4,128)}, f32[3,512]{1,0:T(4,128)S(1)}, u32[]{:S(2)}, u32[]{:S(2)}) collective-permute-start(f32[3,512]{1,0:T(4,128)} %param.13), channel_id=1, source_target_pairs={{0,4},{4,0},{8,12},{12,8},{1,5},{5,1},{9,13},{13,9},{2,6},{6,2},{1... | collective-permute-start | bytes 18440 | tf_op jit(solution)/shard_map/ppermute | solution.py:391
  4.5 6.6 %collective-permute-start.3 = (f32[4,1024]{1,0:T(4,128)S(1)}, f32[4,1024]{1,0:T(4,128)S(1)}, u32[]{:S(2)}, u32[]{:S(2)}) collective-permute-start(f32[4,1024]{1,0:T(4,128)S(1)} %pad_maximum_fusion.1.refs_4_), channel_id=1, source_target_pairs={{0,3},{1,2},{2,1},{3,0},{4,7},{5,6},{6,5},{7,4},{8,11},{9,10},{10,... | collective-permute-start | bytes 49160 | tf_op jit(solution)/shard_map/ppermute | solution.py:391
  5.2 5.9 %collective-permute-start.2 = (f32[4,1024]{1,0:T(4,128)S(1)}, f32[4,1024]{1,0:T(4,128)S(1)}, u32[]{:S(2)}, u32[]{:S(2)}) collective-permute-start(f32[4,1024]{1,0:T(4,128)S(1)} %pad_maximum_fusion.1.refs_4_), channel_id=1, source_target_pairs={{0,2},{1,3},{2,0},{3,1},{4,6},{5,7},{6,4},{7,5},{8,10},{9,11},{10,... | collective-permute-start | bytes 49160 | tf_op jit(solution)/shard_map/ppermute | solution.py:391
  6.1 5.0 %collective-permute-start.1 = (f32[4,1024]{1,0:T(4,128)S(1)}, f32[4,1024]{1,0:T(4,128)S(1)}, u32[]{:S(2)}, u32[]{:S(2)}) collective-permute-start(f32[4,1024]{1,0:T(4,128)S(1)} %pad_maximum_fusion.1.refs_4_), channel_id=1, source_target_pairs={{0,1},{1,0},{2,3},{3,2},{4,5},{5,4},{6,7},{7,6},{8,9},{9,8},{10,11... | collective-permute-start | bytes 49160 | tf_op jit(solution)/shard_map/ppermute | solution.py:391
  8.5 4.7 %collective-permute-start.4 = (f32[4,1024]{1,0:T(4,128)S(1)}, f32[4,1024]{1,0:T(4,128)S(1)}, u32[]{:S(2)}, u32[]{:S(2)}) collective-permute-start(f32[4,1024]{1,0:T(4,128)S(1)} %pad_maximum_fusion.refs_0_.refs_6_), channel_id=1, source_target_pairs={{0,8},{4,12},{8,0},{12,4},{1,9},{5,13},{9,1},{13,5},{2,10},{6,14},... | collective-permute-start | bytes 49160 | tf_op jit(solution)/shard_map/ppermute | solution.py:391
  25.2 6.3 %collective-permute-start.7 = (f32[104,128]{1,0:T(8,128)S(1)}, f32[104,128]{1,0:T(8,128)S(1)}, u32[]{:S(2)}, u32[]{:S(2)}) collective-permute-start(f32[104,128]{1,0:T(8,128)S(1)} %get-tuple-element.35.refs_5_), channel_id=1, source_target_pairs={{0,12},{4,8},{8,4},{12,0},{1,13},{5,9},{9,5},{13,1},{2,14},{6,10},... | collective-permute-start | bytes 159752 | tf_op jit(solution)/shard_map/ppermute | solution.py:391
  27.8 5.6 %collective-permute-start.6 = (f32[104,128]{1,0:T(8,128)S(1)}, f32[104,128]{1,0:T(8,128)S(1)}, u32[]{:S(2)}, u32[]{:S(2)}) collective-permute-start(f32[104,128]{1,0:T(8,128)S(1)} %get-tuple-element.35.refs_5_), channel_id=1, source_target_pairs={{0,8},{4,12},{8,0},{12,4},{1,9},{5,13},{9,1},{13,5},{2,10},{6,14},... | collective-permute-start | bytes 159752 | tf_op jit(solution)/shard_map/ppermute | solution.py:391
  28.0 5.4 %collective-permute-start.5 = (f32[104,128]{1,0:T(8,128)S(1)}, f32[104,128]{1,0:T(8,128)S(1)}, u32[]{:S(2)}, u32[]{:S(2)}) collective-permute-start(f32[104,128]{1,0:T(8,128)S(1)} %get-tuple-element.35.refs_5_), channel_id=1, source_target_pairs={{0,4},{4,0},{8,12},{12,8},{1,5},{5,1},{9,13},{13,9},{2,6},{6,2},{1... | collective-permute-start | bytes 159752 | tf_op jit(solution)/shard_map/ppermute | solution.py:391
  40.4 3.8 %collective-permute-start.10 = (f32[16,640]{1,0:T(8,128)S(1)}, f32[16,640]{1,0:T(8,128)S(1)}, u32[]{:S(2)}, u32[]{:S(2)}) collective-permute-start(f32[16,640]{1,0:T(8,128)S(1)} %get-tuple-element.37.refs_5_), channel_id=1, source_target_pairs={{0,3},{1,2},{2,1},{3,0},{4,7},{5,6},{6,5},{7,4},{8,11},{9,10},{10,... | collective-permute-start | bytes 122888 | tf_op jit(solution)/shard_map/ppermute | solution.py:391
  40.5 4.3 %collective-permute-start.9 = (f32[16,640]{1,0:T(8,128)S(1)}, f32[16,640]{1,0:T(8,128)S(1)}, u32[]{:S(2)}, u32[]{:S(2)}) collective-permute-start(f32[16,640]{1,0:T(8,128)S(1)} %get-tuple-element.37.refs_5_), channel_id=1, source_target_pairs={{0,2},{1,3},{2,0},{3,1},{4,6},{5,7},{6,4},{7,5},{8,10},{9,11},{10,... | collective-permute-start | bytes 122888 | tf_op jit(solution)/shard_map/ppermute | solution.py:391
  42.2 2.6 %collective-permute-start.8 = (f32[16,640]{1,0:T(8,128)S(1)}, f32[16,640]{1,0:T(8,128)S(1)}, u32[]{:S(2)}, u32[]{:S(2)}) collective-permute-start(f32[16,640]{1,0:T(8,128)S(1)} %get-tuple-element.37.refs_5_), channel_id=1, source_target_pairs={{0,1},{1,0},{2,3},{3,2},{4,5},{5,4},{6,7},{7,6},{8,9},{9,8},{10,11... | collective-permute-start | bytes 122888 | tf_op jit(solution)/shard_map/ppermute | solution.py:391
  45.5 5.3 %collective-permute-start.13 = (f32[1,128]{1,0:T(1,128)S(1)}, f32[1,128]{1,0:T(1,128)S(1)}, u32[]{:S(2)}, u32[]{:S(2)}) collective-permute-start(f32[1,128]{1,0:T(1,128)S(1)} %get-tuple-element.41.refs_0_), channel_id=1, source_target_pairs={{0,12},{4,8},{8,4},{12,0},{1,13},{5,9},{9,5},{13,1},{2,14},{6,10},... | collective-permute-start | bytes 1544 | tf_op jit(solution)/shard_map/ppermute | solution.py:391
  47.7 4.4 %collective-permute-start.12 = (f32[1,128]{1,0:T(1,128)S(1)}, f32[1,128]{1,0:T(1,128)S(1)}, u32[]{:S(2)}, u32[]{:S(2)}) collective-permute-start(f32[1,128]{1,0:T(1,128)S(1)} %get-tuple-element.41.refs_0_), channel_id=1, source_target_pairs={{0,8},{4,12},{8,0},{12,4},{1,9},{5,13},{9,1},{13,5},{2,10},{6,14},... | collective-permute-start | bytes 1544 | tf_op jit(solution)/shard_map/ppermute | solution.py:391
  47.7 4.4 %collective-permute-start.11 = (f32[1,128]{1,0:T(1,128)S(1)}, f32[1,128]{1,0:T(1,128)S(1)}, u32[]{:S(2)}, u32[]{:S(2)}) collective-permute-start(f32[1,128]{1,0:T(1,128)S(1)} %get-tuple-element.41.refs_0_), channel_id=1, source_target_pairs={{0,4},{4,0},{8,12},{12,8},{1,5},{5,1},{9,13},{13,9},{2,6},{6,2},{1... | collective-permute-start | bytes 1544 | tf_op jit(solution)/shard_map/ppermute | solution.py:391

commit v5 on v4

--- a/solution.py
+++ b/solution.py
@@ -123,7 +123,7 @@
     return multiply(count.astype(BF16), spread.astype(F32).astype(BF16))
 
 
-def prepare_kernel(cell_pieces, keep, scalars, *refs):
+def prepare_kernel(cell_pieces, keep, filled, scalars, *refs):
     lists_here, cell_refs, refs = refs[:3], refs[3 : 3 + cell_pieces], refs[3 + cell_pieces :]
     cell, count, last_norm, left, source, narrow, units, packed, cell_rows, *held, arrived = refs
     copies = [
@@ -155,7 +155,7 @@
     count[...] = listed_counts(
         station_list,
         cell_list,
-        scalars[3:4, 0:1].astype(jnp.int32),
+        filled[0, 0],
         (lax.axis_index("cell") if keep else 0, lax.axis_index("stn")),
         (width // STATIONS, extent // CELLS),
         (residual.shape[1] // STATIONS, extent // CELLS // lax.axis_size("stn")),
@@ -411,13 +411,7 @@
     own, cell_own = station_place.shape[1], cell_place.shape[1]
     width, extent = cell_size * own, stn_size * cell_own
     rows, blocks = width // 128, extent // CELLS
-    scalar_row = jnp.concatenate(
-        [
-            jnp.broadcast_to(pair_count.astype(F32), (1, own)),
-            jnp.broadcast_to(gradient_norm[None], (1, own)),
-        ],
-        axis=1,
-    )
+    scalar_row = jnp.broadcast_to(gradient_norm[None], (1, 2 * own))
     if direct:
         near = sent(station_place, "cell", cell_size, 1)
         scalars = jnp.concatenate(
@@ -453,7 +447,7 @@
             jax.ShapeDtypeStruct((16, 128), F32),
             jax.ShapeDtypeStruct((6 * own // 128, 128), F32),
         ),
-        in_specs=[in_vmem] + [in_hbm] * 3 + [in_vmem] * len(cell_parts),
+        in_specs=[in_smem, in_vmem] + [in_hbm] * 3 + [in_vmem] * len(cell_parts),
         out_specs=(in_vmem,) * 8,
         scratch_shapes=[
             pltpu.VMEM((DEPTH, extent), F32),
@@ -464,6 +458,7 @@
         cost_estimate=pl.CostEstimate(flops=2**22, bytes_accessed=2**21, transcendentals=0),
         name="prepare",
     )(
+        pair_count,
         scalars,
         *(pltpu.with_memory_space_constraint(here, pltpu.HBM) for here in lists),
         *cell_parts,

time: 53 us -> 52.2 us (0.985)
  waiting for transfers between devices: 8.9 us -> 8.11 us
    ppermute x14, waiting for transfers between devices: 8.9 us -> 8.11 us  [sent(): lax.ppermute(value, axis, [(rank, rank ^ other) for rank in range(size)])]
  transfers between devices with their start and end apart: 14 -> 14, of which waited for: 7 -> 6; matrix products, arithmetic and copies ran while one was open for 3% -> 3% of each run, Pallas kernels for 3% -> 3%
where the time goes in v5:
time: 52.2 us; the launch traced here: 51.9 us
  Pallas kernels  21.9 us (42%)
  starting transfers between devices  18.4 us (35%)
  waiting for transfers between devices  8.11 us (16%)
  between operations  2.04 us (4%)
  other arithmetic  1.45 us (3%)
    ppermute x14, starting transfers between devices, sent(): lax.ppermute(value, axis, [(rank, rank ^ other) for rank in range(size)])  18.4 us
    pallas_call x1, Pallas kernels, on_device(): pl.pallas_call(forward, out_shape=out_shape, in_specs=[in_vmem] * (1 + le...  12 us
    ppermute x14, waiting for transfers between devices, sent(): lax.ppermute(value, axis, [(rank, rank ^ other) for rank in range(size)])  8.11 us
    pallas_call x1, Pallas kernels, on_device(): pl.pallas_call(adjoint, out_shape=(jax.ShapeDtypeStruct((2 * blocks, CELL...  7.05 us
    pallas_call x1, Pallas kernels, on_device(): pl.pallas_call(prepare, out_shape=(jax.ShapeDtypeStruct((8, extent), F32)...  1.48 us
  transfers between devices with their start and end apart: 14, of which 6 were waited for; matrix products, arithmetic and copies ran while one was open for 3% of the time, Pallas kernels for 3%

profile of v5, /device:TPU:0, one launch (start us, length us, event | category | flops | bytes accessed | tf_op | source)
XLA Modules:
  0.0 51.9 jit_solution(2043712006757890467)
XLA Ops:
  0.6 0.0 copy-start.1
  0.6 0.0 copy-start
  0.7 0.0 copy-start.2
  0.7 3.1 %collective-permute-start = (f32[3,512]{1,0:T(4,128)}, f32[3,512]{1,0:T(4,128)S(1)}, u32[]{:S(2)}, u32[]{:S(2)}) collective-permute-start(f32[3,512]{1,0:T(4,128)} %param.13), channel_id=1, source_target_pairs={{0,4},{4,0},{8,12},{12,8},{1,5},{5,1},{9,13},{13,9},{2,6},{6,2},{1... | collective-permute-start | bytes 18440 | tf_op jit(solution)/shard_map/ppermute | solution.py:391
  3.8 0.7 %pad_maximum_fusion.refs_5_ = f32[4,1024]{1,0:T(4,128)S(1)} fusion(f32[1,1024]{1,0:T(1,128)} %bitcast.9, f32[3,1024]{1,0:T(4,128)} %param.14), kind=kLoop, calls=%fused_computation.2 | loop fusion | flops 4096 | bytes 32768 | tf_op jit(solution)/shard_map/concatenate | solution.py:427
  4.5 0.7 %collective-permute-start.3 = (f32[4,1024]{1,0:T(4,128)S(1)}, f32[4,1024]{1,0:T(4,128)S(1)}, u32[]{:S(2)}, u32[]{:S(2)}) collective-permute-start(f32[4,1024]{1,0:T(4,128)S(1)} %pad_maximum_fusion.refs_5_), channel_id=1, source_target_pairs={{0,3},{1,2},{2,1},{3,0},{4,7},{5,6},{6,5},{7,4},{8,11},{9,10},{10,... | collective-permute-start | bytes 49160 | tf_op jit(solution)/shard_map/ppermute | solution.py:391
  5.2 0.9 %collective-permute-start.2 = (f32[4,1024]{1,0:T(4,128)S(1)}, f32[4,1024]{1,0:T(4,128)S(1)}, u32[]{:S(2)}, u32[]{:S(2)}) collective-permute-start(f32[4,1024]{1,0:T(4,128)S(1)} %pad_maximum_fusion.refs_5_), channel_id=1, source_target_pairs={{0,2},{1,3},{2,0},{3,1},{4,6},{5,7},{6,4},{7,5},{8,10},{9,11},{10,... | collective-permute-start | bytes 49160 | tf_op jit(solution)/shard_map/ppermute | solution.py:391
  6.1 0.3 collective-permute-start.1
  7.1 0.0 collective-permute-done
  7.1 0.7 %select_maximum_fusion.refs_1_.refs_6_ = f32[4,1024]{1,0:T(4,128)S(1)} fusion(f32[3,512]{1,0:T(4,128)S(1)} %collective-permute-done, f32[3,512]{1,0:T(4,128)} %param.13, f32[]{:T(128)} %bitcast.8), kind=kLoop, calls=%fused_computation | loop fusion | flops 16384 | bytes 28676 | tf_op jit(solution)/shard_map/concatenate | solution.py:418
  7.8 2.6 %collective-permute-start.4 = (f32[4,1024]{1,0:T(4,128)S(1)}, f32[4,1024]{1,0:T(4,128)S(1)}, u32[]{:S(2)}, u32[]{:S(2)}) collective-permute-start(f32[4,1024]{1,0:T(4,128)S(1)} %select_maximum_fusion.refs_1_.refs_6_), channel_id=1, source_target_pairs={{0,8},{4,12},{8,0},{12,4},{1,9},{5,13},{9,1},{13,5},{2,10},{6,14},... | collective-permute-start | bytes 49160 | tf_op jit(solution)/shard_map/ppermute | solution.py:391
  11.0 0.0 collective-permute-done.3.refs_8_
  11.0 0.0 collective-permute-done.2.refs_7_
  11.1 0.0 collective-permute-done.1.refs_6_
  11.1 1.5 %prepare.1 = (f32[8,4096]{1,0:T(8,128)S(1)}, f32[8,2048]{1,0:T(8,128)S(1)}, f32[1,128]{1,0:T(1,128)S(1)}, bf16[4096,32]{1,0:T(8,128)(2,1)S(1)}, bf16[48,4096]{1,...) custom-call(s32[1,1]{1,0:T(1,128)S(6)} %copy.14.refs_0_, ...), custom_call_target="tpu_custom_call" | custom-call | flops 4194304 | bytes 2097152 | tf_op jit(solution)/shard_map/prepare/pallas_call | solution.py:438
  12.6 0.0 collective-permute-done.4.refs_7_
  12.6 12.0 %forward.1 = (f32[104,128]{1,0:T(8,128)S(1)}, f32[16,2048]{1,0:T(8,128)S(1)}, bf16[4096,2048]{1,0:T(8,128)(2,1)S(1)}, f8e4m3fn[4096,2048]{1,0:T(32,128)(4,1)S(1)}) custom-call(f32[8,2048]{1,0:T(8,128)S(1)} %get-tuple-element.25.refs_0_, bf16[4096,32]{1,0:T(8,128)(2,1)S(1)} %get-tuple-element.26.refs_1_, bf16[48,4096]{1,0:T(8,128)(2,1)S(1)} %get-tuple-element.27.refs_2_, ...), custom_call_target="tpu_custom_call" | custom-call | tf_op jit(solution)/shard_map/forward/pallas_call | solution.py:479
  24.6 2.5 %collective-permute-start.7 = (f32[104,128]{1,0:T(8,128)S(1)}, f32[104,128]{1,0:T(8,128)S(1)}, u32[]{:S(2)}, u32[]{:S(2)}) collective-permute-start(f32[104,128]{1,0:T(8,128)S(1)} %get-tuple-element.35.refs_5_), channel_id=1, source_target_pairs={{0,12},{4,8},{8,4},{12,0},{1,13},{5,9},{9,5},{13,1},{2,14},{6,10},... | collective-permute-start | bytes 159752 | tf_op jit(solution)/shard_map/ppermute | solution.py:391
  27.1 0.1 collective-permute-start.6
  27.2 1.9 %collective-permute-start.5 = (f32[104,128]{1,0:T(8,128)S(1)}, f32[104,128]{1,0:T(8,128)S(1)}, u32[]{:S(2)}, u32[]{:S(2)}) collective-permute-start(f32[104,128]{1,0:T(8,128)S(1)} %get-tuple-element.35.refs_5_), channel_id=1, source_target_pairs={{0,4},{4,0},{8,12},{12,8},{1,5},{5,1},{9,13},{13,9},{2,6},{6,2},{1... | collective-permute-start | bytes 159752 | tf_op jit(solution)/shard_map/ppermute | solution.py:391
  29.1 2.0 %collective-permute-done.7.refs_8_ = f32[104,128]{1,0:T(8,128)S(1)} collective-permute-done((f32[104,128]{1,0:T(8,128)S(1)}, f32[104,128]{1,0:T(8,128)S(1)}, u32[]{:S(2)}, u32[]{:S(2)}) %collective-permute-start.7) | collective-permute-done | bytes 53280 | tf_op jit(solution)/shard_map/ppermute | solution.py:391
  31.0 1.7 %collective-permute-done.6.refs_7_ = f32[104,128]{1,0:T(8,128)S(1)} collective-permute-done((f32[104,128]{1,0:T(8,128)S(1)}, f32[104,128]{1,0:T(8,128)S(1)}, u32[]{:S(2)}, u32[]{:S(2)}) %collective-permute-start.6) | collective-permute-done | bytes 53280 | tf_op jit(solution)/shard_map/ppermute | solution.py:391
  32.7 0.0 collective-permute-done.5.refs_6_
  32.7 7.1 %adjoint.1 = (f32[16,640]{1,0:T(8,128)S(1)}, f32[8,512]{1,0:T(8,128)S(1)}) custom-call(f32[8,2048]{1,0:T(8,128)S(1)} %get-tuple-element.25.refs_0_, f32[16,2048]{1,0:T(8,128)S(1)} %get-tuple-element.31.refs_1_, f32[8,4096]{1,0:T(8,128)S(1)} %get-tuple-element.32.refs_2_, bf16[4096,2048]{1,0:T(8,128)(2,1)S(1)} %get-tuple-element.33.refs_3_, ...), custom_call_target="tpu_custom_call" | custom-call | tf_op jit(solution)/shard_map/adjoint/pallas_call | solution.py:510
  39.8 0.1 collective-permute-start.10
  39.8 1.6 %collective-permute-start.9 = (f32[16,640]{1,0:T(8,128)S(1)}, f32[16,640]{1,0:T(8,128)S(1)}, u32[]{:S(2)}, u32[]{:S(2)}) collective-permute-start(f32[16,640]{1,0:T(8,128)S(1)} %get-tuple-element.37.refs_5_), channel_id=1, source_target_pairs={{0,2},{1,3},{2,0},{3,1},{4,6},{5,7},{6,4},{7,5},{8,10},{9,11},{10,... | collective-permute-start | bytes 122888 | tf_op jit(solution)/shard_map/ppermute | solution.py:391
  41.4 0.2 collective-permute-start.8
  41.7 1.9 %collective-permute-done.10.refs_8_ = f32[16,640]{1,0:T(8,128)S(1)} collective-permute-done((f32[16,640]{1,0:T(8,128)S(1)}, f32[16,640]{1,0:T(8,128)S(1)}, u32[]{:S(2)}, u32[]{:S(2)}) %collective-permute-start.10) | collective-permute-done | bytes 40992 | tf_op jit(solution)/shard_map/ppermute | solution.py:391
  43.6 0.6 %collective-permute-done.9.refs_7_ = f32[16,640]{1,0:T(8,128)S(1)} collective-permute-done((f32[16,640]{1,0:T(8,128)S(1)}, f32[16,640]{1,0:T(8,128)S(1)}, u32[]{:S(2)}, u32[]{:S(2)}) %collective-permute-start.9) | collective-permute-done | bytes 40992 | tf_op jit(solution)/shard_map/ppermute | solution.py:391
  44.2 0.0 collective-permute-done.8.refs_6_
  44.2 0.0 copy-done.1
  44.2 0.0 copy-done
  44.2 0.0 copy-done.2
  44.2 0.7 %update.1 = (f32[8,128]{1,0:T(8,128)}, f32[6,512]{1,0:T(8,128)}, f32[8,128]{1,0:T(8,128)S(1)}, f32[1,128]{1,0:T(1,128)S(1)}) custom-call(f32[1,128]{1,0:T(1,128)S(1)} %get-tuple-element.24.refs_0_.gradient_norm, f32[8,128]{1,0:T(8,128)S(1)} %bitcast.12, f32[8,128]{1,0:T(8,128)S(1)} %bitcast.10, f32[6,512]{1,0:T(8,128)S(1)} %copy-done, ...), custom_call_target="tpu_custom_call" | custom-call | tf_op jit(solution)/shard_map/update/pallas_call | solution.py:534
  44.9 1.9 %collective-permute-start.13 = (f32[1,128]{1,0:T(1,128)S(1)}, f32[1,128]{1,0:T(1,128)S(1)}, u32[]{:S(2)}, u32[]{:S(2)}) collective-permute-start(f32[1,128]{1,0:T(1,128)S(1)} %get-tuple-element.41.refs_0_), channel_id=1, source_target_pairs={{0,12},{4,8},{8,4},{12,0},{1,13},{5,9},{9,5},{13,1},{2,14},{6,10},... | collective-permute-start | bytes 1544 | tf_op jit(solution)/shard_map/ppermute | solution.py:391
  46.8 0.1 collective-permute-start.12
  46.9 2.4 %collective-permute-start.11 = (f32[1,128]{1,0:T(1,128)S(1)}, f32[1,128]{1,0:T(1,128)S(1)}, u32[]{:S(2)}, u32[]{:S(2)}) collective-permute-start(f32[1,128]{1,0:T(1,128)S(1)} %get-tuple-element.41.refs_0_), channel_id=1, source_target_pairs={{0,4},{4,0},{8,12},{12,8},{1,5},{5,1},{9,13},{13,9},{2,6},{6,2},{1... | collective-permute-start | bytes 1544 | tf_op jit(solution)/shard_map/ppermute | solution.py:391
  49.3 0.9 %collective-permute-done.13.refs_3_ = f32[1,128]{1,0:T(1,128)S(1)} collective-permute-done((f32[1,128]{1,0:T(1,128)S(1)}, f32[1,128]{1,0:T(1,128)S(1)}, u32[]{:S(2)}, u32[]{:S(2)}) %collective-permute-start.13) | collective-permute-done | bytes 544 | tf_op jit(solution)/shard_map/ppermute | solution.py:391
  50.2 1.0 %collective-permute-done.12.refs_2_ = f32[1,128]{1,0:T(1,128)S(1)} collective-permute-done((f32[1,128]{1,0:T(1,128)S(1)}, f32[1,128]{1,0:T(1,128)S(1)}, u32[]{:S(2)}, u32[]{:S(2)}) %collective-permute-start.12) | collective-permute-done | bytes 544 | tf_op jit(solution)/shard_map/ppermute | solution.py:391
  51.3 0.0 collective-permute-done.11.refs_1_
  51.3 0.6 %finish.1 = (f32[8,128]{1,0:T(8,128)}, f32[1]{0:T(128)}) custom-call(f32[1,128]{1,0:T(1,128)S(1)} %get-tuple-element.24.refs_0_.gradient_norm, f32[8,128]{1,0:T(8,128)S(1)} %get-tuple-element.40.gradient, f32[8,128]{1,0:T(8,128)S(1)} %bitcast.11, f32[1,128]{1,0:T(1,128)S(1)} %get-tuple-element.41.refs_0_, f32[1,128]{1,0:T(1,128)S(1)} %collective-permute-done.11.refs_1_, ...), custom_call_target="tpu_custom_call" | custom-call | tf_op jit(solution)/shard_map/finish/pallas_call | solution.py:551
Async XLA Ops:
  0.6 43.5 %copy-start.1 = (f32[1024]{0:T(1024)S(1)}, f32[1024]{0:T(1024)}, u32[]{:S(2)}) copy-start(f32[1024]{0:T(1024)} %param.11) | copy-start | bytes 12292
  0.6 43.5 %copy-start = (f32[6,512]{1,0:T(8,128)S(1)}, f32[6,512]{1,0:T(8,128)}, u32[]{:S(2)}) copy-start(f32[6,512]{1,0:T(8,128)} %refs_3_.1) | copy-start | bytes 36868
  0.7 43.5 %copy-start.2 = (f32[1024]{0:T(1024)S(1)}, f32[1024]{0:T(1024)}, u32[]{:S(2)}) copy-start(f32[1024]{0:T(1024)} %param.9) | copy-start | bytes 12292
  0.7 6.4 %collective-permute-start = (f32[3,512]{1,0:T(4,128)}, f32[3,512]{1,0:T(4,128)S(1)}, u32[]{:S(2)}, u32[]{:S(2)}) collective-permute-start(f32[3,512]{1,0:T(4,128)} %param.13), channel_id=1, source_target_pairs={{0,4},{4,0},{8,12},{12,8},{1,5},{5,1},{9,13},{13,9},{2,6},{6,2},{1... | collective-permute-start | bytes 18440 | tf_op jit(solution)/shard_map/ppermute | solution.py:391
  4.5 6.5 %collective-permute-start.3 = (f32[4,1024]{1,0:T(4,128)S(1)}, f32[4,1024]{1,0:T(4,128)S(1)}, u32[]{:S(2)}, u32[]{:S(2)}) collective-permute-start(f32[4,1024]{1,0:T(4,128)S(1)} %pad_maximum_fusion.refs_5_), channel_id=1, source_target_pairs={{0,3},{1,2},{2,1},{3,0},{4,7},{5,6},{6,5},{7,4},{8,11},{9,10},{10,... | collective-permute-start | bytes 49160 | tf_op jit(solution)/shard_map/ppermute | solution.py:391
  5.2 5.8 %collective-permute-start.2 = (f32[4,1024]{1,0:T(4,128)S(1)}, f32[4,1024]{1,0:T(4,128)S(1)}, u32[]{:S(2)}, u32[]{:S(2)}) collective-permute-start(f32[4,1024]{1,0:T(4,128)S(1)} %pad_maximum_fusion.refs_5_), channel_id=1, source_target_pairs={{0,2},{1,3},{2,0},{3,1},{4,6},{5,7},{6,4},{7,5},{8,10},{9,11},{10,... | collective-permute-start | bytes 49160 | tf_op jit(solution)/shard_map/ppermute | solution.py:391
  6.1 4.9 %collective-permute-start.1 = (f32[4,1024]{1,0:T(4,128)S(1)}, f32[4,1024]{1,0:T(4,128)S(1)}, u32[]{:S(2)}, u32[]{:S(2)}) collective-permute-start(f32[4,1024]{1,0:T(4,128)S(1)} %pad_maximum_fusion.refs_5_), channel_id=1, source_target_pairs={{0,1},{1,0},{2,3},{3,2},{4,5},{5,4},{6,7},{7,6},{8,9},{9,8},{10,11... | collective-permute-start | bytes 49160 | tf_op jit(solution)/shard_map/ppermute | solution.py:391
  7.8 4.8 %collective-permute-start.4 = (f32[4,1024]{1,0:T(4,128)S(1)}, f32[4,1024]{1,0:T(4,128)S(1)}, u32[]{:S(2)}, u32[]{:S(2)}) collective-permute-start(f32[4,1024]{1,0:T(4,128)S(1)} %select_maximum_fusion.refs_1_.refs_6_), channel_id=1, source_target_pairs={{0,8},{4,12},{8,0},{12,4},{1,9},{5,13},{9,1},{13,5},{2,10},{6,14},... | collective-permute-start | bytes 49160 | tf_op jit(solution)/shard_map/ppermute | solution.py:391
  24.6 6.4 %collective-permute-start.7 = (f32[104,128]{1,0:T(8,128)S(1)}, f32[104,128]{1,0:T(8,128)S(1)}, u32[]{:S(2)}, u32[]{:S(2)}) collective-permute-start(f32[104,128]{1,0:T(8,128)S(1)} %get-tuple-element.35.refs_5_), channel_id=1, source_target_pairs={{0,12},{4,8},{8,4},{12,0},{1,13},{5,9},{9,5},{13,1},{2,14},{6,10},... | collective-permute-start | bytes 159752 | tf_op jit(solution)/shard_map/ppermute | solution.py:391
  27.1 5.6 %collective-permute-start.6 = (f32[104,128]{1,0:T(8,128)S(1)}, f32[104,128]{1,0:T(8,128)S(1)}, u32[]{:S(2)}, u32[]{:S(2)}) collective-permute-start(f32[104,128]{1,0:T(8,128)S(1)} %get-tuple-element.35.refs_5_), channel_id=1, source_target_pairs={{0,8},{4,12},{8,0},{12,4},{1,9},{5,13},{9,1},{13,5},{2,10},{6,14},... | collective-permute-start | bytes 159752 | tf_op jit(solution)/shard_map/ppermute | solution.py:391
  27.2 5.5 %collective-permute-start.5 = (f32[104,128]{1,0:T(8,128)S(1)}, f32[104,128]{1,0:T(8,128)S(1)}, u32[]{:S(2)}, u32[]{:S(2)}) collective-permute-start(f32[104,128]{1,0:T(8,128)S(1)} %get-tuple-element.35.refs_5_), channel_id=1, source_target_pairs={{0,4},{4,0},{8,12},{12,8},{1,5},{5,1},{9,13},{13,9},{2,6},{6,2},{1... | collective-permute-start | bytes 159752 | tf_op jit(solution)/shard_map/ppermute | solution.py:391
  39.8 3.8 %collective-permute-start.10 = (f32[16,640]{1,0:T(8,128)S(1)}, f32[16,640]{1,0:T(8,128)S(1)}, u32[]{:S(2)}, u32[]{:S(2)}) collective-permute-start(f32[16,640]{1,0:T(8,128)S(1)} %get-tuple-element.37.refs_5_), channel_id=1, source_target_pairs={{0,3},{1,2},{2,1},{3,0},{4,7},{5,6},{6,5},{7,4},{8,11},{9,10},{10,... | collective-permute-start | bytes 122888 | tf_op jit(solution)/shard_map/ppermute | solution.py:391
  39.8 4.3 %collective-permute-start.9 = (f32[16,640]{1,0:T(8,128)S(1)}, f32[16,640]{1,0:T(8,128)S(1)}, u32[]{:S(2)}, u32[]{:S(2)}) collective-permute-start(f32[16,640]{1,0:T(8,128)S(1)} %get-tuple-element.37.refs_5_), channel_id=1, source_target_pairs={{0,2},{1,3},{2,0},{3,1},{4,6},{5,7},{6,4},{7,5},{8,10},{9,11},{10,... | collective-permute-start | bytes 122888 | tf_op jit(solution)/shard_map/ppermute | solution.py:391
  41.4 2.7 %collective-permute-start.8 = (f32[16,640]{1,0:T(8,128)S(1)}, f32[16,640]{1,0:T(8,128)S(1)}, u32[]{:S(2)}, u32[]{:S(2)}) collective-permute-start(f32[16,640]{1,0:T(8,128)S(1)} %get-tuple-element.37.refs_5_), channel_id=1, source_target_pairs={{0,1},{1,0},{2,3},{3,2},{4,5},{5,4},{6,7},{7,6},{8,9},{9,8},{10,11... | collective-permute-start | bytes 122888 | tf_op jit(solution)/shard_map/ppermute | solution.py:391
  44.9 5.3 %collective-permute-start.13 = (f32[1,128]{1,0:T(1,128)S(1)}, f32[1,128]{1,0:T(1,128)S(1)}, u32[]{:S(2)}, u32[]{:S(2)}) collective-permute-start(f32[1,128]{1,0:T(1,128)S(1)} %get-tuple-element.41.refs_0_), channel_id=1, source_target_pairs={{0,12},{4,8},{8,4},{12,0},{1,13},{5,9},{9,5},{13,1},{2,14},{6,10},... | collective-permute-start | bytes 1544 | tf_op jit(solution)/shard_map/ppermute | solution.py:391
  46.8 4.4 %collective-permute-start.12 = (f32[1,128]{1,0:T(1,128)S(1)}, f32[1,128]{1,0:T(1,128)S(1)}, u32[]{:S(2)}, u32[]{:S(2)}) collective-permute-start(f32[1,128]{1,0:T(1,128)S(1)} %get-tuple-element.41.refs_0_), channel_id=1, source_target_pairs={{0,8},{4,12},{8,0},{12,4},{1,9},{5,13},{9,1},{13,5},{2,10},{6,14},... | collective-permute-start | bytes 1544 | tf_op jit(solution)/shard_map/ppermute | solution.py:391
  46.9 4.4 %collective-permute-start.11 = (f32[1,128]{1,0:T(1,128)S(1)}, f32[1,128]{1,0:T(1,128)S(1)}, u32[]{:S(2)}, u32[]{:S(2)}) collective-permute-start(f32[1,128]{1,0:T(1,128)S(1)} %get-tuple-element.41.refs_0_), channel_id=1, source_target_pairs={{0,4},{4,0},{8,12},{12,8},{1,5},{5,1},{9,13},{13,9},{2,6},{6,2},{1... | collective-permute-start | bytes 1544 | tf_op jit(solution)/shard_map/ppermute | solution.py:391
